TPU v7x, 32 devices: a whole 2x2x4 slice. The times are simulated.
32 devices in a mesh: sec: 4 (over y, core), blk: 8 (over z, x).
Axes of the slice: x: 2, y: 2, z: 4, core: 2. Of those that a mesh axis runs over, the one named last changes fastest.
Arguments:
- fluid_temp: float32 [8, 256, 1024], P(None, 'sec', 'blk'), may hold values from -6 to 6
- stream_velocity: float32 [8, 256, 1024], P(None, 'sec', 'blk'), may hold values from 0.2 to 1
- pitch_velocity: float32 [8, 256, 1024], P(None, 'sec', 'blk'), may hold values from -0.5 to 0.5
- film_coeff: float32 [256, 1024], P('sec', 'blk'), may hold values from 0.1 to 0.3
- solid_temp: float32 [4, 32, 1024], P('sec', None, 'blk'), may hold values from -6 to 6
- conductivity: float32 [4, 32, 1024], P('sec', None, 'blk'), may hold values from 0.5 to 2
- face_owner: int32 [4, 8, 64, 1], P('sec', 'blk'), may hold values from 0 to 7; in each aligned block of 64 rows (0 to 63, 64 to 127, ..., all dimensions but the last counted through in order) at most 8 rows name the same one
Outputs:
- fluid_out: float32 [8, 256, 1024], P(None, 'sec', 'blk')
- solid_out: float32 [4, 32, 1024], P('sec', None, 'blk')
Inputs may be any that keep to these rules, and one draw needn't show every extreme that they name: `face_owner`: the 64 wall blocks of one device name any one owner at most 8 times; some device names some owner exactly 8 times.
All inputs are finite; a program needn't handle non-finite values.
Results may differ from a plain program's by a relative error of at most 0.0001.
Values sent between devices are 32-bit elements; how exact they have to be, the bound alone decides.
No kernel may reach another device: no remote copies, remote signals or barrier semaphores. Data moves between devices by JAX's collectives and lax.ppermute only.
A program may use at most 64 MiB of HBM per device.

v0:
```python
import jax
import jax.numpy as jnp
from jax import lax
from jax.sharding import PartitionSpec as P

SUB = 4


ADVECT = 0.4
SPREAD = 0.04
WALL = 0.4
SOLID_STEP = 0.04
COOLING = 0.5
COOLANT = -1.0


def padded(block, sides, width, periodic):
    for axis, dim in sides:
        count = lax.axis_size(axis)
        forward = [(i, i + 1) for i in range(count - 1)]
        if periodic:
            forward.append((count - 1, 0))
        backward = [(target, source) for source, target in forward]
        low = lax.ppermute(
            lax.slice_in_dim(block, block.shape[dim] - width, None, axis=dim), axis, forward
        )
        high = lax.ppermute(lax.slice_in_dim(block, 0, width, axis=dim), axis, backward)
        block = jnp.concatenate([low, block, high], axis=dim)
    return block


def fluid_update(
    fluid, stream_velocity, pitch_velocity, wall_flux, pitch_extended, stream_extended
):
    pitch_prev = pitch_extended[:, :-2]
    pitch_next = pitch_extended[:, 2:]
    stream_prev = stream_extended[:, :, :-2]
    stream_next = stream_extended[:, :, 2:]
    span_prev = jnp.concatenate([fluid[:1], fluid[:-1]], 0)
    span_next = jnp.concatenate([fluid[1:], fluid[-1:]], 0)
    spread = SPREAD * (
        pitch_prev + pitch_next + stream_prev + stream_next + span_prev + span_next - 6.0 * fluid
    )
    carried = (
        -ADVECT * stream_velocity * (fluid - stream_prev)
        - ADVECT * jnp.maximum(pitch_velocity, 0.0) * (fluid - pitch_prev)
        + ADVECT * jnp.maximum(-pitch_velocity, 0.0) * (pitch_next - fluid)
    )
    updated = fluid + spread + carried
    return updated.at[0].add(-WALL * wall_flux)


def solid_update(solid, conduct, inflow, solid_extended, conduct_extended):
    stream_prev = solid_extended[..., :-2]
    stream_next = solid_extended[..., 2:]
    conduct_prev = conduct_extended[..., :-2]
    conduct_next = conduct_extended[..., 2:]
    depth_prev = jnp.concatenate([solid[:, :1], solid[:, :-1]], 1)
    depth_next = jnp.concatenate([solid[:, 1:], solid[:, -1:]], 1)
    kdepth_prev = jnp.concatenate([conduct[:, :1], conduct[:, :-1]], 1)
    kdepth_next = jnp.concatenate([conduct[:, 1:], conduct[:, -1:]], 1)
    flow = (
        0.5 * (conduct + conduct_prev) * (stream_prev - solid)
        + 0.5 * (conduct + conduct_next) * (stream_next - solid)
        + 0.5 * (conduct + kdepth_prev) * (depth_prev - solid)
        + 0.5 * (conduct + kdepth_next) * (depth_next - solid)
    )
    updated = solid + SOLID_STEP * flow
    updated = updated.at[:, 0].add(SOLID_STEP * inflow)
    updated = updated.at[:, -1].add(SOLID_STEP * COOLING * (COOLANT - solid[:, -1]))
    return updated


def local(
    fluid_temp, stream_velocity, pitch_velocity, film_coeff, solid_temp, conductivity, face_owner
):
    span_cells, pitch_cells, stream_cells = fluid_temp.shape
    depth_cells = solid_temp.shape[1]
    block_count = lax.axis_size("blk")
    capacity = max(2, (pitch_cells + block_count - 1) // block_count)
    owners = face_owner.reshape(-1)
    onehot = (owners[:, None] == jnp.arange(block_count, dtype=jnp.int32)[None, :]).astype(
        jnp.float32
    )
    same_owner = owners[:, None] == owners[None, :]
    earlier = lax.broadcasted_iota(jnp.int32, (pitch_cells, pitch_cells), 0) < lax.broadcasted_iota(
        jnp.int32, (pitch_cells, pitch_cells), 1
    )
    slot_rank = jnp.sum((same_owner & earlier).astype(jnp.int32), axis=0)
    slot_table = (slot_rank[None, :] == jnp.arange(capacity, dtype=jnp.int32)[:, None]).astype(
        jnp.float32
    )
    placing = onehot.T[:, None, :] * slot_table[None, :, :]
    fluid = fluid_temp
    solid = solid_temp
    gas_rows = span_cells * pitch_cells
    for subiter in range(SUB):
        wall_row = solid[0, 0:1, :]
        wall_temp = jnp.dot(
            onehot,
            lax.all_gather(wall_row, "blk", axis=0, tiled=True),
            precision=lax.Precision.HIGHEST,
            preferred_element_type=jnp.float32,
        )
        flux = film_coeff * (fluid[0] - wall_temp)
        outgoing = jnp.einsum("ocb,bf->ocf", placing, flux, precision=lax.Precision.HIGHEST)
        received = lax.all_to_all(outgoing, "blk", split_axis=0, concat_axis=0, tiled=True)
        inflow = jnp.sum(received, axis=(0, 1))
        conduct = conductivity * (1.0 + 0.25 * jnp.tanh(solid))
        stacked = jnp.concatenate([fluid.reshape(gas_rows, stream_cells), solid[0], conduct[0]], 0)
        stream_ext = padded(stacked, (("blk", 1),), 1, False)
        pitch_extended = padded(fluid, (("sec", 1),), 1, True)
        fluid_stream = stream_ext[:gas_rows].reshape(span_cells, pitch_cells, stream_cells + 2)
        solid_stream = stream_ext[gas_rows : gas_rows + depth_cells][None]
        conduct_stream = stream_ext[gas_rows + depth_cells :][None]
        fluid = fluid_update(
            fluid, stream_velocity, pitch_velocity, flux, pitch_extended, fluid_stream
        )
        solid = solid_update(solid, conduct, inflow[None, :], solid_stream, conduct_stream)
    return (fluid, solid)


def solution(mesh):
    placed = (
        P(None, "sec", "blk"),
        P(None, "sec", "blk"),
        P(None, "sec", "blk"),
        P("sec", "blk"),
        P("sec", None, "blk"),
        P("sec", None, "blk"),
        P("sec", "blk", None, None),
    )
    return jax.shard_map(
        local,
        mesh=mesh,
        in_specs=placed,
        out_specs=(P(None, "sec", "blk"), P("sec", None, "blk")),
        check_vma=False,
    )
```

profile of v0, /device:TPU:0, one launch (start us, length us, event | category | flops | bytes accessed | tf_op | source)
XLA Modules:
  0.0 155.9 jit_solution(16590910425942912968)
XLA Ops:
  0.6 0.8 add_multiply_fusion.3
  1.4 1.0 pad_maximum_fusion.4
  2.6 4.9 %collective-permute-start.2 = (f32[576,1]{1,0:T(8,128)S(1)}, f32[576,1]{1,0:T(8,128)S(1)}, u32[]{:S(2)}, u32[]{:S(2)}) collective-permute-start(f32[576,1]{1,0:T(8,128)S(1)} %get-tuple-element.166), channel_id=1, source_target_pairs={{0,1},{1,2},{2,3},{3,4},{4,5},{5,6},{6,7},{8,9},{9,10},{10,11},{11... | collective-permute-start | bytes 6920 | tf_op jit(solution)/shard_map/ppermute | solution.py:24
  7.4 1.3 collective-permute-start.3
  8.8 1.7 %collective-permute-start.1 = (f32[8,1,128]{2,1,0:T(1,128)S(1)}, f32[8,1,128]{2,1,0:T(1,128)S(1)}, u32[]{:S(2)}, u32[]{:S(2)}) collective-permute-start(f32[8,1,128]{2,1,0:T(1,128)S(1)} %get-tuple-element.185), channel_id=1, source_target_pairs={{8,0},{16,8},{24,16},{0,24},{9,1},{17,9},{25,17},{1,25},{10,2},{18... | collective-permute-start | bytes 12296 | tf_op jit(solution)/shard_map/ppermute | solution.py:27
  10.7 0.6 copy-done.8
  11.4 21.8 %all-gather = f32[8,1,128]{2,1,0:T(1,128)S(1)} all-gather(f32[1,1,128]{2,1,0:T(1,128)S(1)} %get-tuple-element.207), channel_id=2, replica_groups=mesh['sec'=4,'blk'=8] {'blk'}, dimensions={0}, use_global_device_ids=true | all-gather | bytes 4608 | tf_op jit(solution)/shard_map/all_gather | solution.py:101
  33.4 0.3 pad_maximum_fusion
  33.8 0.9 copy-done.1
  34.8 0.3 fusion.51
  35.1 0.5 copy-done.4
  35.5 0.2 constant_dynamic-update-slice_fusion.2
  35.7 0.8 fusion.66
  36.5 3.3 %all-to-all-start = ((f32[8,8,128]{2,1,0:T(8,128)}), f32[8,8,128]{2,1,0:T(8,128)S(1)}, u32[]{:S(2)}, u32[]{:S(2)}) async-start(f32[8,8,128]{2,1,0:T(8,128)} %fusion.66), calls=%async_computation | async-start | bytes 65536 | tf_op jit(solution)/shard_map/all_to_all | solution.py:107
  40.0 1.7 %collective-permute-start.5 = (f32[8,1,128]{2,1,0:T(1,128)S(1)}, f32[8,1,128]{2,1,0:T(1,128)S(1)}, u32[]{:S(2)}, u32[]{:S(2)}) collective-permute-start(f32[8,1,128]{2,1,0:T(1,128)S(1)} %get-tuple-element.179), channel_id=1, source_target_pairs={{8,0},{16,8},{24,16},{0,24},{9,1},{17,9},{25,17},{1,25},{10,2},{18... | collective-permute-start | bytes 12296 | tf_op jit(solution)/shard_map/ppermute | solution.py:27
  41.8 4.7 %all-to-all-done = f32[8,8,128]{2,1,0:T(8,128)S(1)} async-done(((f32[8,8,128]{2,1,0:T(8,128)}), f32[8,8,128]{2,1,0:T(8,128)S(1)}, u32[]{:S(2)}, u32[]{:S(2)}) %all-to-all-start) | async-done | bytes 32800 | tf_op jit(solution)/shard_map/all_to_all | solution.py:107
  46.8 2.4 %collective-permute-start.6 = (f32[576,1]{1,0:T(8,128)S(1)}, f32[576,1]{1,0:T(8,128)S(1)}, u32[]{:S(2)}, u32[]{:S(2)}) collective-permute-start(f32[576,1]{1,0:T(8,128)S(1)} %get-tuple-element.164), channel_id=1, source_target_pairs={{0,1},{1,2},{2,3},{3,4},{4,5},{5,6},{6,7},{8,9},{9,10},{10,11},{11... | collective-permute-start | bytes 6920 | tf_op jit(solution)/shard_map/ppermute | solution.py:24
  49.3 1.3 collective-permute-start.7
  50.6 21.0 %all-gather.1 = f32[8,1,128]{2,1,0:T(1,128)S(1)} all-gather(f32[1,1,128]{2,1,0:T(1,128)S(1)} %slice.737), channel_id=3, replica_groups=mesh['sec'=4,'blk'=8] {'blk'}, dimensions={0}, use_global_device_ids=true | all-gather | bytes 4608 | tf_op jit(solution)/shard_map/all_gather | solution.py:101
  71.6 0.3 pad_maximum_fusion.1
  72.0 0.3 fusion.37
  72.3 0.2 constant_dynamic-update-slice_fusion.1
  72.6 0.8 fusion.64
  73.3 3.3 %all-to-all-start.1 = ((f32[8,8,128]{2,1,0:T(8,128)}), f32[8,8,128]{2,1,0:T(8,128)S(1)}, u32[]{:S(2)}, u32[]{:S(2)}) async-start(f32[8,8,128]{2,1,0:T(8,128)} %fusion.64), calls=%async_computation.1 | async-start | bytes 65536 | tf_op jit(solution)/shard_map/all_to_all | solution.py:107
  76.8 1.7 %collective-permute-start.9 = (f32[8,1,128]{2,1,0:T(1,128)S(1)}, f32[8,1,128]{2,1,0:T(1,128)S(1)}, u32[]{:S(2)}, u32[]{:S(2)}) collective-permute-start(f32[8,1,128]{2,1,0:T(1,128)S(1)} %get-tuple-element.175), channel_id=1, source_target_pairs={{8,0},{16,8},{24,16},{0,24},{9,1},{17,9},{25,17},{1,25},{10,2},{18... | collective-permute-start | bytes 12296 | tf_op jit(solution)/shard_map/ppermute | solution.py:27
  78.7 4.6 %all-to-all-done.1 = f32[8,8,128]{2,1,0:T(8,128)S(1)} async-done(((f32[8,8,128]{2,1,0:T(8,128)}), f32[8,8,128]{2,1,0:T(8,128)S(1)}, u32[]{:S(2)}, u32[]{:S(2)}) %all-to-all-start.1) | async-done | bytes 32800 | tf_op jit(solution)/shard_map/all_to_all | solution.py:107
  83.5 0.1 fusion.141
  83.7 2.4 %collective-permute-start.10 = (f32[576,1]{1,0:T(8,128)S(1)}, f32[576,1]{1,0:T(8,128)S(1)}, u32[]{:S(2)}, u32[]{:S(2)}) collective-permute-start(f32[576,1]{1,0:T(8,128)S(1)} %get-tuple-element.162), channel_id=1, source_target_pairs={{0,1},{1,2},{2,3},{3,4},{4,5},{5,6},{6,7},{8,9},{9,10},{10,11},{11... | collective-permute-start | bytes 6920 | tf_op jit(solution)/shard_map/ppermute | solution.py:24
  86.1 1.3 collective-permute-start.11
  87.4 19.9 %all-gather.2 = f32[8,1,128]{2,1,0:T(1,128)S(1)} all-gather(f32[1,1,128]{2,1,0:T(1,128)S(1)} %slice.761), channel_id=4, replica_groups=mesh['sec'=4,'blk'=8] {'blk'}, dimensions={0}, use_global_device_ids=true | all-gather | bytes 4608 | tf_op jit(solution)/shard_map/all_gather | solution.py:101
  107.3 0.3 pad_maximum_fusion.2
  107.7 0.3 fusion.23
  108.0 0.2 constant_dynamic-update-slice_fusion
  108.3 0.8 fusion.62
  109.0 3.3 %all-to-all-start.2 = ((f32[8,8,128]{2,1,0:T(8,128)}), f32[8,8,128]{2,1,0:T(8,128)S(1)}, u32[]{:S(2)}, u32[]{:S(2)}) async-start(f32[8,8,128]{2,1,0:T(8,128)} %fusion.62), calls=%async_computation.2 | async-start | bytes 65536 | tf_op jit(solution)/shard_map/all_to_all | solution.py:107
  112.4 1.7 %collective-permute-start.13 = (f32[8,1,128]{2,1,0:T(1,128)S(1)}, f32[8,1,128]{2,1,0:T(1,128)S(1)}, u32[]{:S(2)}, u32[]{:S(2)}) collective-permute-start(f32[8,1,128]{2,1,0:T(1,128)S(1)} %get-tuple-element.171), channel_id=1, source_target_pairs={{8,0},{16,8},{24,16},{0,24},{9,1},{17,9},{25,17},{1,25},{10,2},{18... | collective-permute-start | bytes 12296 | tf_op jit(solution)/shard_map/ppermute | solution.py:27
  114.4 4.6 %all-to-all-done.2 = f32[8,8,128]{2,1,0:T(8,128)S(1)} async-done(((f32[8,8,128]{2,1,0:T(8,128)}), f32[8,8,128]{2,1,0:T(8,128)S(1)}, u32[]{:S(2)}, u32[]{:S(2)}) %all-to-all-start.2) | async-done | bytes 32800 | tf_op jit(solution)/shard_map/all_to_all | solution.py:107
  119.2 0.1 fusion.140
  119.3 2.4 %collective-permute-start.14 = (f32[576,1]{1,0:T(8,128)S(1)}, f32[576,1]{1,0:T(8,128)S(1)}, u32[]{:S(2)}, u32[]{:S(2)}) collective-permute-start(f32[576,1]{1,0:T(8,128)S(1)} %get-tuple-element.160), channel_id=1, source_target_pairs={{0,1},{1,2},{2,3},{3,4},{4,5},{5,6},{6,7},{8,9},{9,10},{10,11},{11... | collective-permute-start | bytes 6920 | tf_op jit(solution)/shard_map/ppermute | solution.py:24
  121.7 1.3 collective-permute-start.15
  123.1 20.5 %all-gather.3 = f32[8,1,128]{2,1,0:T(1,128)S(1)} all-gather(f32[1,1,128]{2,1,0:T(1,128)S(1)} %slice.785), channel_id=5, replica_groups=mesh['sec'=4,'blk'=8] {'blk'}, dimensions={0}, use_global_device_ids=true | all-gather | bytes 4608 | tf_op jit(solution)/shard_map/all_gather | solution.py:101
  143.6 0.3 pad_maximum_fusion.3
  144.0 0.3 fusion.9
  144.2 0.2 fusion.68
  144.5 0.8 fusion.60
  145.3 3.3 %all-to-all-start.3 = ((f32[8,8,128]{2,1,0:T(8,128)}), f32[8,8,128]{2,1,0:T(8,128)S(1)}, u32[]{:S(2)}, u32[]{:S(2)}) async-start(f32[8,8,128]{2,1,0:T(8,128)} %fusion.60), calls=%async_computation.3 | async-start | bytes 65536 | tf_op jit(solution)/shard_map/all_to_all | solution.py:107
  148.8 6.4 %all-to-all-done.3 = f32[8,8,128]{2,1,0:T(8,128)S(1)} async-done(((f32[8,8,128]{2,1,0:T(8,128)}), f32[8,8,128]{2,1,0:T(8,128)S(1)}, u32[]{:S(2)}, u32[]{:S(2)}) %all-to-all-start.3) | async-done | bytes 32800 | tf_op jit(solution)/shard_map/all_to_all | solution.py:107
  155.3 0.6 copy-done.7
  (103 shorter events, 2.4 us)
Async XLA Ops:
  0.6 0.8 copy-start.3
  2.4 6.3 %copy-start = (f32[8,64,128]{2,1,0:T(8,128)S(1)}, f32[8,64,128]{2,1,0:T(8,128)}, u32[]{:S(2)}) copy-start(f32[8,64,128]{2,1,0:T(8,128)} %param.31) | copy-start | bytes 786436
  2.6 30.7 %collective-permute-start.2 = (f32[576,1]{1,0:T(8,128)S(1)}, f32[576,1]{1,0:T(8,128)S(1)}, u32[]{:S(2)}, u32[]{:S(2)}) collective-permute-start(f32[576,1]{1,0:T(8,128)S(1)} %get-tuple-element.166), channel_id=1, source_target_pairs={{0,1},{1,2},{2,3},{3,4},{4,5},{5,6},{6,7},{8,9},{9,10},{10,11},{11... | collective-permute-start | bytes 6920 | tf_op jit(solution)/shard_map/ppermute | solution.py:24
  7.4 25.8 %collective-permute-start.3 = (f32[576,1]{1,0:T(8,128)S(1)}, f32[576,1]{1,0:T(8,128)S(1)}, u32[]{:S(2)}, u32[]{:S(2)}) collective-permute-start(f32[576,1]{1,0:T(8,128)S(1)} %get-tuple-element.167), channel_id=1, source_target_pairs={{1,0},{2,1},{3,2},{4,3},{5,4},{6,5},{7,6},{9,8},{10,9},{11,10},{12... | collective-permute-start | bytes 6920 | tf_op jit(solution)/shard_map/ppermute | solution.py:27
  8.8 25.0 %collective-permute-start = (f32[8,1,128]{2,1,0:T(1,128)S(1)}, f32[8,1,128]{2,1,0:T(1,128)S(1)}, u32[]{:S(2)}, u32[]{:S(2)}) collective-permute-start(f32[8,1,128]{2,1,0:T(1,128)S(1)} %get-tuple-element.184), channel_id=1, source_target_pairs={{0,8},{8,16},{16,24},{24,0},{1,9},{9,17},{17,25},{25,1},{2,10},{10... | collective-permute-start | bytes 12296 | tf_op jit(solution)/shard_map/ppermute | solution.py:24
  8.8 25.0 %collective-permute-start.1 = (f32[8,1,128]{2,1,0:T(1,128)S(1)}, f32[8,1,128]{2,1,0:T(1,128)S(1)}, u32[]{:S(2)}, u32[]{:S(2)}) collective-permute-start(f32[8,1,128]{2,1,0:T(1,128)S(1)} %get-tuple-element.185), channel_id=1, source_target_pairs={{8,0},{16,8},{24,16},{0,24},{9,1},{17,9},{25,17},{1,25},{10,2},{18... | collective-permute-start | bytes 12296 | tf_op jit(solution)/shard_map/ppermute | solution.py:27
  10.6 0.7 copy-start.8
  33.7 1.0 copy-start.1
  33.8 1.0 copy-start.2
  34.8 0.8 copy-start.4
  36.5 10.0 %all-to-all-start = ((f32[8,8,128]{2,1,0:T(8,128)}), f32[8,8,128]{2,1,0:T(8,128)S(1)}, u32[]{:S(2)}, u32[]{:S(2)}) async-start(f32[8,8,128]{2,1,0:T(8,128)} %fusion.66), calls=%async_computation | async-start | bytes 65536 | tf_op jit(solution)/shard_map/all_to_all | solution.py:107
  40.0 32.0 %collective-permute-start.4 = (f32[8,1,128]{2,1,0:T(1,128)S(1)}, f32[8,1,128]{2,1,0:T(1,128)S(1)}, u32[]{:S(2)}, u32[]{:S(2)}) collective-permute-start(f32[8,1,128]{2,1,0:T(1,128)S(1)} %get-tuple-element.178), channel_id=1, source_target_pairs={{0,8},{8,16},{16,24},{24,0},{1,9},{9,17},{17,25},{25,1},{2,10},{10... | collective-permute-start | bytes 12296 | tf_op jit(solution)/shard_map/ppermute | solution.py:24
  40.0 6.6 %copy-start.6 = (f32[1,32,128]{2,1,0:T(8,128)S(1)}, f32[1,32,128]{2,1,0:T(8,128)}, u32[]{:S(2)}) copy-start(f32[1,32,128]{2,1,0:T(8,128)} %param.36) | copy-start | bytes 49156
  40.0 31.9 %collective-permute-start.5 = (f32[8,1,128]{2,1,0:T(1,128)S(1)}, f32[8,1,128]{2,1,0:T(1,128)S(1)}, u32[]{:S(2)}, u32[]{:S(2)}) collective-permute-start(f32[8,1,128]{2,1,0:T(1,128)S(1)} %get-tuple-element.179), channel_id=1, source_target_pairs={{8,0},{16,8},{24,16},{0,24},{9,1},{17,9},{25,17},{1,25},{10,2},{18... | collective-permute-start | bytes 12296 | tf_op jit(solution)/shard_map/ppermute | solution.py:27
  46.8 24.8 %collective-permute-start.6 = (f32[576,1]{1,0:T(8,128)S(1)}, f32[576,1]{1,0:T(8,128)S(1)}, u32[]{:S(2)}, u32[]{:S(2)}) collective-permute-start(f32[576,1]{1,0:T(8,128)S(1)} %get-tuple-element.164), channel_id=1, source_target_pairs={{0,1},{1,2},{2,3},{3,4},{4,5},{5,6},{6,7},{8,9},{9,10},{10,11},{11... | collective-permute-start | bytes 6920 | tf_op jit(solution)/shard_map/ppermute | solution.py:24
  49.3 22.4 %collective-permute-start.7 = (f32[576,1]{1,0:T(8,128)S(1)}, f32[576,1]{1,0:T(8,128)S(1)}, u32[]{:S(2)}, u32[]{:S(2)}) collective-permute-start(f32[576,1]{1,0:T(8,128)S(1)} %get-tuple-element.165), channel_id=1, source_target_pairs={{1,0},{2,1},{3,2},{4,3},{5,4},{6,5},{7,6},{9,8},{10,9},{11,10},{12... | collective-permute-start | bytes 6920 | tf_op jit(solution)/shard_map/ppermute | solution.py:27
  73.3 10.0 %all-to-all-start.1 = ((f32[8,8,128]{2,1,0:T(8,128)}), f32[8,8,128]{2,1,0:T(8,128)S(1)}, u32[]{:S(2)}, u32[]{:S(2)}) async-start(f32[8,8,128]{2,1,0:T(8,128)} %fusion.64), calls=%async_computation.1 | async-start | bytes 65536 | tf_op jit(solution)/shard_map/all_to_all | solution.py:107
  76.7 31.0 %collective-permute-start.8 = (f32[8,1,128]{2,1,0:T(1,128)S(1)}, f32[8,1,128]{2,1,0:T(1,128)S(1)}, u32[]{:S(2)}, u32[]{:S(2)}) collective-permute-start(f32[8,1,128]{2,1,0:T(1,128)S(1)} %get-tuple-element.174), channel_id=1, source_target_pairs={{0,8},{8,16},{16,24},{24,0},{1,9},{9,17},{17,25},{25,1},{2,10},{10... | collective-permute-start | bytes 12296 | tf_op jit(solution)/shard_map/ppermute | solution.py:24
  76.8 30.9 %collective-permute-start.9 = (f32[8,1,128]{2,1,0:T(1,128)S(1)}, f32[8,1,128]{2,1,0:T(1,128)S(1)}, u32[]{:S(2)}, u32[]{:S(2)}) collective-permute-start(f32[8,1,128]{2,1,0:T(1,128)S(1)} %get-tuple-element.175), channel_id=1, source_target_pairs={{8,0},{16,8},{24,16},{0,24},{9,1},{17,9},{25,17},{1,25},{10,2},{18... | collective-permute-start | bytes 12296 | tf_op jit(solution)/shard_map/ppermute | solution.py:27
  83.7 23.7 %collective-permute-start.10 = (f32[576,1]{1,0:T(8,128)S(1)}, f32[576,1]{1,0:T(8,128)S(1)}, u32[]{:S(2)}, u32[]{:S(2)}) collective-permute-start(f32[576,1]{1,0:T(8,128)S(1)} %get-tuple-element.162), channel_id=1, source_target_pairs={{0,1},{1,2},{2,3},{3,4},{4,5},{5,6},{6,7},{8,9},{9,10},{10,11},{11... | collective-permute-start | bytes 6920 | tf_op jit(solution)/shard_map/ppermute | solution.py:24
  86.1 21.2 %collective-permute-start.11 = (f32[576,1]{1,0:T(8,128)S(1)}, f32[576,1]{1,0:T(8,128)S(1)}, u32[]{:S(2)}, u32[]{:S(2)}) collective-permute-start(f32[576,1]{1,0:T(8,128)S(1)} %get-tuple-element.163), channel_id=1, source_target_pairs={{1,0},{2,1},{3,2},{4,3},{5,4},{6,5},{7,6},{9,8},{10,9},{11,10},{12... | collective-permute-start | bytes 6920 | tf_op jit(solution)/shard_map/ppermute | solution.py:27
  109.0 10.0 %all-to-all-start.2 = ((f32[8,8,128]{2,1,0:T(8,128)}), f32[8,8,128]{2,1,0:T(8,128)S(1)}, u32[]{:S(2)}, u32[]{:S(2)}) async-start(f32[8,8,128]{2,1,0:T(8,128)} %fusion.62), calls=%async_computation.2 | async-start | bytes 65536 | tf_op jit(solution)/shard_map/all_to_all | solution.py:107
  112.4 31.6 %collective-permute-start.12 = (f32[8,1,128]{2,1,0:T(1,128)S(1)}, f32[8,1,128]{2,1,0:T(1,128)S(1)}, u32[]{:S(2)}, u32[]{:S(2)}) collective-permute-start(f32[8,1,128]{2,1,0:T(1,128)S(1)} %get-tuple-element.170), channel_id=1, source_target_pairs={{0,8},{8,16},{16,24},{24,0},{1,9},{9,17},{17,25},{25,1},{2,10},{10... | collective-permute-start | bytes 12296 | tf_op jit(solution)/shard_map/ppermute | solution.py:24
  112.4 31.5 %collective-permute-start.13 = (f32[8,1,128]{2,1,0:T(1,128)S(1)}, f32[8,1,128]{2,1,0:T(1,128)S(1)}, u32[]{:S(2)}, u32[]{:S(2)}) collective-permute-start(f32[8,1,128]{2,1,0:T(1,128)S(1)} %get-tuple-element.171), channel_id=1, source_target_pairs={{8,0},{16,8},{24,16},{0,24},{9,1},{17,9},{25,17},{1,25},{10,2},{18... | collective-permute-start | bytes 12296 | tf_op jit(solution)/shard_map/ppermute | solution.py:27
  119.3 24.3 %collective-permute-start.14 = (f32[576,1]{1,0:T(8,128)S(1)}, f32[576,1]{1,0:T(8,128)S(1)}, u32[]{:S(2)}, u32[]{:S(2)}) collective-permute-start(f32[576,1]{1,0:T(8,128)S(1)} %get-tuple-element.160), channel_id=1, source_target_pairs={{0,1},{1,2},{2,3},{3,4},{4,5},{5,6},{6,7},{8,9},{9,10},{10,11},{11... | collective-permute-start | bytes 6920 | tf_op jit(solution)/shard_map/ppermute | solution.py:24
  121.7 21.9 %collective-permute-start.15 = (f32[576,1]{1,0:T(8,128)S(1)}, f32[576,1]{1,0:T(8,128)S(1)}, u32[]{:S(2)}, u32[]{:S(2)}) collective-permute-start(f32[576,1]{1,0:T(8,128)S(1)} %get-tuple-element.161), channel_id=1, source_target_pairs={{1,0},{2,1},{3,2},{4,3},{5,4},{6,5},{7,6},{9,8},{10,9},{11,10},{12... | collective-permute-start | bytes 6920 | tf_op jit(solution)/shard_map/ppermute | solution.py:27
  144.5 4.2 %copy-start.5 = (f32[8,64,128]{2,1,0:T(8,128)}, f32[8,64,128]{2,1,0:T(8,128)S(1)}, u32[]{:S(2)}) copy-start(f32[8,64,128]{2,1,0:T(8,128)S(1)} %get-tuple-element.215) | copy-start | bytes 786436
  145.3 10.0 %all-to-all-start.3 = ((f32[8,8,128]{2,1,0:T(8,128)}), f32[8,8,128]{2,1,0:T(8,128)S(1)}, u32[]{:S(2)}, u32[]{:S(2)}) async-start(f32[8,8,128]{2,1,0:T(8,128)} %fusion.60), calls=%async_computation.3 | async-start | bytes 65536 | tf_op jit(solution)/shard_map/all_to_all | solution.py:107
  155.3 0.6 copy-start.7
where the time goes:
time: 157 us; the launch traced here: 156 us
  blocking collectives  83.3 us (53%)
  starting transfers between devices  37.7 us (24%)
  waiting for transfers between devices  20.5 us (13%)
  other arithmetic  5.14 us (3%)
  local copies, waits for them, and re-layouts  3.96 us (3%)
  matrix products  3.96 us (3%)
    all_gather x4, blocking collectives, local(): lax.all_gather(wall_row, 'blk', axis=0, tiled=True)  83.3 us
    all_to_all x4, waiting for transfers between devices, local(): lax.all_to_all(outgoing, 'blk', split_axis=0, concat_axis=0, tiled=True)  20.4 us
    all_to_all x4, starting transfers between devices, local(): lax.all_to_all(outgoing, 'blk', split_axis=0, concat_axis=0, tiled=True)  13.4 us
    ppermute x8, starting transfers between devices, padded(): lax.ppermute(lax.slice_in_dim(block, block.shape[dim] - width, None, axis...  12.3 us
    ppermute x8, starting transfers between devices, padded(): lax.ppermute(lax.slice_in_dim(block, 0, width, axis=dim), axis, backward)  12.1 us
  transfers between devices with their start and end apart: 20, of which 4 were waited for; matrix products, arithmetic and copies ran while one was open for 2% of the time, Pallas kernels for 0%

commit v1 on v0

--- a/solution.py
+++ b/solution.py
@@ -1,6 +1,8 @@
 import jax
 import jax.numpy as jnp
 from jax import lax
+from jax.experimental import pallas as pl
+from jax.experimental.pallas import tpu as pltpu
 from jax.sharding import PartitionSpec as P
 
 SUB = 4
@@ -12,6 +14,550 @@
 SOLID_STEP = 0.04
 COOLING = 0.5
 COOLANT = -1.0
+
+F32 = jnp.float32
+NB = 8
+FZ = 8
+FP = 64
+FS = 128
+SD = 32
+R0 = 48
+R1 = 40
+
+
+def lanes(rows):
+    return lax.broadcasted_iota(jnp.int32, (rows, FS), 1)
+
+
+def subs(rows):
+    return lax.broadcasted_iota(jnp.int32, (rows, FS), 0)
+
+
+def turn(x, shift, axis=1):
+    return pltpu.roll(x, shift % x.shape[axis], axis)
+
+
+def by_owner(owner, values):
+    sub = subs(NB)
+    outs = [jnp.zeros((NB, FS), F32) for _ in values]
+    for o in range(NB):
+        mine = owner == o
+        for i, value in enumerate(values):
+            total = jnp.sum(jnp.where(mine, value, 0.0), axis=0, keepdims=True)
+            outs[i] = jnp.where(sub == o, total, outs[i])
+    return outs
+
+
+def pick(owner, table):
+    out = jnp.zeros(owner.shape, F32)
+    for o in range(NB):
+        out = jnp.where(owner == o, table[o : o + 1], out)
+    return out
+
+
+def pick_lane(owner_row, table, lane):
+    column = jnp.broadcast_to(table[:, lane : lane + 1], (NB, FS))
+    named = jnp.broadcast_to(owner_row, (NB, FS)) == subs(NB).astype(F32)
+    return jnp.sum(jnp.where(named, column, 0.0), axis=0, keepdims=True)
+
+
+def stencil(x, low, high, left, right, below, above, sv, pv):
+    spread = SPREAD * (low + high + left + right + below + above - 6.0 * x)
+    carried = (
+        -ADVECT * sv * (x - left)
+        - ADVECT * jnp.maximum(pv, 0.0) * (x - low)
+        + ADVECT * jnp.maximum(-pv, 0.0) * (high - x)
+    )
+    return x + spread + carried
+
+
+def span(x):
+    sub = subs(FZ)
+    below = jnp.where(sub == 0, x, turn(x, 1, 0))
+    above = jnp.where(sub == FZ - 1, x, turn(x, FZ - 1, 0))
+    return below, above
+
+
+def halo_column(x, corners, left, right, sv, pv, film, wall, keep):
+    lane = lanes(FZ)
+    low = jnp.where(lane == 0, turn(corners, 32), turn(x, 1))
+    high = jnp.where(lane == FP - 1, turn(corners, FP - 1 - 97), turn(x, -1))
+    below, above = span(x)
+    new = stencil(x, low, high, left, right, below, above, sv, pv)
+    new = new - jnp.where(subs(FZ) == 0, WALL * film * (x - wall), 0.0)
+    return new * keep
+
+
+def halo_row(x, low, high, left_corner, right_corner, sv, pv, film, wall):
+    lane = lanes(FZ)
+    left = jnp.where(lane == 0, left_corner, turn(x, 1))
+    right = jnp.where(lane == FS - 1, right_corner, turn(x, -1))
+    below, above = span(x)
+    new = stencil(x, low, high, left, right, below, above, sv, pv)
+    return new - jnp.where(subs(FZ) == 0, WALL * film * (x - wall), 0.0)
+
+
+def advance(src, dst, low_row, high_row, columns, base, sv, pv, film, wall):
+    lane = lanes(FP)
+    sub = subs(FP)
+    for z in range(FZ):
+        x = src[z]
+        low = jnp.where(sub == 0, low_row[z : z + 1], turn(x, 1, 0))
+        high = jnp.where(sub == FP - 1, high_row[z : z + 1], turn(x, -1, 0))
+        edge = turn(columns, -(base + 2 * z + 1))
+        left = jnp.where(lane == 0, edge, turn(x, 1))
+        right = jnp.where(lane == FS - 1, edge, turn(x, -1))
+        new = stencil(
+            x, low, high, left, right, src[max(z - 1, 0)], src[min(z + 1, FZ - 1)], sv[z], pv[z]
+        )
+        if z == 0:
+            new = new - WALL * film * (x - wall)
+        dst[z] = new
+
+
+def strip_row(here, k_here, under, k_under):
+    sub, lane = subs(NB), lanes(NB)
+
+    def prev(x):
+        moved = turn(x, 1)
+        carried = jnp.where(sub == 0, 0.0, turn(moved, 1, 0))
+        return jnp.where(lane == 0, carried, moved)
+
+    def following(x):
+        moved = turn(x, -1)
+        carried = jnp.where(sub == NB - 1, 0.0, turn(moved, -1, 0))
+        return jnp.where(lane == FS - 1, carried, moved)
+
+    flow = (
+        0.5 * (k_here + prev(k_here)) * (prev(here) - here)
+        + 0.5 * (k_here + following(k_here)) * (following(here) - here)
+        + 0.5 * (k_here + k_under) * (under - here)
+    )
+    return here + SOLID_STEP * flow
+
+
+def conduct_of(conductivity, solid):
+    return conductivity * (1.0 + 0.25 * jnp.tanh(solid))
+
+
+def metal_step(own, halo, c_own, c_halo, keep):
+    k_own, k_halo = conduct_of(c_own, own), conduct_of(c_halo, halo)
+    lane, sub = lanes(SD), subs(SD)
+
+    def depth(x):
+        up = jnp.where(sub == 0, x, turn(x, 1, 0))
+        down = jnp.where(sub == SD - 1, x, turn(x, -1, 0))
+        return up, down
+
+    def stream(x, other):
+        prev = jnp.where(lane == 0, turn(other, 1), turn(x, 1))
+        following = jnp.where(lane == FS - 1, turn(other, -1), turn(x, -1))
+        return prev, following
+
+    def update(x, k, other, k_other):
+        flow = jnp.zeros_like(x)
+        for (a, ka) in zip(stream(x, other) + depth(x), stream(k, k_other) + depth(k)):
+            flow = flow + 0.5 * (k + ka) * (a - x)
+        new = x + SOLID_STEP * flow
+        return new + jnp.where(sub == SD - 1, SOLID_STEP * COOLING * (COOLANT - x), 0.0)
+
+    return update(own, k_own, halo, k_halo), update(halo, k_halo, own, k_own) * keep
+
+
+def add_inflow(own, halo, inflow, me, keep):
+    sub, lane = subs(SD), lanes(SD)
+    row = subs(NB)
+    mine = jnp.sum(jnp.where(row == me, inflow, 0.0), axis=0, keepdims=True)
+    before = jnp.sum(jnp.where(row == me - 1, inflow, 0.0), axis=0, keepdims=True)
+    after = jnp.sum(jnp.where(row == me + 1, inflow, 0.0), axis=0, keepdims=True)
+    beside = jnp.where(lane >= FS // 2, before, after)
+    own = own + jnp.where(sub == 0, SOLID_STEP * mine, 0.0)
+    halo = halo + jnp.where(sub == 0, SOLID_STEP * beside, 0.0) * keep
+    return own, halo
+
+
+def column_blocks(mt):
+    right = mt[pl.ds(1, FZ, stride=4), :], mt[pl.ds(0, FZ, stride=4), :]
+    left = mt[pl.ds(2, FZ, stride=4), :], mt[pl.ds(3, FZ, stride=4), :]
+    return right, left
+
+
+def with_corners(block, low, high, lane_from):
+    lane = lanes(FZ)
+    block = jnp.where(lane == 96, turn(low, 96 - lane_from), block)
+    return jnp.where(lane == 97, turn(high, 97 - lane_from), block)
+
+
+def gather_columns(fluid, lane):
+    acc = jnp.zeros((FP, FS), F32)
+    for z in range(FZ):
+        acc = jnp.where(lane // 4 == z, turn(fluid[z], 4 * z + 2), acc)
+    return acc
+
+
+def first_kernel(fluid, sv, pv, film, solid, cond, owner, mt, sums):
+    lane = lanes(FP)
+    named = jnp.broadcast_to(owner[...], (FP, FS))
+    top = gather_columns(fluid, lane)
+    bottom = jnp.zeros((FP, FS), F32)
+    pair = (lane - 32) // 2
+    for z in range(FZ):
+        here = (pair == z) & (lane >= 32)
+        top = jnp.where(here, turn(pv[z], 33 + 2 * z), top)
+        bottom = jnp.where(here, turn(sv[z], 33 + 2 * z), bottom)
+    top = jnp.where(lane // 2 == 24, turn(film[...], 49), top)
+    top = jnp.where(lane == 50, named.astype(F32), top)
+    metal = bottom[:SD]
+    thin = lanes(SD)
+    s, c = solid[...], cond[...]
+    for k in range(4):
+        metal = jnp.where(thin == 4 * k + 1, turn(s, 3 * k + 5), metal)
+        metal = jnp.where(thin == 4 * k + 2, turn(s, 3 * k + 2), metal)
+        metal = jnp.where(thin == 4 * k + 17, turn(c, 3 * k + 21), metal)
+        metal = jnp.where(thin == 4 * k + 18, turn(c, 3 * k + 18), metal)
+    whole = jnp.concatenate([top, metal, bottom[SD:]], axis=0)
+    mt[...] = whole.T
+    sums[0:8, :], sums[8:16, :] = by_owner(named, [film[...] * fluid[0], film[...]])
+
+
+def pack_kernel(mt, sums, solid, cond, lo, hi, out):
+    me = lax.axis_index("blk")
+    lane, sub = lanes(FZ), subs(FZ)
+    (r0, r1), (l0, l1) = column_blocks(mt)
+    r2, l2 = mt[pl.ds(32, FZ, stride=2), :], mt[pl.ds(33, FZ, stride=2), :]
+    low, high = lo[8:16, :], hi[8:16, :]
+    r0 = with_corners(r0, low, high, FS - 1)
+    l0 = with_corners(l0, low, high, 0)
+    owner = turn(mt[50:51, :], 64)
+
+    def with_walls(block, film):
+        extra = jnp.where(sub == 0, turn(film, 64), jnp.where(sub == 1, owner, 0.0))
+        return jnp.where(lane >= 64, extra, block)
+
+    r1, l1 = with_walls(r1, mt[48:49, :]), with_walls(l1, mt[49:50, :])
+    head = jnp.concatenate(
+        [solid[0:2, :], cond[0:2, :], lo[33:34, :], hi[33:34, :], lo[34:35, :], hi[34:35, :]], axis=0
+    )
+    for peer in range(NB):
+        out[peer, 0:8, :] = head
+        out[peer, 8:24, :] = sums[...]
+        ahead = (me + 1 == peer).astype(F32)
+        behind = (me - 1 == peer).astype(F32)
+        for i, (r, l) in enumerate(((r0, l0), (r1, l1), (r2, l2))):
+            out[peer, 24 + 8 * i : 32 + 8 * i, :] = r * ahead + l * behind
+
+
+def neighbours(recv, me, count):
+    before = jnp.maximum(me - 1, 0)
+    after = jnp.minimum(me + 1, NB - 1)
+    keep_l = (me > 0).astype(F32)
+    keep_r = (me < NB - 1).astype(F32)
+    start = 24
+    left = [recv[before, start + 8 * i : start + 8 * i + 8, :] * keep_l for i in range(count)]
+    right = [recv[after, start + 8 * i : start + 8 * i + 8, :] * keep_r for i in range(count)]
+    return left, right, keep_l, keep_r
+
+
+def edge_terms(blocks):
+    sv = turn(blocks[2], 64)
+    film, owner = turn(blocks[1][0:1], 64), turn(blocks[1][1:2], 64)
+    return sv, blocks[2], film, owner
+
+
+def second_kernel(
+    recv, mt, fluid, sv, pv, film, solid, cond, owner, lo, hi, fluid2, up, down, metal, tm, fluid1
+):
+    me = lax.axis_index("blk")
+    left, right, keep_l, keep_r = neighbours(recv, me, 3)
+    sv_l, pv_l, film_l, own_l = edge_terms(left)
+    sv_r, pv_r, film_r, own_r = edge_terms(right)
+    wall0, under0 = recv[:, 0, :], recv[:, 1, :]
+    c0, c1 = recv[:, 2, :], recv[:, 3, :]
+    a0, h = recv[0, 8:16, :], recv[0, 16:24, :]
+    for j in range(1, NB):
+        a0, h = a0 + recv[j, 8:16, :], h + recv[j, 16:24, :]
+    inflow0 = a0 - h * wall0
+    wall1 = strip_row(wall0, conduct_of(c0, wall0), under0, conduct_of(c1, under0))
+    wall1 = wall1 + SOLID_STEP * inflow0
+
+    own_cols, _ = None, None
+    mine_right, mine_left = mt[pl.ds(1, FZ, stride=4), :], mt[pl.ds(2, FZ, stride=4), :]
+    new_l = halo_column(
+        left[0], left[0], left[1], mine_left, sv_l, pv_l, film_l,
+        pick_lane(own_l, wall0, FS - 1), keep_l,
+    )
+    new_r = halo_column(
+        right[0], right[0], mine_right, right[1], sv_r, pv_r, film_r,
+        pick_lane(own_r, wall0, 0), keep_r,
+    )
+    tm[...] = jnp.zeros((FS, FS), F32)
+    tm[pl.ds(0, FZ, stride=2), :] = right[0]
+    tm[pl.ds(1, FZ, stride=2), :] = left[0]
+    tm[16:24, :] = left[0]
+    tm[24:32, :] = right[0]
+    tm[pl.ds(32, FZ, stride=2), :] = new_r
+    tm[pl.ds(33, FZ, stride=2), :] = new_l
+    turned = tm[...].T
+    columns = turned[:FP]
+    deep = turned[64 : 64 + SD]
+    thin = lanes(SD)
+    halo = jnp.where(thin >= 124, turn(deep, 108), jnp.where(thin < 4, turn(deep, 104), 0.0))
+    c_halo = jnp.where(thin >= 124, turn(deep, 104), jnp.where(thin < 4, turn(deep, 100), 0.0))
+    keep = jnp.where(thin >= 64, keep_l, keep_r)
+
+    low, high = lo[8:16, :], hi[8:16, :]
+    first, last = fluid[:, 0, :], fluid[:, FP - 1, :]
+    wall_lo = pick(lo[34:35, :], recv[:, 4, :])
+    wall_hi = pick(hi[34:35, :], recv[:, 5, :])
+    new_low = halo_row(
+        low, lo[0:8, :], first, turn(left[0], 32), turn(right[0], 31),
+        lo[16:24, :], lo[24:32, :], lo[32:33, :], wall_lo,
+    )
+    new_high = halo_row(
+        high, last, hi[0:8, :], turn(left[0], 31), turn(right[0], 30),
+        hi[16:24, :], hi[24:32, :], hi[32:33, :], wall_hi,
+    )
+    named = jnp.broadcast_to(owner[...], (FP, FS))
+    walls0, walls1 = pick(named, wall0), pick(named, wall1)
+    advance(fluid, fluid1, low, high, columns, 0, sv, pv, film[...], walls0)
+    advance(fluid1, fluid2, new_low, new_high, columns, 32, sv, pv, film[...], walls1)
+    (flux,) = by_owner(named, [film[...] * (fluid1[0] - walls1)])
+
+    own, halo = metal_step(solid[...], halo, cond[...], c_halo, keep)
+    own, halo = add_inflow(own, halo, inflow0, me, keep)
+    own, halo = metal_step(own, halo, cond[...], c_halo, keep)
+    metal[0:SD, :] = own
+    metal[SD : 2 * SD, :] = halo
+    metal[2 * SD : 3 * SD, :] = c_halo
+    up[0:8, :], up[8:16, :] = fluid2[:, FP - 2, :], fluid2[:, FP - 1, :]
+    down[0:8, :], down[8:16, :] = fluid2[:, 1, :], fluid2[:, 0, :]
+    for ref in (up, down):
+        ref[16:24, :] = flux
+        ref[24:32, :] = own[0:8]
+
+
+def sums_kernel(recv, fluid2, sv, pv, film, owner, mt, sums):
+    me = lax.axis_index("blk")
+    left, right, keep_l, keep_r = neighbours(recv, me, 3)
+    _, _, film_l, own_l = edge_terms(left)
+    sv_r, _, film_r, own_r = edge_terms(right)
+    lane, sub = lanes(FP), subs(FP)
+    named = jnp.broadcast_to(owner[...], (FP, FS))
+    x, f = fluid2[0], film[...]
+    low = jnp.where(sub == 0, 0.0, turn(x, 1, 0))
+    high = jnp.where(sub == FP - 1, 0.0, turn(x, -1, 0))
+    before = jnp.where(lane == 0, 0.0, turn(x, 1))
+    after = jnp.where(lane == FS - 1, 0.0, turn(x, -1))
+    moved = stencil(x, low, high, before, after, x, fluid2[1], sv[0], pv[0]) - WALL * f * x
+    a2, b3, h2 = by_owner(named, [f * x, f * moved, f * f])
+    whole = jnp.concatenate([gather_columns(fluid2, lane), jnp.zeros((FP, FS), F32)], axis=0)
+    mt[0:FS, :] = whole.T
+    thin = subs(NB)
+    inside = lanes(NB) < FP
+    right_term = film_r * (SPREAD + ADVECT * sv_r[0:1]) * mt[1:2, :] * keep_r
+    left_term = film_l * SPREAD * mt[2:3, :] * keep_l
+
+    def shared(own_row, term):
+        hit = (jnp.broadcast_to(own_row, (NB, FS)) == thin.astype(F32)) & inside
+        return jnp.sum(jnp.where(hit, term, 0.0), axis=1, keepdims=True)
+
+    b3 = b3 + jnp.where(lanes(NB) == 0, shared(own_r, right_term), 0.0)
+    b3 = b3 + jnp.where(lanes(NB) == FS - 1, shared(own_l, left_term), 0.0)
+    top, end = f[0:1], f[FP - 1 : FP]
+    up = top * (SPREAD + ADVECT * jnp.maximum(pv[0, 0:1, :], 0.0))
+    down = end * (SPREAD + ADVECT * jnp.maximum(-pv[0, FP - 1 : FP, :], 0.0))
+    mt[FS : FS + 8, :] = jnp.concatenate(
+        [up, down, named[0:1].astype(F32), named[FP - 1 : FP].astype(F32), jnp.zeros((4, FS), F32)],
+        axis=0,
+    )
+    sums[0:8, :], sums[8:16, :], sums[16:24, :] = a2, b3, h2
+
+
+def send_kernel(recv, mt, sums, up, metal, lo, hi, out):
+    me = lax.axis_index("blk")
+    sub = subs(NB)
+    rows = sub.astype(F32)
+    (r0, r1), (l0, l1) = column_blocks(mt)
+    low, high = lo[8:16, :], hi[8:16, :]
+    r0 = with_corners(r0, low, high, FS - 1)
+    l0 = with_corners(l0, low, high, 0)
+    b3 = sums[8:16, :]
+    b3 = b3 + jnp.where(rows == mt[FS + 2 : FS + 3, :], mt[FS : FS + 1, :] * low[0:1], 0.0)
+    b3 = b3 + jnp.where(rows == mt[FS + 3 : FS + 4, :], mt[FS + 1 : FS + 2, :] * high[0:1], 0.0)
+    relay_lo = pick(recv[:, 6, :], lo[16:24, :])
+    relay_hi = pick(recv[:, 7, :], hi[16:24, :])
+    h2 = sums[16:24, :]
+    for peer in range(NB):
+        out[peer, 0:8, :] = jnp.concatenate(
+            [
+                metal[0:2, :],
+                lo[24:25, :],
+                hi[24:25, :],
+                b3[peer : peer + 1],
+                h2[peer : peer + 1],
+                relay_lo[peer : peer + 1],
+                relay_hi[peer : peer + 1],
+            ],
+            axis=0,
+        )
+        out[peer, 8:16, :] = up[16:24, :]
+        out[peer, 16:24, :] = sums[0:8, :]
+        ahead = (me + 1 == peer).astype(F32)
+        behind = (me - 1 == peer).astype(F32)
+        out[peer, 24:32, :] = r0 * ahead + l0 * behind
+        out[peer, 32:40, :] = r1 * ahead + l1 * behind
+
+
+def last_kernel(
+    recv1, recv, mt, fluid2, sv, pv, film, cond, owner, lo, hi, lo1, hi1, metal, fluid_out, solid_out,
+    tm, fluid3,
+):
+    me = lax.axis_index("blk")
+    stat_l, stat_r, keep_l, keep_r = neighbours(recv, me, 3)
+    left, right, _, _ = neighbours(recv1, me, 2)
+    sv_l, pv_l, film_l, own_l = edge_terms(stat_l)
+    sv_r, pv_r, film_r, own_r = edge_terms(stat_r)
+    c0, c1 = recv[:, 2, :], recv[:, 3, :]
+    h = recv[0, 16:24, :]
+    tail, inflow1, a2 = recv1[0, 0:8, :], recv1[0, 8:16, :], recv1[0, 16:24, :]
+    for j in range(1, NB):
+        h = h + recv[j, 16:24, :]
+        tail = tail + recv1[j, 0:8, :]
+        inflow1 = inflow1 + recv1[j, 8:16, :]
+        a2 = a2 + recv1[j, 16:24, :]
+    wall2 = recv1[:, 0, :] + SOLID_STEP * inflow1
+    under2 = recv1[:, 1, :]
+    inflow2 = a2 - h * wall2
+    wall3 = strip_row(wall2, conduct_of(c0, wall2), under2, conduct_of(c1, under2))
+    wall3 = wall3 + SOLID_STEP * inflow2
+    inflow3 = tail[4:5] + WALL * tail[5:6] * wall2 - h * wall3
+    wall_lo = pick(lo[34:35, :], recv1[:, 2, :]) + SOLID_STEP * tail[6:7]
+    wall_hi = pick(hi[34:35, :], recv1[:, 3, :]) + SOLID_STEP * tail[7:8]
+
+    mine_right, mine_left = mt[pl.ds(1, FZ, stride=4), :], mt[pl.ds(2, FZ, stride=4), :]
+    new_l = halo_column(
+        left[0], left[0], left[1], mine_left, sv_l, pv_l, film_l,
+        pick_lane(own_l, wall2, FS - 1), keep_l,
+    )
+    new_r = halo_column(
+        right[0], right[0], mine_right, right[1], sv_r, pv_r, film_r,
+        pick_lane(own_r, wall2, 0), keep_r,
+    )
+    tm[...] = jnp.zeros((FS, FS), F32)
+    tm[pl.ds(0, FZ, stride=2), :] = right[0]
+    tm[pl.ds(1, FZ, stride=2), :] = left[0]
+    tm[pl.ds(32, FZ, stride=2), :] = new_r
+    tm[pl.ds(33, FZ, stride=2), :] = new_l
+    columns = tm[...].T[:FP]
+    low, high = lo1[8:16, :], hi1[8:16, :]
+    first, last = fluid2[:, 0, :], fluid2[:, FP - 1, :]
+    new_low = halo_row(
+        low, lo1[0:8, :], first, turn(left[0], 32), turn(right[0], 31),
+        lo[16:24, :], lo[24:32, :], lo[32:33, :], wall_lo,
+    )
+    new_high = halo_row(
+        high, last, hi1[0:8, :], turn(left[0], 31), turn(right[0], 30),
+        hi[16:24, :], hi[24:32, :], hi[32:33, :], wall_hi,
+    )
+    named = jnp.broadcast_to(owner[...], (FP, FS))
+    advance(fluid2, fluid3, low, high, columns, 0, sv, pv, film[...], pick(named, wall2))
+    advance(fluid3, fluid_out, new_low, new_high, columns, 32, sv, pv, film[...], pick(named, wall3))
+
+    thin = lanes(SD)
+    keep = jnp.where(thin >= 64, keep_l, keep_r)
+    own, halo, c_halo = metal[0:SD, :], metal[SD : 2 * SD, :], metal[2 * SD : 3 * SD, :]
+    own, halo = add_inflow(own, halo, inflow1, me, keep)
+    own, halo = metal_step(own, halo, cond[...], c_halo, keep)
+    own, halo = add_inflow(own, halo, inflow2, me, keep)
+    own, halo = metal_step(own, halo, cond[...], c_halo, keep)
+    own, _ = add_inflow(own, halo, inflow3, me, keep)
+    solid_out[...] = own
+
+
+def shape(*dims):
+    return jax.ShapeDtypeStruct(dims, F32)
+
+
+VMEM = pl.BlockSpec(memory_space=pltpu.VMEM)
+
+
+def call(kernel, outs, args, name, scratch=()):
+    return pl.pallas_call(
+        kernel,
+        out_shape=outs,
+        in_specs=[VMEM] * len(args),
+        out_specs=jax.tree.map(lambda _: VMEM, outs),
+        scratch_shapes=scratch,
+        name=name,
+        compiler_params=pltpu.CompilerParams(vmem_limit_bytes=32 * 1024 * 1024),
+    )(*args)
+
+
+def both_ways(up, down):
+    count = lax.axis_size("sec")
+    forward = [(i, (i + 1) % count) for i in range(count)]
+    backward = [(target, source) for source, target in forward]
+    return lax.ppermute(up, "sec", forward), lax.ppermute(down, "sec", backward)
+
+
+def swap(message):
+    return lax.all_to_all(message, "blk", split_axis=0, concat_axis=0, tiled=True)
+
+
+def two_exchanges(fluid, sv, pv, film, solid, cond, face_owner):
+    owner = face_owner.reshape(FP, 1)
+    solid, cond = solid.reshape(SD, FS), cond.reshape(SD, FS)
+
+    def rows(outer, inner):
+        name = jnp.broadcast_to(owner[outer : outer + 1].astype(F32), (1, FS))
+        return jnp.concatenate(
+            [
+                fluid[:, inner],
+                fluid[:, outer],
+                sv[:, outer],
+                pv[:, outer],
+                film[outer : outer + 1],
+                solid[0:1],
+                name,
+                jnp.zeros((5, FS), F32),
+            ],
+            axis=0,
+        )
+
+    lo, hi = both_ways(rows(FP - 1, FP - 2), rows(0, 1))
+    mt, sums = call(
+        first_kernel,
+        (shape(FS, FS), shape(16, FS)),
+        (fluid, sv, pv, film, solid, cond, owner),
+        "columns",
+    )
+    recv = swap(call(pack_kernel, shape(NB, R0, FS), (mt, sums, solid, cond, lo, hi), "pack"))
+    work = [pltpu.VMEM((FS, FS), F32), pltpu.VMEM((FZ, FP, FS), F32)]
+    fluid2, up, down, metal = call(
+        second_kernel,
+        (shape(FZ, FP, FS), shape(32, FS), shape(32, FS), shape(3 * SD, FS)),
+        (recv, mt, fluid, sv, pv, film, solid, cond, owner, lo, hi),
+        "steps",
+        work,
+    )
+    lo1, hi1 = both_ways(up, down)
+    mt1, sums1 = call(
+        sums_kernel,
+        (shape(FS + 8, FS), shape(24, FS)),
+        (recv, fluid2, sv, pv, film, owner),
+        "sums",
+    )
+    recv1 = swap(
+        call(send_kernel, shape(NB, R1, FS), (recv, mt1, sums1, up, metal, lo1, hi1), "pack")
+    )
+    fluid, solid = call(
+        last_kernel,
+        (shape(FZ, FP, FS), shape(SD, FS)),
+        (recv1, recv, mt1, fluid2, sv, pv, film, cond, owner, lo, hi, lo1, hi1, metal),
+        "steps",
+        work,
+    )
+    return fluid, solid.reshape(1, SD, FS)
 
 
 def padded(block, sides, width, periodic):
@@ -130,8 +676,14 @@
         P("sec", None, "blk"),
         P("sec", "blk", None, None),
     )
+    sizes = dict(mesh.shape)
+
+    def chosen(*args):
+        fits = args[0].shape == (FZ, FP, FS) and args[4].shape == (1, SD, FS)
+        return two_exchanges(*args) if fits and sizes["blk"] == NB else local(*args)
+
     return jax.shard_map(
-        local,
+        chosen,
         mesh=mesh,
         in_specs=placed,
         out_specs=(P(None, "sec", "blk"), P("sec", None, "blk")),

time: 157 us -> 44.8 us (0.29)
  blocking collectives: 83.3 us -> 25 us
  starting transfers between devices: 37.7 us -> 3.07 us
  waiting for transfers between devices: 20.5 us -> 2.42 us
  other arithmetic: 5.14 us -> 0 us
  local copies, waits for them, and re-layouts: 3.96 us -> 8.1 us
  matrix products: 3.96 us -> 0 us
  Pallas kernels: 0 us -> 3.45 us
    all_gather x4 -> x0, blocking collectives: 83.3 us -> none  [local(): lax.all_gather(wall_row, 'blk', axis=0, tiled=True)]
    all_to_all x0 -> x2, blocking collectives: none -> 25 us  [swap(): lax.all_to_all(message, 'blk', split_axis=0, concat_axis=0, tiled=True)]
    ppermute x16 -> x4, starting transfers between devices: 24.4 us -> 3.07 us  [the longest x2 2.07 us: both_ways(): lax.ppermute(down, 'sec', backward)]
    all_to_all x4 -> x0, waiting for transfers between devices: 20.4 us -> none  [local(): lax.all_to_all(outgoing, 'blk', split_axis=0, concat_axis=0, tiled=True)]
    all_to_all x4 -> x0, starting transfers between devices: 13.4 us -> none  [local(): lax.all_to_all(outgoing, 'blk', split_axis=0, concat_axis=0, tiled=True)]
    dot_general x8 -> x0, matrix products: 3.96 us -> none  [the longest x4 3.11 us: local(): jnp.einsum('ocb,bf->ocf', placing, flux, precision=lax.Precision.HIGHEST)]
    pallas_call x0 -> x6, Pallas kernels: none -> 3.45 us  [call(): pl.pallas_call(kernel, out_shape=outs, in_specs=[VMEM] * len(args), out_s...]
    slice x35 -> x6, local copies, waits for them, and re-layouts: 0.98 us -> 4.42 us  [the longest x1 0.88 us: rows(): fluid[:, outer]]
  transfers between devices with their start and end apart: 20 -> 4, of which waited for: 4 -> 2; matrix products, arithmetic and copies ran while one was open for 2% -> 0% of each run, Pallas kernels for 0% -> 2%
where the time goes in v1:
time: 44.8 us; the launch traced here: 44.1 us
  blocking collectives  25 us (56%)
  local copies, waits for them, and re-layouts  8.1 us (18%)
  Pallas kernels  3.45 us (8%)
  starting transfers between devices  3.07 us (7%)
  waiting for transfers between devices  2.42 us (5%)
  between operations  2.05 us (5%)
    all_to_all x2, blocking collectives, swap(): lax.all_to_all(message, 'blk', split_axis=0, concat_axis=0, tiled=True)  25 us
    unnamed x20, local copies, waits for them, and re-layouts  3.51 us
    pallas_call x6, Pallas kernels, call(): pl.pallas_call(kernel, out_shape=outs, in_specs=[VMEM] * len(args), out_s...  3.45 us
    ppermute x2, starting transfers between devices, both_ways(): lax.ppermute(down, 'sec', backward)  2.07 us
    ppermute x2, waiting for transfers between devices, both_ways(): lax.ppermute(up, 'sec', forward)  1.78 us
    ppermute x2, starting transfers between devices, both_ways(): lax.ppermute(up, 'sec', forward)  1 us
  transfers between devices with their start and end apart: 4, of which 2 were waited for; matrix products, arithmetic and copies ran while one was open for 0% of the time, Pallas kernels for 2%

profile of v1, /device:TPU:0, one launch (start us, length us, event | category | flops | bytes accessed | tf_op | source)
XLA Modules:
  0.0 44.1 jit_solution(2306826368158794874)
XLA Ops:
  0.6 0.0 copy-start.9
  0.6 0.7 %slice_bitcast_fusion = f32[1,128]{1,0:T(1,128)S(1)} fusion(f32[1,32,128]{2,1,0:T(8,128)} %param.11), kind=kLoop, calls=%fused_computation | loop fusion | bytes 1024 | tf_op jit(solution)/shard_map/slice | solution.py:520
  1.3 0.0 copy-done.9
  1.3 0.6 %fusion.4 = (s32[1,1,1,1]{2,3,1,0:T(1,128)}, s32[1,1,1,1]{2,3,1,0:T(1,128)}) fusion(s32[1,1,64,1]{2,3,1,0:T(1,128)S(1)} %copy-done.9), kind=kLoop, calls=%fused_computation.5 | loop fusion | bytes 16 | tf_op jit(solution)/shard_map/slice | solution.py:512
  2.6 0.7 %fusion.3 = (f32[1,128]{1,0:T(1,128)S(1)}, f32[1,128]{1,0:T(1,128)S(1)}) fusion(f32[64,128]{1,0:T(8,128)} %film.7), kind=kLoop, calls=%fused_computation.4 | loop fusion | bytes 2048 | tf_op jit(solution)/shard_map/slice | solution.py:519
  3.3 0.8 %fusion.1 = (f32[8,1,128]{2,1,0:T(1,128)S(1)}, f32[8,1,128]{2,1,0:T(1,128)S(1)}) fusion(f32[8,64,128]{2,1,0:T(8,128)} %sv.7), kind=kLoop, calls=%fused_computation.2 | loop fusion | bytes 16384 | tf_op jit(solution)/shard_map/slice | solution.py:517
  4.1 0.8 %fusion = (f32[8,1,128]{2,1,0:T(1,128)S(1)}, f32[8,1,128]{2,1,0:T(1,128)S(1)}) fusion(f32[8,64,128]{2,1,0:T(8,128)} %pv.7), kind=kLoop, calls=%fused_computation.1 | loop fusion | bytes 16384 | tf_op jit(solution)/shard_map/slice | solution.py:518
  4.8 0.9 %fusion.2 = (f32[8,1,128]{2,1,0:T(1,128)S(1)}, f32[8,1,128]{2,1,0:T(1,128)S(1)}, f32[8,1,128]{2,1,0:T(1,128)S(1)}, f32[8,1,128]{2,1,0:T(1,128)S(1)}) fusion(f32[8,64,128]{2,1,0:T(8,128)} %fluid.3), kind=kLoop, calls=%fused_computation.3 | loop fusion | bytes 32768 | tf_op jit(solution)/shard_map/slice | solution.py:516
  5.8 0.5 %collective-permute-start = (f32[40,128]{1,0:T(8,128)S(1)}, f32[40,128]{1,0:T(8,128)S(1)}, u32[]{:S(2)}, u32[]{:S(2)}) collective-permute-start(f32[40,128]{1,0:T(8,128)S(1)} %concatenate.6), channel_id=1, source_target_pairs={{0,8},{8,16},{16,24},{24,0},{1,9},{9,17},{17,25},{25,1},{2,10},{10... | collective-permute-start | bytes 61448 | tf_op jit(solution)/shard_map/ppermute | solution.py:500
  6.9 0.0 copy-start.6
  7.0 2.0 %collective-permute-start.1 = (f32[40,128]{1,0:T(8,128)S(1)}, f32[40,128]{1,0:T(8,128)S(1)}, u32[]{:S(2)}, u32[]{:S(2)}) collective-permute-start(f32[40,128]{1,0:T(8,128)S(1)} %concatenate.7), channel_id=1, source_target_pairs={{8,0},{16,8},{24,16},{0,24},{9,1},{17,9},{25,17},{1,25},{10,2},{18... | collective-permute-start | bytes 61448 | tf_op jit(solution)/shard_map/ppermute | solution.py:500
  9.0 0.0 copy-start.7
  9.0 0.0 copy-start.8
  9.0 0.1 copy.9.owner
  9.1 0.0 copy-done.6
  9.1 0.6 %copy-done.7 = f32[1,32,128]{2,1,0:T(8,128)S(1)} copy-done((f32[1,32,128]{2,1,0:T(8,128)S(1)}, f32[1,32,128]{2,1,0:T(8,128)}, u32[]{:S(2)}) %copy-start.7) | copy-done | bytes 16408
  9.7 0.0 copy-done.8
  9.7 0.0 copy-start
  9.7 0.9 %copy-done = f32[8,64,128]{2,1,0:T(8,128)S(1)} copy-done((f32[8,64,128]{2,1,0:T(8,128)S(1)}, f32[8,64,128]{2,1,0:T(8,128)}, u32[]{:S(2)}) %copy-start) | copy-done | bytes 262168
  10.7 0.0 copy-start.2
  10.7 0.9 %copy-done.2 = f32[8,64,128]{2,1,0:T(8,128)S(1)} copy-done((f32[8,64,128]{2,1,0:T(8,128)S(1)}, f32[8,64,128]{2,1,0:T(8,128)}, u32[]{:S(2)}) %copy-start.2) | copy-done | bytes 262168
  11.6 0.0 copy-start.4
  11.6 0.9 %copy-done.4 = f32[8,64,128]{2,1,0:T(8,128)S(1)} copy-done((f32[8,64,128]{2,1,0:T(8,128)S(1)}, f32[8,64,128]{2,1,0:T(8,128)}, u32[]{:S(2)}) %copy-start.4) | copy-done | bytes 262168
  12.6 0.4 columns.1
  13.0 0.0 collective-permute-done.lo
  13.0 0.0 collective-permute-done.1.hi
  13.0 0.0 copy-start.5
  13.0 0.1 pack.2
  13.1 0.0 copy-start.1
  13.1 14.5 %all_to_all.10.recv = f32[8,48,128]{2,1,0:T(8,128)S(1)} all-to-all(f32[8,48,128]{2,1,0:T(8,128)S(1)} %pack.2), channel_id=1, replica_groups=mesh['sec'=4,'blk'=8] {'blk'}, dimensions={0} | all-to-all | bytes 393216 | tf_op jit(solution)/shard_map/all_to_all | solution.py:504
  27.6 0.0 copy-done.5
  27.6 0.0 copy-done.1
  27.6 0.0 copy-start.3
  27.7 1.0 %steps.2 = (f32[8,64,128]{2,1,0:T(8,128)S(1)}, f32[32,128]{1,0:T(8,128)S(1)}, f32[32,128]{1,0:T(8,128)S(1)}, f32[96,128]{1,0:T(8,128)S(1)}) custom-call(f32[8,48,128]{2,1,0:T(8,128)S(1)} %all_to_all.10.recv, f32[128,128]{1,0:T(8,128)S(1)} %get-tuple-element.12.mt, f32[8,64,128]{2,1,0:T(8,128)S(1)} %copy-done.5, f32[8,64,128]{2,1,0:T(8,128)S(1)} %copy-done.1, ...), custom_call_target="tpu_custom_call" | custom-call | tf_op jit(solution)/shard_map/steps/pallas_call | solution.py:485
  28.6 0.1 collective-permute-start.3
  28.7 0.5 %collective-permute-start.2 = (f32[32,128]{1,0:T(8,128)S(1)}, f32[32,128]{1,0:T(8,128)S(1)}, u32[]{:S(2)}, u32[]{:S(2)}) collective-permute-start(f32[32,128]{1,0:T(8,128)S(1)} %get-tuple-element.17.up), channel_id=1, source_target_pairs={{0,8},{8,16},{16,24},{24,0},{1,9},{9,17},{17,25},{25,1},{2,10},{10... | collective-permute-start | bytes 49160 | tf_op jit(solution)/shard_map/ppermute | solution.py:500
  29.2 0.0 copy-done.3
  29.2 0.3 sums.1
  29.5 0.6 %collective-permute-done.3.hi.hi1 = f32[32,128]{1,0:T(8,128)S(1)} collective-permute-done((f32[32,128]{1,0:T(8,128)S(1)}, f32[32,128]{1,0:T(8,128)S(1)}, u32[]{:S(2)}, u32[]{:S(2)}) %collective-permute-start.3) | collective-permute-done | bytes 16416 | tf_op jit(solution)/shard_map/ppermute | solution.py:500
  30.1 1.8 %collective-permute-done.2.lo.lo1 = f32[32,128]{1,0:T(8,128)S(1)} collective-permute-done((f32[32,128]{1,0:T(8,128)S(1)}, f32[32,128]{1,0:T(8,128)S(1)}, u32[]{:S(2)}, u32[]{:S(2)}) %collective-permute-start.2) | collective-permute-done | bytes 16416 | tf_op jit(solution)/shard_map/ppermute | solution.py:500
  31.9 0.1 pack.3
  32.0 10.5 %all_to_all.11.recv1 = f32[8,40,128]{2,1,0:T(8,128)S(1)} all-to-all(f32[8,40,128]{2,1,0:T(8,128)S(1)} %pack.3), channel_id=1, replica_groups=mesh['sec'=4,'blk'=8] {'blk'}, dimensions={0} | all-to-all | bytes 327680 | tf_op jit(solution)/shard_map/all_to_all | solution.py:504
  42.5 1.6 %steps.3 = (f32[8,64,128]{2,1,0:T(8,128)}, f32[32,128]{1,0:T(8,128)}) custom-call(f32[8,40,128]{2,1,0:T(8,128)S(1)} %all_to_all.11.recv1, f32[8,48,128]{2,1,0:T(8,128)S(1)} %all_to_all.10.recv, f32[136,128]{1,0:T(8,128)S(1)} %get-tuple-element.15.mt, f32[8,64,128]{2,1,0:T(8,128)S(1)} %get-tuple-element.14.fluid2, f32[8,64,128]{2,1,0:T(8,128)S(1)} %copy-done.1, ...), custom_call_target="tpu_custom_call" | custom-call | tf_op jit(solution)/shard_map/steps/pallas_call | solution.py:485
  (5 shorter events, 0.1 us)
Async XLA Ops:
  0.6 0.7 %copy-start.9 = (s32[1,1,64,1]{2,3,1,0:T(1,128)S(1)}, s32[1,1,64,1]{2,3,1,0:T(1,128)}, u32[]{:S(2)}) copy-start(s32[1,1,64,1]{2,3,1,0:T(1,128)} %param.13) | copy-start | bytes 772
  5.8 7.2 %collective-permute-start = (f32[40,128]{1,0:T(8,128)S(1)}, f32[40,128]{1,0:T(8,128)S(1)}, u32[]{:S(2)}, u32[]{:S(2)}) collective-permute-start(f32[40,128]{1,0:T(8,128)S(1)} %concatenate.6), channel_id=1, source_target_pairs={{0,8},{8,16},{16,24},{24,0},{1,9},{9,17},{17,25},{25,1},{2,10},{10... | collective-permute-start | bytes 61448 | tf_op jit(solution)/shard_map/ppermute | solution.py:500
  6.9 2.2 %copy-start.6 = (f32[64,128]{1,0:T(8,128)S(1)}, f32[64,128]{1,0:T(8,128)}, u32[]{:S(2)}) copy-start(f32[64,128]{1,0:T(8,128)} %film.7) | copy-start | bytes 98308
  7.0 6.0 %collective-permute-start.1 = (f32[40,128]{1,0:T(8,128)S(1)}, f32[40,128]{1,0:T(8,128)S(1)}, u32[]{:S(2)}, u32[]{:S(2)}) collective-permute-start(f32[40,128]{1,0:T(8,128)S(1)} %concatenate.7), channel_id=1, source_target_pairs={{8,0},{16,8},{24,16},{0,24},{9,1},{17,9},{25,17},{1,25},{10,2},{18... | collective-permute-start | bytes 61448 | tf_op jit(solution)/shard_map/ppermute | solution.py:500
  9.0 0.7 %copy-start.7 = (f32[1,32,128]{2,1,0:T(8,128)S(1)}, f32[1,32,128]{2,1,0:T(8,128)}, u32[]{:S(2)}) copy-start(f32[1,32,128]{2,1,0:T(8,128)} %param.12) | copy-start | bytes 49156
  9.0 0.7 %copy-start.8 = (f32[1,32,128]{2,1,0:T(8,128)S(1)}, f32[1,32,128]{2,1,0:T(8,128)}, u32[]{:S(2)}) copy-start(f32[1,32,128]{2,1,0:T(8,128)} %param.11) | copy-start | bytes 49156
  9.7 0.9 %copy-start = (f32[8,64,128]{2,1,0:T(8,128)S(1)}, f32[8,64,128]{2,1,0:T(8,128)}, u32[]{:S(2)}) copy-start(f32[8,64,128]{2,1,0:T(8,128)} %sv.7) | copy-start | bytes 786436
  10.7 0.9 %copy-start.2 = (f32[8,64,128]{2,1,0:T(8,128)S(1)}, f32[8,64,128]{2,1,0:T(8,128)}, u32[]{:S(2)}) copy-start(f32[8,64,128]{2,1,0:T(8,128)} %pv.7) | copy-start | bytes 786436
  11.6 0.9 %copy-start.4 = (f32[8,64,128]{2,1,0:T(8,128)S(1)}, f32[8,64,128]{2,1,0:T(8,128)}, u32[]{:S(2)}) copy-start(f32[8,64,128]{2,1,0:T(8,128)} %fluid.3) | copy-start | bytes 786436
  13.0 14.7 %copy-start.5 = (f32[8,64,128]{2,1,0:T(8,128)S(1)}, f32[8,64,128]{2,1,0:T(8,128)}, u32[]{:S(2)}) copy-start(f32[8,64,128]{2,1,0:T(8,128)} %fluid.3) | copy-start | bytes 786436
  13.1 14.6 %copy-start.1 = (f32[8,64,128]{2,1,0:T(8,128)S(1)}, f32[8,64,128]{2,1,0:T(8,128)}, u32[]{:S(2)}) copy-start(f32[8,64,128]{2,1,0:T(8,128)} %sv.7) | copy-start | bytes 786436
  27.6 1.5 %copy-start.3 = (f32[8,64,128]{2,1,0:T(8,128)S(1)}, f32[8,64,128]{2,1,0:T(8,128)}, u32[]{:S(2)}) copy-start(f32[8,64,128]{2,1,0:T(8,128)} %pv.7) | copy-start | bytes 786436
  28.6 1.5 %collective-permute-start.3 = (f32[32,128]{1,0:T(8,128)S(1)}, f32[32,128]{1,0:T(8,128)S(1)}, u32[]{:S(2)}, u32[]{:S(2)}) collective-permute-start(f32[32,128]{1,0:T(8,128)S(1)} %get-tuple-element.19), channel_id=1, source_target_pairs={{8,0},{16,8},{24,16},{0,24},{9,1},{17,9},{25,17},{1,25},{10,2},{18... | collective-permute-start | bytes 49160 | tf_op jit(solution)/shard_map/ppermute | solution.py:500
  28.7 3.2 %collective-permute-start.2 = (f32[32,128]{1,0:T(8,128)S(1)}, f32[32,128]{1,0:T(8,128)S(1)}, u32[]{:S(2)}, u32[]{:S(2)}) collective-permute-start(f32[32,128]{1,0:T(8,128)S(1)} %get-tuple-element.17.up), channel_id=1, source_target_pairs={{0,8},{8,16},{16,24},{24,0},{1,9},{9,17},{17,25},{25,1},{2,10},{10... | collective-permute-start | bytes 49160 | tf_op jit(solution)/shard_map/ppermute | solution.py:500

commit v2 on v1

--- a/solution.py
+++ b/solution.py
@@ -195,19 +195,63 @@
     return acc
 
 
-def first_kernel(fluid, sv, pv, film, solid, cond, owner, mt, sums):
+def fetch(copies, sems):
+    started = [
+        pltpu.make_async_copy(src, dst, sems.at[i]) for i, (src, dst) in enumerate(copies)
+    ]
+    for copy in started:
+        copy.start()
+    return started
+
+
+def rows_kernel(fluid, sv, pv, film, solid, owner, first, second, tiles, flat, ids, sems):
+    starts = (FP - 8, 0)
+    copies = []
+    for side, start in enumerate(starts):
+        for i, ref in enumerate((fluid, sv, pv)):
+            copies.append((ref.at[:, pl.ds(start, 8), :], tiles.at[3 * side + i]))
+        copies.append((film.at[pl.ds(start, 8), :], flat.at[side]))
+    copies += [(solid.at[pl.ds(0, 8), :], flat.at[2]), (owner, ids)]
+    for copy in fetch(copies, sems):
+        copy.wait()
+    even = lax.axis_index("sec") % 2 == 0
+    wall = flat[2, 0:1, :]
+
+    def rows(side, outer, inner, row):
+        name = jnp.broadcast_to(ids[:, row : row + 1].astype(F32), (1, FS))
+        blank = jnp.zeros((5, FS), F32)
+        return (
+            tiles[3 * side, :, inner, :],
+            tiles[3 * side, :, outer, :],
+            tiles[3 * side + 1, :, outer, :],
+            tiles[3 * side + 2, :, outer, :],
+            jnp.concatenate([flat[side, outer : outer + 1, :], wall, name, blank], axis=0),
+        )
+
+    for i, (up, down) in enumerate(zip(rows(0, 7, 6, FP - 1), rows(1, 0, 1, 0))):
+        first[8 * i : 8 * i + 8, :] = jnp.where(even, up, down)
+        second[8 * i : 8 * i + 8, :] = jnp.where(even, down, up)
+
+
+def first_kernel(
+    fluid_in, sv_in, pv_in, film_in, solid_in, cond_in, owner,
+    mt, sums, fluid, sv, pv, film, solid, cond, names, ids, sems,
+):
+    half = FZ // 2
+    copies = [(owner, ids), (film_in, film), (solid_in, solid), (cond_in, cond)]
+    for src, dst in ((fluid_in, fluid), (pv_in, pv), (sv_in, sv)):
+        for part in range(2):
+            copies.append((src.at[pl.ds(half * part, half)], dst.at[pl.ds(half * part, half)]))
+    started = fetch(copies, sems)
     lane = lanes(FP)
-    named = jnp.broadcast_to(owner[...], (FP, FS))
-    top = gather_columns(fluid, lane)
+    for copy in started[:4]:
+        copy.wait()
+    ids_row = jnp.concatenate([ids[...].astype(F32), jnp.zeros((1, FS - FP), F32)], axis=1)
+    named = jnp.broadcast_to(ids_row, (FS, FS)).T[:FP]
+    names[...] = named
     bottom = jnp.zeros((FP, FS), F32)
     pair = (lane - 32) // 2
-    for z in range(FZ):
-        here = (pair == z) & (lane >= 32)
-        top = jnp.where(here, turn(pv[z], 33 + 2 * z), top)
-        bottom = jnp.where(here, turn(sv[z], 33 + 2 * z), bottom)
-    top = jnp.where(lane // 2 == 24, turn(film[...], 49), top)
-    top = jnp.where(lane == 50, named.astype(F32), top)
-    metal = bottom[:SD]
+    metal = jnp.zeros((SD, FS), F32)
     thin = lanes(SD)
     s, c = solid[...], cond[...]
     for k in range(4):
@@ -215,12 +259,31 @@
         metal = jnp.where(thin == 4 * k + 2, turn(s, 3 * k + 2), metal)
         metal = jnp.where(thin == 4 * k + 17, turn(c, 3 * k + 21), metal)
         metal = jnp.where(thin == 4 * k + 18, turn(c, 3 * k + 18), metal)
+    started[4].wait()
+    sums[0:8, :], sums[8:16, :] = by_owner(named, [film[...] * fluid[0], film[...]])
+    started[5].wait()
+    top = gather_columns(fluid, lane)
+    for copy in started[6:]:
+        copy.wait()
+    for z in range(FZ):
+        here = (pair == z) & (lane >= 32)
+        top = jnp.where(here, turn(pv[z], 33 + 2 * z), top)
+        bottom = jnp.where(here, turn(sv[z], 33 + 2 * z), bottom)
+    top = jnp.where(lane // 2 == 24, turn(film[...], 49), top)
+    top = jnp.where(lane == 50, named, top)
+    metal = jnp.where(thin < 32, metal, bottom[:SD])
     whole = jnp.concatenate([top, metal, bottom[SD:]], axis=0)
     mt[...] = whole.T
-    sums[0:8, :], sums[8:16, :] = by_owner(named, [film[...] * fluid[0], film[...]])
-
-
-def pack_kernel(mt, sums, solid, cond, lo, hi, out):
+
+
+def sort_rows(first, second, lo, hi):
+    even = lax.axis_index("sec") % 2 == 0
+    lo[...] = jnp.where(even, second[...], first[...])
+    hi[...] = jnp.where(even, first[...], second[...])
+
+
+def pack_kernel(mt, sums, solid, cond, first, second, out, lo, hi):
+    sort_rows(first, second, lo, hi)
     me = lax.axis_index("blk")
     lane, sub = lanes(FZ), subs(FZ)
     (r0, r1), (l0, l1) = column_blocks(mt)
@@ -265,7 +328,8 @@
 
 
 def second_kernel(
-    recv, mt, fluid, sv, pv, film, solid, cond, owner, lo, hi, fluid2, up, down, metal, tm, fluid1
+    recv, mt, fluid, sv, pv, film, solid, cond, owner, lo, hi,
+    fluid2, first_out, second_out, metal, tm, fluid1,
 ):
     me = lax.axis_index("blk")
     left, right, keep_l, keep_r = neighbours(recv, me, 3)
@@ -280,7 +344,6 @@
     wall1 = strip_row(wall0, conduct_of(c0, wall0), under0, conduct_of(c1, under0))
     wall1 = wall1 + SOLID_STEP * inflow0
 
-    own_cols, _ = None, None
     mine_right, mine_left = mt[pl.ds(1, FZ, stride=4), :], mt[pl.ds(2, FZ, stride=4), :]
     new_l = halo_column(
         left[0], left[0], left[1], mine_left, sv_l, pv_l, film_l,
@@ -317,7 +380,7 @@
         high, last, hi[0:8, :], turn(left[0], 31), turn(right[0], 30),
         hi[16:24, :], hi[24:32, :], hi[32:33, :], wall_hi,
     )
-    named = jnp.broadcast_to(owner[...], (FP, FS))
+    named = owner[...]
     walls0, walls1 = pick(named, wall0), pick(named, wall1)
     advance(fluid, fluid1, low, high, columns, 0, sv, pv, film[...], walls0)
     advance(fluid1, fluid2, new_low, new_high, columns, 32, sv, pv, film[...], walls1)
@@ -329,9 +392,12 @@
     metal[0:SD, :] = own
     metal[SD : 2 * SD, :] = halo
     metal[2 * SD : 3 * SD, :] = c_halo
-    up[0:8, :], up[8:16, :] = fluid2[:, FP - 2, :], fluid2[:, FP - 1, :]
-    down[0:8, :], down[8:16, :] = fluid2[:, 1, :], fluid2[:, 0, :]
-    for ref in (up, down):
+    even = lax.axis_index("sec") % 2 == 0
+    for i, (inner, outer) in enumerate(((FP - 2, 1), (FP - 1, 0))):
+        up, down = fluid2[:, inner, :], fluid2[:, outer, :]
+        first_out[8 * i : 8 * i + 8, :] = jnp.where(even, up, down)
+        second_out[8 * i : 8 * i + 8, :] = jnp.where(even, down, up)
+    for ref in (first_out, second_out):
         ref[16:24, :] = flux
         ref[24:32, :] = own[0:8]
 
@@ -342,7 +408,7 @@
     _, _, film_l, own_l = edge_terms(left)
     sv_r, _, film_r, own_r = edge_terms(right)
     lane, sub = lanes(FP), subs(FP)
-    named = jnp.broadcast_to(owner[...], (FP, FS))
+    named = owner[...]
     x, f = fluid2[0], film[...]
     low = jnp.where(sub == 0, 0.0, turn(x, 1, 0))
     high = jnp.where(sub == FP - 1, 0.0, turn(x, -1, 0))
@@ -367,13 +433,14 @@
     up = top * (SPREAD + ADVECT * jnp.maximum(pv[0, 0:1, :], 0.0))
     down = end * (SPREAD + ADVECT * jnp.maximum(-pv[0, FP - 1 : FP, :], 0.0))
     mt[FS : FS + 8, :] = jnp.concatenate(
-        [up, down, named[0:1].astype(F32), named[FP - 1 : FP].astype(F32), jnp.zeros((4, FS), F32)],
+        [up, down, named[0:1], named[FP - 1 : FP], jnp.zeros((4, FS), F32)],
         axis=0,
     )
     sums[0:8, :], sums[8:16, :], sums[16:24, :] = a2, b3, h2
 
 
-def send_kernel(recv, mt, sums, up, metal, lo, hi, out):
+def send_kernel(recv, mt, sums, mine, metal, first, second, out, lo, hi):
+    sort_rows(first, second, lo, hi)
     me = lax.axis_index("blk")
     sub = subs(NB)
     rows = sub.astype(F32)
@@ -400,7 +467,7 @@
             ],
             axis=0,
         )
-        out[peer, 8:16, :] = up[16:24, :]
+        out[peer, 8:16, :] = mine[16:24, :]
         out[peer, 16:24, :] = sums[0:8, :]
         ahead = (me + 1 == peer).astype(F32)
         behind = (me - 1 == peer).astype(F32)
@@ -459,7 +526,7 @@
         high, last, hi1[0:8, :], turn(left[0], 31), turn(right[0], 30),
         hi[16:24, :], hi[24:32, :], hi[32:33, :], wall_hi,
     )
-    named = jnp.broadcast_to(owner[...], (FP, FS))
+    named = owner[...]
     advance(fluid2, fluid3, low, high, columns, 0, sv, pv, film[...], pick(named, wall2))
     advance(fluid3, fluid_out, new_low, new_high, columns, 32, sv, pv, film[...], pick(named, wall3))
 
@@ -479,25 +546,28 @@
 
 
 VMEM = pl.BlockSpec(memory_space=pltpu.VMEM)
-
-
-def call(kernel, outs, args, name, scratch=()):
+GRANT = 54 * 1024 * 1024
+HBM = pl.BlockSpec(memory_space=pltpu.HBM)
+
+
+def call(kernel, outs, args, name, scratch=(), far=0, limit=32 * 1024 * 1024):
     return pl.pallas_call(
         kernel,
         out_shape=outs,
-        in_specs=[VMEM] * len(args),
+        in_specs=[HBM] * far + [VMEM] * (len(args) - far),
         out_specs=jax.tree.map(lambda _: VMEM, outs),
         scratch_shapes=scratch,
         name=name,
-        compiler_params=pltpu.CompilerParams(vmem_limit_bytes=32 * 1024 * 1024),
+        compiler_params=pltpu.CompilerParams(vmem_limit_bytes=limit),
     )(*args)
 
 
-def both_ways(up, down):
+def both_ways(first, second):
     count = lax.axis_size("sec")
-    forward = [(i, (i + 1) % count) for i in range(count)]
-    backward = [(target, source) for source, target in forward]
-    return lax.ppermute(up, "sec", forward), lax.ppermute(down, "sec", backward)
+    near = [(i, i ^ 1) for i in range(count)]
+    far = [(i, (i + 1 if i % 2 else i - 1) % count) for i in range(count)]
+    second = lax.ppermute(second, "sec", far)
+    return lax.ppermute(first, "sec", near), second
 
 
 def swap(message):
@@ -505,54 +575,70 @@
 
 
 def two_exchanges(fluid, sv, pv, film, solid, cond, face_owner):
-    owner = face_owner.reshape(FP, 1)
+    owner = face_owner.reshape(1, FP)
     solid, cond = solid.reshape(SD, FS), cond.reshape(SD, FS)
 
-    def rows(outer, inner):
-        name = jnp.broadcast_to(owner[outer : outer + 1].astype(F32), (1, FS))
-        return jnp.concatenate(
+    field = shape(FZ, FP, FS)
+    first, second = both_ways(
+        *call(
+            rows_kernel,
+            (shape(40, FS), shape(40, FS)),
+            (fluid, sv, pv, film, solid, owner),
+            "rows",
             [
-                fluid[:, inner],
-                fluid[:, outer],
-                sv[:, outer],
-                pv[:, outer],
-                film[outer : outer + 1],
-                solid[0:1],
-                name,
-                jnp.zeros((5, FS), F32),
+                pltpu.VMEM((6, FZ, 8, FS), F32),
+                pltpu.VMEM((3, 8, FS), F32),
+                pltpu.VMEM((1, FP), jnp.int32),
+                pltpu.SemaphoreType.DMA((10,)),
             ],
-            axis=0,
+            far=6,
+            limit=GRANT - 56 * 1024,
         )
-
-    lo, hi = both_ways(rows(FP - 1, FP - 2), rows(0, 1))
-    mt, sums = call(
+    )
+    mt, sums, fluid, sv, pv, film, solid, cond, owner = call(
         first_kernel,
-        (shape(FS, FS), shape(16, FS)),
+        (
+            shape(FS, FS), shape(16, FS), field, field, field,
+            shape(FP, FS), shape(SD, FS), shape(SD, FS), shape(FP, FS),
+        ),
         (fluid, sv, pv, film, solid, cond, owner),
         "columns",
-    )
-    recv = swap(call(pack_kernel, shape(NB, R0, FS), (mt, sums, solid, cond, lo, hi), "pack"))
+        [pltpu.VMEM((1, FP), jnp.int32), pltpu.SemaphoreType.DMA((10,))],
+        far=7,
+        limit=GRANT - 1104 * 1024,
+    )
+    message, lo, hi = call(
+        pack_kernel,
+        (shape(NB, R0, FS), shape(40, FS), shape(40, FS)),
+        (mt, sums, solid, cond, first, second),
+        "pack",
+    )
+    recv = swap(message)
     work = [pltpu.VMEM((FS, FS), F32), pltpu.VMEM((FZ, FP, FS), F32)]
-    fluid2, up, down, metal = call(
+    fluid2, first, second, metal = call(
         second_kernel,
-        (shape(FZ, FP, FS), shape(32, FS), shape(32, FS), shape(3 * SD, FS)),
+        (field, shape(32, FS), shape(32, FS), shape(3 * SD, FS)),
         (recv, mt, fluid, sv, pv, film, solid, cond, owner, lo, hi),
         "steps",
         work,
     )
-    lo1, hi1 = both_ways(up, down)
+    first1, second1 = both_ways(first, second)
     mt1, sums1 = call(
         sums_kernel,
         (shape(FS + 8, FS), shape(24, FS)),
         (recv, fluid2, sv, pv, film, owner),
         "sums",
     )
-    recv1 = swap(
-        call(send_kernel, shape(NB, R1, FS), (recv, mt1, sums1, up, metal, lo1, hi1), "pack")
-    )
+    message, lo1, hi1 = call(
+        send_kernel,
+        (shape(NB, R1, FS), shape(32, FS), shape(32, FS)),
+        (recv, mt1, sums1, first, metal, first1, second1),
+        "pack",
+    )
+    recv1 = swap(message)
     fluid, solid = call(
         last_kernel,
-        (shape(FZ, FP, FS), shape(SD, FS)),
+        (field, shape(SD, FS)),
         (recv1, recv, mt1, fluid2, sv, pv, film, cond, owner, lo, hi, lo1, hi1, metal),
         "steps",
         work,
@@ -680,7 +766,8 @@
 
     def chosen(*args):
         fits = args[0].shape == (FZ, FP, FS) and args[4].shape == (1, SD, FS)
-        return two_exchanges(*args) if fits and sizes["blk"] == NB else local(*args)
+        fits = fits and sizes["blk"] == NB and sizes["sec"] % 2 == 0
+        return two_exchanges(*args) if fits else local(*args)
 
     return jax.shard_map(
         chosen,

time: 44.8 us -> 38.7 us (0.86)
  local copies, waits for them, and re-layouts: 8.1 us -> 0.02 us
  Pallas kernels: 3.45 us -> 6.44 us
  starting transfers between devices: 3.07 us -> 4.85 us
  between operations: 2.05 us -> 0.72 us
  waiting for transfers between devices: 2.42 us -> 1.34 us
    slice x6 -> x0, local copies, waits for them, and re-layouts: 4.42 us -> none  [the longest x1 0.88 us: rows(): fluid[:, outer]]
    unnamed x20 -> x8, local copies, waits for them, and re-layouts: 3.51 us -> 0.02 us
    pallas_call x6 -> x7, Pallas kernels: 3.45 us -> 6.44 us  [call(): pl.pallas_call(kernel, out_shape=outs, in_specs=[HBM] * far + [VMEM] * (l...]
    ppermute x4, starting transfers between devices: 3.07 us -> 4.85 us  [the longest x2 2.71 us: both_ways(): second = lax.ppermute(second, 'sec', far)]
    ppermute x4, waiting for transfers between devices: 2.42 us -> 1.34 us  [the longest x2 1.33 us: both_ways(): second = lax.ppermute(second, 'sec', far)]
  transfers between devices with their start and end apart: 4 -> 4, of which waited for: 2 -> 1; matrix products, arithmetic and copies ran while one was open for 0% -> 0% of each run, Pallas kernels for 2% -> 5%
where the time goes in v2:
time: 38.7 us; the launch traced here: 38.4 us
  blocking collectives  25 us (65%)
  Pallas kernels  6.44 us (17%)
  starting transfers between devices  4.85 us (13%)
  waiting for transfers between devices  1.34 us (3%)
  between operations  0.72 us (2%)
    all_to_all x2, blocking collectives, swap(): lax.all_to_all(message, 'blk', split_axis=0, concat_axis=0, tiled=True)  25 us
    pallas_call x7, Pallas kernels, call(): pl.pallas_call(kernel, out_shape=outs, in_specs=[HBM] * far + [VMEM] * (l...  6.44 us
    ppermute x2, starting transfers between devices, both_ways(): second = lax.ppermute(second, 'sec', far)  2.71 us
    ppermute x2, starting transfers between devices, both_ways(): return (lax.ppermute(first, 'sec', near), second)  2.14 us
    ppermute x2, waiting for transfers between devices, both_ways(): second = lax.ppermute(second, 'sec', far)  1.33 us
  transfers between devices with their start and end apart: 4, of which 1 were waited for; matrix products, arithmetic and copies ran while one was open for 0% of the time, Pallas kernels for 5%

profile of v2, /device:TPU:0, one launch (start us, length us, event | category | flops | bytes accessed | tf_op | source)
XLA Modules:
  0.0 38.4 jit_solution(2705618806980444215)
XLA Ops:
  0.6 0.0 copy-start
  0.6 0.0 copy-start.1
  0.7 0.0 copy-start.2
  0.7 1.7 %rows.1 = (f32[40,128]{1,0:T(8,128)}, f32[40,128]{1,0:T(8,128)}) custom-call(f32[8,64,128]{2,1,0:T(8,128)} %fluid.1, f32[8,64,128]{2,1,0:T(8,128)} %sv.1, f32[8,64,128]{2,1,0:T(8,128)} %pv.1, f32[64,128]{1,0:T(8,128)} %film.1, f32[32,128]{1,0:T(8,128)} %bitcast.4, s32[1,64]{1,0:T(1,128)} %bitcast.7), custom_call_target="tpu_custom_call" | custom-call | tf_op jit(solution)/shard_map/rows/pallas_call | solution.py:554
  2.3 0.5 %collective-permute-start = (f32[40,128]{1,0:T(8,128)}, f32[40,128]{1,0:T(8,128)S(1)}, u32[]{:S(2)}, u32[]{:S(2)}) collective-permute-start(f32[40,128]{1,0:T(8,128)} %get-tuple-element.31), channel_id=1, source_target_pairs={{0,8},{8,0},{16,24},{24,16},{1,9},{9,1},{17,25},{25,17},{2,10},{10... | collective-permute-start | bytes 61448 | tf_op jit(solution)/shard_map/ppermute | solution.py:570
  2.8 0.0 copy-start.3
  2.8 2.6 %collective-permute-start.1 = (f32[40,128]{1,0:T(8,128)}, f32[40,128]{1,0:T(8,128)S(1)}, u32[]{:S(2)}, u32[]{:S(2)}) collective-permute-start(f32[40,128]{1,0:T(8,128)} %get-tuple-element.32), channel_id=1, source_target_pairs={{0,24},{8,16},{16,8},{24,0},{1,25},{9,17},{17,9},{25,1},{2,26},{10... | collective-permute-start | bytes 61448 | tf_op jit(solution)/shard_map/ppermute | solution.py:569
  5.5 0.0 copy-done
  5.5 0.0 copy-done.1
  5.5 0.0 copy-done.2
  5.5 0.0 copy-done.3
  5.5 1.7 %columns.1 = (f32[128,128]{1,0:T(8,128)S(1)}, f32[16,128]{1,0:T(8,128)S(1)}, f32[8,64,128]{2,1,0:T(8,128)S(1)}, f32[8,64,128]{2,1,0:T(8,128)S(1)}, f32[8,64,128]...) custom-call(f32[8,64,128]{2,1,0:T(8,128)} %fluid.1, ...), custom_call_target="tpu_custom_call" | custom-call | tf_op jit(solution)/shard_map/columns/pallas_call | solution.py:554
  7.2 0.0 collective-permute-done.first
  7.2 0.0 collective-permute-done.1.second
  7.2 0.1 pack.2
  7.3 14.3 %all_to_all.10.recv = f32[8,48,128]{2,1,0:T(8,128)S(1)} all-to-all(f32[8,48,128]{2,1,0:T(8,128)S(1)} %get-tuple-element.33), channel_id=1, replica_groups=mesh['sec'=4,'blk'=8] {'blk'}, dimensions={0} | all-to-all | bytes 393216 | tf_op jit(solution)/shard_map/all_to_all | solution.py:574
  21.6 1.0 %steps.2 = (f32[8,64,128]{2,1,0:T(8,128)S(1)}, f32[32,128]{1,0:T(8,128)S(1)}, f32[32,128]{1,0:T(8,128)S(1)}, f32[96,128]{1,0:T(8,128)S(1)}) custom-call(f32[8,48,128]{2,1,0:T(8,128)S(1)} %all_to_all.10.recv, f32[128,128]{1,0:T(8,128)S(1)} %get-tuple-element.27.mt, f32[8,64,128]{2,1,0:T(8,128)S(1)} %get-tuple-element.34.fluid, ...), custom_call_target="tpu_custom_call" | custom-call | tf_op jit(solution)/shard_map/steps/pallas_call | solution.py:554
  22.6 0.1 collective-permute-start.3
  22.7 1.6 %collective-permute-start.2 = (f32[32,128]{1,0:T(8,128)S(1)}, f32[32,128]{1,0:T(8,128)S(1)}, u32[]{:S(2)}, u32[]{:S(2)}) collective-permute-start(f32[32,128]{1,0:T(8,128)S(1)} %get-tuple-element.44.mine), channel_id=1, source_target_pairs={{0,8},{8,0},{16,24},{24,16},{1,9},{9,1},{17,25},{25,17},{2,10},{10... | collective-permute-start | bytes 49160 | tf_op jit(solution)/shard_map/ppermute | solution.py:570
  24.3 0.3 sums.1
  24.6 1.3 %collective-permute-done.3.second = f32[32,128]{1,0:T(8,128)S(1)} collective-permute-done((f32[32,128]{1,0:T(8,128)S(1)}, f32[32,128]{1,0:T(8,128)S(1)}, u32[]{:S(2)}, u32[]{:S(2)}) %collective-permute-start.3) | collective-permute-done | bytes 16416 | tf_op jit(solution)/shard_map/ppermute | solution.py:569
  25.9 0.0 collective-permute-done.2.first
  25.9 0.1 pack.3
  26.0 10.7 %all_to_all.11.recv1 = f32[8,40,128]{2,1,0:T(8,128)S(1)} all-to-all(f32[8,40,128]{2,1,0:T(8,128)S(1)} %get-tuple-element.47), channel_id=1, replica_groups=mesh['sec'=4,'blk'=8] {'blk'}, dimensions={0} | all-to-all | bytes 327680 | tf_op jit(solution)/shard_map/all_to_all | solution.py:574
  36.7 1.7 %steps.3 = (f32[8,64,128]{2,1,0:T(8,128)}, f32[32,128]{1,0:T(8,128)}) custom-call(f32[8,40,128]{2,1,0:T(8,128)S(1)} %all_to_all.11.recv1, f32[8,48,128]{2,1,0:T(8,128)S(1)} %all_to_all.10.recv, f32[136,128]{1,0:T(8,128)S(1)} %get-tuple-element.42.mt, f32[8,64,128]{2,1,0:T(8,128)S(1)} %get-tuple-element.41.fluid2, f32[8,64,128]{2,1,0:T(8,128)S(1)} %get-tuple-element.35.sv, ...), custom_call_target="tpu_custom_call" | custom-call | tf_op jit(solution)/shard_map/steps/pallas_call | solution.py:554
Async XLA Ops:
  0.6 4.9 %copy-start = (f32[64,128]{1,0:T(8,128)S(1)}, f32[64,128]{1,0:T(8,128)}, u32[]{:S(2)}) copy-start(f32[64,128]{1,0:T(8,128)} %film.1) | copy-start | bytes 98308
  0.6 4.9 %copy-start.1 = (f32[1,32,128]{2,1,0:T(8,128)S(1)}, f32[1,32,128]{2,1,0:T(8,128)}, u32[]{:S(2)}) copy-start(f32[1,32,128]{2,1,0:T(8,128)} %param.11) | copy-start | bytes 49156
  0.7 4.8 %copy-start.2 = (f32[1,32,128]{2,1,0:T(8,128)S(1)}, f32[1,32,128]{2,1,0:T(8,128)}, u32[]{:S(2)}) copy-start(f32[1,32,128]{2,1,0:T(8,128)} %param.12) | copy-start | bytes 49156
  2.3 4.8 %collective-permute-start = (f32[40,128]{1,0:T(8,128)}, f32[40,128]{1,0:T(8,128)S(1)}, u32[]{:S(2)}, u32[]{:S(2)}) collective-permute-start(f32[40,128]{1,0:T(8,128)} %get-tuple-element.31), channel_id=1, source_target_pairs={{0,8},{8,0},{16,24},{24,16},{1,9},{9,1},{17,25},{25,17},{2,10},{10... | collective-permute-start | bytes 61448 | tf_op jit(solution)/shard_map/ppermute | solution.py:570
  2.8 2.7 %copy-start.3 = (s32[1,1,64,1]{2,3,1,0:T(1,128)S(1)}, s32[1,1,64,1]{2,3,1,0:T(1,128)}, u32[]{:S(2)}) copy-start(s32[1,1,64,1]{2,3,1,0:T(1,128)} %param.13) | copy-start | bytes 772
  2.8 4.3 %collective-permute-start.1 = (f32[40,128]{1,0:T(8,128)}, f32[40,128]{1,0:T(8,128)S(1)}, u32[]{:S(2)}, u32[]{:S(2)}) collective-permute-start(f32[40,128]{1,0:T(8,128)} %get-tuple-element.32), channel_id=1, source_target_pairs={{0,24},{8,16},{16,8},{24,0},{1,25},{9,17},{17,9},{25,1},{2,26},{10... | collective-permute-start | bytes 61448 | tf_op jit(solution)/shard_map/ppermute | solution.py:569
  22.6 3.3 %collective-permute-start.3 = (f32[32,128]{1,0:T(8,128)S(1)}, f32[32,128]{1,0:T(8,128)S(1)}, u32[]{:S(2)}, u32[]{:S(2)}) collective-permute-start(f32[32,128]{1,0:T(8,128)S(1)} %get-tuple-element.46), channel_id=1, source_target_pairs={{0,24},{8,16},{16,8},{24,0},{1,25},{9,17},{17,9},{25,1},{2,26},{10... | collective-permute-start | bytes 49160 | tf_op jit(solution)/shard_map/ppermute | solution.py:569
  22.7 3.3 %collective-permute-start.2 = (f32[32,128]{1,0:T(8,128)S(1)}, f32[32,128]{1,0:T(8,128)S(1)}, u32[]{:S(2)}, u32[]{:S(2)}) collective-permute-start(f32[32,128]{1,0:T(8,128)S(1)} %get-tuple-element.44.mine), channel_id=1, source_target_pairs={{0,8},{8,0},{16,24},{24,16},{1,9},{9,1},{17,25},{25,17},{2,10},{10... | collective-permute-start | bytes 49160 | tf_op jit(solution)/shard_map/ppermute | solution.py:570

commit v3 on v0

--- a/solution.py
+++ b/solution.py
@@ -1,6 +1,8 @@
 import jax
 import jax.numpy as jnp
 from jax import lax
+from jax.experimental import pallas as pl
+from jax.experimental.pallas import tpu as pltpu
 from jax.sharding import PartitionSpec as P
 
 SUB = 4
@@ -12,6 +14,736 @@
 SOLID_STEP = 0.04
 COOLING = 0.5
 COOLANT = -1.0
+
+F32 = jnp.float32
+NB = 8
+FZ = 8
+FP = 64
+FS = 128
+SD = 32
+R0 = 40
+R1 = 32
+ROWS = 48
+OPEN_ROOM = 56 * 1024
+
+
+def lanes(rows):
+    return lax.broadcasted_iota(jnp.int32, (rows, FS), 1)
+
+
+def subs(rows):
+    return lax.broadcasted_iota(jnp.int32, (rows, FS), 0)
+
+
+def turn(x, shift, axis=1):
+    return pltpu.roll(x, shift % x.shape[axis], axis)
+
+
+def by_owner(owner, values):
+    sub = subs(NB)
+    outs = [jnp.zeros((NB, FS), F32) for _ in values]
+    for o in range(NB):
+        mine = owner == o
+        for i, value in enumerate(values):
+            total = jnp.sum(jnp.where(mine, value, 0.0), axis=0, keepdims=True)
+            outs[i] = jnp.where(sub == o, total, outs[i])
+    return outs
+
+
+def pick(owner, table):
+    out = jnp.zeros(owner.shape, F32)
+    for o in range(NB):
+        out = jnp.where(owner == o, table[o : o + 1], out)
+    return out
+
+
+def pick_lane(owner_row, table, lane):
+    column = jnp.broadcast_to(table[:, lane : lane + 1], (NB, FS))
+    named = jnp.broadcast_to(owner_row, (NB, FS)) == subs(NB).astype(F32)
+    return jnp.sum(jnp.where(named, column, 0.0), axis=0, keepdims=True)
+
+
+def stencil(x, low, high, left, right, below, above, sv, pv):
+    spread = SPREAD * (low + high + left + right + below + above - 6.0 * x)
+    carried = (
+        -ADVECT * sv * (x - left)
+        - ADVECT * jnp.maximum(pv, 0.0) * (x - low)
+        + ADVECT * jnp.maximum(-pv, 0.0) * (high - x)
+    )
+    return x + spread + carried
+
+
+def span(x):
+    sub = subs(FZ)
+    below = jnp.where(sub == 0, x, turn(x, 1, 0))
+    above = jnp.where(sub == FZ - 1, x, turn(x, FZ - 1, 0))
+    return below, above
+
+
+def halo_row(x, low, high, left_corner, right_corner, sv, pv, flux):
+    lane = lanes(FZ)
+    left = jnp.where(lane == 0, left_corner, turn(x, 1))
+    right = jnp.where(lane == FS - 1, right_corner, turn(x, -1))
+    below, above = span(x)
+    new = stencil(x, low, high, left, right, below, above, sv, pv)
+    return new - jnp.where(subs(FZ) == 0, WALL * flux, 0.0)
+
+
+def edge_part(x, low_end, high_end, left, right, sv, pv, film):
+    lane = lanes(FZ)
+    low = jnp.where(lane == 0, low_end, turn(x, 1))
+    high = jnp.where(lane == FP - 1, high_end, turn(x, -1))
+    below, above = span(x)
+    new = stencil(x, low, high, left, right, below, above, sv, pv)
+    return new - jnp.where(subs(FZ) == 0, WALL * film * x, 0.0)
+
+
+def set_row(x, row, at):
+    if at == 0:
+        return jnp.concatenate([jnp.where(subs(8) == 0, row, x[:8]), x[8:]], axis=0)
+    return jnp.concatenate([x[:-8], jnp.where(subs(8) == 7, row, x[-8:])], axis=0)
+
+
+def advance(src, dst, low_row, high_row, columns, base, sv, pv, film, wall):
+    lane = lanes(FP)
+    for z in range(FZ):
+        x = src[z]
+        low = set_row(turn(x, 1, 0), low_row[z : z + 1], 0)
+        high = set_row(turn(x, -1, 0), high_row[z : z + 1], 1)
+        edge = turn(columns, -(base + 2 * z + 1))
+        left = jnp.where(lane == 0, edge, turn(x, 1))
+        right = jnp.where(lane == FS - 1, edge, turn(x, -1))
+        new = stencil(
+            x, low, high, left, right, src[max(z - 1, 0)], src[min(z + 1, FZ - 1)], sv[z], pv[z]
+        )
+        if z == 0:
+            new = new - WALL * film * (x - wall)
+        dst[z] = new
+
+
+def strip_row(here, k_here, under, k_under):
+    sub, lane = subs(NB), lanes(NB)
+
+    def prev(x):
+        moved = turn(x, 1)
+        carried = jnp.where(sub == 0, 0.0, turn(moved, 1, 0))
+        return jnp.where(lane == 0, carried, moved)
+
+    def following(x):
+        moved = turn(x, -1)
+        carried = jnp.where(sub == NB - 1, 0.0, turn(moved, -1, 0))
+        return jnp.where(lane == FS - 1, carried, moved)
+
+    flow = (
+        0.5 * (k_here + prev(k_here)) * (prev(here) - here)
+        + 0.5 * (k_here + following(k_here)) * (following(here) - here)
+        + 0.5 * (k_here + k_under) * (under - here)
+    )
+    return here + SOLID_STEP * flow
+
+
+def conduct_of(conductivity, solid):
+    return conductivity * (1.0 + 0.25 * jnp.tanh(solid))
+
+
+def metal_step(own, halo, c_own, c_halo, keep):
+    depth_cells = own.shape[0]
+    k_own, k_halo = conduct_of(c_own, own), conduct_of(c_halo, halo)
+    lane, sub = lanes(depth_cells), subs(depth_cells)
+
+    def depth(x):
+        up = jnp.where(sub == 0, x, turn(x, 1, 0))
+        down = jnp.where(sub == depth_cells - 1, x, turn(x, -1, 0))
+        return up, down
+
+    def stream(x, other):
+        prev = jnp.where(lane == 0, turn(other, 1), turn(x, 1))
+        following = jnp.where(lane == FS - 1, turn(other, -1), turn(x, -1))
+        return prev, following
+
+    def update(x, k, other, k_other):
+        flow = jnp.zeros_like(x)
+        for a, ka in zip(stream(x, other) + depth(x), stream(k, k_other) + depth(k)):
+            flow = flow + 0.5 * (k + ka) * (a - x)
+        new = x + SOLID_STEP * flow
+        return new + jnp.where(sub == SD - 1, SOLID_STEP * COOLING * (COOLANT - x), 0.0)
+
+    return update(own, k_own, halo, k_halo), update(halo, k_halo, own, k_own) * keep
+
+
+def row_of(table, index):
+    return jnp.sum(jnp.where(subs(NB) == index, table, 0.0), axis=0, keepdims=True)
+
+
+def set_walls(own, halo, walls, me, keep):
+    sub, lane = subs(own.shape[0]), lanes(own.shape[0])
+    beside = jnp.where(lane >= FS // 2, row_of(walls, me - 1), row_of(walls, me + 1)) * keep
+    return jnp.where(sub == 0, row_of(walls, me), own), jnp.where(sub == 0, beside, halo)
+
+
+def metal_halo(turned, rows):
+    deep = turned[FP : FP + rows]
+    lane = lanes(rows)
+
+    def placed(left, right):
+        return jnp.where(
+            lane >= 124, turn(deep, left), jnp.where(lane < 4, turn(deep, right), 0.0)
+        )
+
+    return placed(108, 104), placed(104, 100)
+
+
+def keeps(me):
+    return (me > 0).astype(F32), (me < NB - 1).astype(F32)
+
+
+def block_of(recv, me, start):
+    keep_l, keep_r = keeps(me)
+    before, after = jnp.maximum(me - 1, 0), jnp.minimum(me + 1, NB - 1)
+    part = slice(start, start + 8)
+    return recv[before, part, :] * keep_l, recv[after, part, :] * keep_r
+
+
+def column_blocks(mt):
+    right = mt[pl.ds(1, FZ, stride=4), :], mt[pl.ds(0, FZ, stride=4), :]
+    left = mt[pl.ds(2, FZ, stride=4), :], mt[pl.ds(3, FZ, stride=4), :]
+    return right, left
+
+
+def flows(mt):
+    right, left = mt[pl.ds(32, FZ, stride=2), :], mt[pl.ds(33, FZ, stride=2), :]
+    return (turn(right, 64), right, mt[48:49, :]), (turn(left, 64), left, mt[49:50, :])
+
+
+def gather_columns(fluid, lane):
+    acc = jnp.zeros((FP, FS), F32)
+    for z in range(FZ):
+        acc = jnp.where(lane // 4 == z, turn(fluid[z], 4 * z + 2), acc)
+    return acc
+
+
+def sorted_rows(first, second):
+    even = lax.axis_index("sec") % 2 == 0
+    return (
+        lambda a, b: jnp.where(even, second[a:b, :], first[a:b, :]),
+        lambda a, b: jnp.where(even, first[a:b, :], second[a:b, :]),
+    )
+
+
+def send_rows(first, second, start, up, down):
+    even = lax.axis_index("sec") % 2 == 0
+    part = slice(start, start + up.shape[0])
+    first[part, :] = jnp.where(even, up, down)
+    second[part, :] = jnp.where(even, down, up)
+
+
+def up_factor(pv):
+    return SPREAD + ADVECT * jnp.maximum(pv, 0.0)
+
+
+def down_factor(pv):
+    return SPREAD + ADVECT * jnp.maximum(-pv, 0.0)
+
+
+def fetch(copies, sems):
+    started = [
+        pltpu.make_async_copy(src, dst, sems.at[i]) for i, (src, dst) in enumerate(copies)
+    ]
+    for copy in started:
+        copy.start()
+    return started
+
+
+def open_kernel(
+    fluid_in, sv_in, pv_in, film_in, solid_in, cond_in, owner,
+    out, first, second, mt, names, fluid, sv, pv, film, solid, cond, ids, sems,
+):
+    me = lax.axis_index("blk")
+    half = FZ // 2
+    copies = [(owner, ids), (film_in, film), (solid_in, solid), (cond_in, cond)]
+    for src, dst in ((fluid_in, fluid), (pv_in, pv), (sv_in, sv)):
+        for part in range(2):
+            copies.append((src.at[pl.ds(half * part, half)], dst.at[pl.ds(half * part, half)]))
+    started = fetch(copies, sems)
+    lane = lanes(FP)
+    for copy in started[:4]:
+        copy.wait()
+    ids_row = jnp.concatenate([ids[...].astype(F32), jnp.zeros((1, FS - FP), F32)], axis=1)
+    named = jnp.broadcast_to(ids_row, (FS, FS)).T[:FP]
+    names[...] = named
+    metal = jnp.zeros((SD, FS), F32)
+    thin = lanes(SD)
+    s, c = solid[...], cond[...]
+    for k in range(4):
+        metal = jnp.where(thin == 4 * k + 1, turn(s, 3 * k + 5), metal)
+        metal = jnp.where(thin == 4 * k + 2, turn(s, 3 * k + 2), metal)
+        metal = jnp.where(thin == 4 * k + 17, turn(c, 3 * k + 21), metal)
+        metal = jnp.where(thin == 4 * k + 18, turn(c, 3 * k + 18), metal)
+    started[4].wait()
+    a0, h = by_owner(named, [film[...] * fluid[0], film[...]])
+    started[5].wait()
+    top = gather_columns(fluid, lane)
+    send_rows(first, second, 0, fluid[:, FP - 1, :], fluid[:, 0, :])
+    blank = jnp.zeros((7, FS), F32)
+    send_rows(
+        first, second, 40,
+        jnp.concatenate([film[FP - 1 : FP, :], blank], axis=0),
+        jnp.concatenate([film[0:1, :], blank], axis=0),
+    )
+    for copy in started[6:]:
+        copy.wait()
+    send_rows(first, second, 8, sv[:, FP - 2, :], sv[:, 1, :])
+    send_rows(first, second, 16, sv[:, FP - 1, :], sv[:, 0, :])
+    send_rows(first, second, 24, pv[:, FP - 2, :], pv[:, 1, :])
+    send_rows(first, second, 32, pv[:, FP - 1, :], pv[:, 0, :])
+    bottom = jnp.zeros((FP, FS), F32)
+    pair = (lane - 32) // 2
+    for z in range(FZ):
+        here = (pair == z) & (lane >= 32)
+        top = jnp.where(here, turn(pv[z], 33 + 2 * z), top)
+        bottom = jnp.where(here, turn(sv[z], 33 + 2 * z), bottom)
+    top = jnp.where(lane // 2 == 24, turn(film[...], 49), top)
+    top = jnp.where(lane == 50, named, top)
+    metal = jnp.where(thin < 32, metal, bottom[:SD])
+    mt[...] = jnp.concatenate([top, metal, bottom[SD:]], axis=0).T
+
+    (r0, r1), (l0, l1) = column_blocks(mt)
+    (sv_r, pv_r, film_r), (sv_l, pv_l, film_l) = flows(mt)
+    wide = lanes(FZ)
+    right_part = edge_part(r0, 0.0, 0.0, r1, 0.0, sv_r, pv_r, film_r)
+    left_part = edge_part(l0, 0.0, 0.0, 0.0, l1, sv_l, pv_l, film_l)
+    right_part = jnp.where(wide < FP, right_part, SPREAD)
+    left_part = jnp.where(wide < FP, left_part, turn(SPREAD + ADVECT * sv_l, 64))
+
+    def with_factors(block, p):
+        block = jnp.where(wide == 96, turn(up_factor(p), 96), block)
+        return jnp.where(wide == 97, turn(down_factor(p), 97 - (FP - 1)), block)
+
+    r0, l0 = with_factors(r0, pv_r), with_factors(l0, pv_l)
+    owner_row = turn(mt[50:51, :], 64)
+    inside = lanes(1) < FP
+    right_row, left_row = (jnp.where(inside, f, owner_row) for f in (film_r, film_l))
+    head = jnp.concatenate([s[0:2], c[0:2], named[FP - 1 : FP], named[0:1]], axis=0)
+    for peer in range(NB):
+        ahead = (me + 1 == peer).astype(F32)
+        behind = (me - 1 == peer).astype(F32)
+        special = right_row * ahead + left_row * behind
+        out[peer, 0:8, :] = jnp.concatenate([head, special, special], axis=0)
+        out[peer, 8:16, :] = a0
+        out[peer, 16:24, :] = h
+        same = (me == peer).astype(F32)
+        out[peer, 24:32, :] = r0 * ahead + l0 * behind + r0 * same
+        out[peer, 32:40, :] = right_part * ahead + left_part * behind + l0 * same
+
+
+def halo_columns(known_l, known_r, factor_l, factor_r, rows, mine_right, mine_left, walls, me):
+    keep_l, keep_r = keeps(me)
+    (film_l, own_l), (film_r, own_r) = rows
+    top = subs(FZ) == 0
+    wall_l, wall_r = pick_lane(own_l, walls, FS - 1), pick_lane(own_r, walls, 0)
+    new_l = known_l + factor_l * mine_left + jnp.where(top, WALL * film_l * wall_l, 0.0)
+    new_r = known_r + factor_r * mine_right + jnp.where(top, WALL * film_r * wall_r, 0.0)
+    return new_l * keep_l, new_r * keep_r
+
+
+def edge_rows(recv, me):
+    return [(block[6:7], turn(block[6:7], 64)) for block in block_of(recv, me, 0)]
+
+
+def first_kernel(
+    recv, fluid, sv, pv, film, solid, cond, owner, first, second,
+    fluid1, first_out, second_out, turned, side, tm,
+):
+    me = lax.axis_index("blk")
+    lo, hi = sorted_rows(first, second)
+    left, right = block_of(recv, me, 24)
+    part_l, part_r = block_of(recv, me, 32)
+    wall0, under0 = recv[:, 0, :], recv[:, 1, :]
+    c0, c1 = recv[:, 2, :], recv[:, 3, :]
+    a0, h = recv[0, 8:16, :], recv[0, 16:24, :]
+    for j in range(1, NB):
+        a0, h = a0 + recv[j, 8:16, :], h + recv[j, 16:24, :]
+    wall1 = strip_row(wall0, conduct_of(c0, wall0), under0, conduct_of(c1, under0))
+    wall1 = wall1 + SOLID_STEP * (a0 - h * wall0)
+
+    mine_right, mine_left = recv[me, 24:32, :], recv[me, 32:40, :]
+    new_l, new_r = halo_columns(
+        part_l, part_r, turn(part_l, 64), turn(part_r, 64), edge_rows(recv, me),
+        mine_right, mine_left, wall0, me,
+    )
+    tm[...] = jnp.zeros((FS, FS), F32)
+    tm[pl.ds(0, FZ, stride=2), :] = right
+    tm[pl.ds(1, FZ, stride=2), :] = left
+    tm[16:24, :] = left
+    tm[24:32, :] = right
+    tm[pl.ds(32, FZ, stride=2), :] = new_r
+    tm[pl.ds(33, FZ, stride=2), :] = new_l
+    turned[...] = tm[...].T
+    named = owner[...]
+    walls0, walls1 = pick(named, wall0), pick(named, wall1)
+    advance(fluid, fluid1, lo(0, 8), hi(0, 8), turned[:FP, :], 0, sv, pv, film[...], walls0)
+    flux = film[...] * (fluid1[0] - walls1)
+    (shares,) = by_owner(named, [flux])
+
+    keep_l, keep_r = keeps(me)
+    keep = jnp.where(lanes(8) >= FS // 2, keep_l, keep_r)
+    halo, c_halo = metal_halo(turned, 8)
+    own, halo = metal_step(solid[0:8, :], halo, cond[0:8, :], c_halo, keep)
+    own, halo = set_walls(own, halo, wall1, me, keep)
+    own, _ = metal_step(own, halo, cond[0:8, :], c_halo, keep)
+    shares = SOLID_STEP * shares + jnp.where(subs(NB) == me, own[0:1], 0.0)
+    side[0:8, :], side[8:16, :], side[16:24, :] = wall1, shares, h
+
+    lane = lanes(FZ)
+
+    def corners(at, beside, factor):
+        out = jnp.zeros((FZ, FS), F32)
+        for i, (old, new) in enumerate(((left, new_l), (right, new_r))):
+            for k, (source, lane_of) in enumerate(
+                ((old, at), (new, at), (old, factor), (new, beside))
+            ):
+                out = jnp.where(lane == 4 * i + k, turn(source, 4 * i + k - lane_of), out)
+        return out
+
+    blank = jnp.zeros((6, FS), F32)
+    for i in range(3):
+        send_rows(first_out, second_out, 8 * i, fluid1[:, FP - 3 + i, :], fluid1[:, 2 - i, :])
+    send_rows(first_out, second_out, 24, corners(FP - 1, FP - 2, 97), corners(0, 1, 96))
+    send_rows(first_out, second_out, 32, pick(recv[:, 4, :], shares), pick(recv[:, 5, :], shares))
+    send_rows(
+        first_out, second_out, 40,
+        jnp.concatenate([flux[FP - 2 : FP], blank], axis=0),
+        jnp.concatenate([flux[1:2], flux[0:1], blank], axis=0),
+    )
+
+
+def sums_kernel(
+    fluid1, turned, side, sv, pv, film, solid, cond, owner, fluid2, mt, sums, metal
+):
+    me = lax.axis_index("blk")
+    lane, sub = lanes(FP), subs(FP)
+    named, f = owner[...], film[...]
+    wall1 = side[0:8, :]
+    none = jnp.zeros((FZ, FS), F32)
+    advance(fluid1, fluid2, none, none, turned[:FP, :], 32, sv, pv, f, pick(named, wall1))
+    x = fluid2[0]
+    low, high = turn(x, 1, 0), turn(x, -1, 0)
+    before = jnp.where(lane == 0, 0.0, turn(x, 1))
+    after = jnp.where(lane == FS - 1, 0.0, turn(x, -1))
+    moved = stencil(x, low, high, before, after, x, fluid2[1], sv[0], pv[0]) - WALL * f * x
+    within = jnp.where((sub == 0) | (sub == FP - 1), 0.0, f)
+    deep = jnp.where((sub < 2) | (sub >= FP - 2), 0.0, f)
+    sums[0:8, :], sums[8:16, :], sums[16:24, :] = by_owner(
+        named, [within * x, deep * moved, f * f]
+    )
+    whole = jnp.concatenate([gather_columns(fluid2, lane), jnp.zeros((FP, FS), F32)], axis=0)
+    mt[...] = whole.T
+    keep_l, keep_r = keeps(me)
+    keep = jnp.where(lanes(SD) >= FS // 2, keep_l, keep_r)
+    halo, c_halo = metal_halo(turned, SD)
+    own, halo = metal_step(solid[...], halo, cond[...], c_halo, keep)
+    own, halo = set_walls(own, halo, wall1, me, keep)
+    own, halo = metal_step(own, halo, cond[...], c_halo, keep)
+    metal[0:SD, :], metal[SD : 2 * SD, :], metal[2 * SD : 3 * SD, :] = own, halo, c_halo
+
+
+def pack_kernel(
+    recv, mt_old, mt, sums, metal, side, fluid1, fluid2, sv, pv, film, owner,
+    first, second, first1, second1, out, edge,
+):
+    me = lax.axis_index("blk")
+    lane, sub = lanes(FZ), subs(FZ)
+    keep_l, keep_r = keeps(me)
+    lo, hi = sorted_rows(first, second)
+    lo1, hi1 = sorted_rows(first1, second1)
+    left, right = block_of(recv, me, 24)
+    pv_first, pv_last = pv[:, 0, :], pv[:, FP - 1, :]
+
+    def outside(rows, rows1, inner, near_l, near_r):
+        far, mid, near = rows1(0, 8), rows1(8, 16), rows1(16, 24)
+        corner = rows1(24, 32)
+
+        def at(k, to):
+            return turn(corner, to - k)
+
+        def lane_at(x, of, to):
+            return turn(x, to - of)
+
+        old_l, old_r = at(0, 0), at(4, FS - 1)
+        side_l = at(1, 0) + at(2, 0) * lane_at(left, near_l, 0)
+        side_r = at(5, FS - 1) + at(6, FS - 1) * lane_at(right, near_r, FS - 1)
+        return far, mid, near, (old_l, old_r), (side_l, side_r), (at(3, 0), at(7, FS - 1))
+
+    def finish(rows, rows1, inner, own_partial, own_pv, factor, near_lane, factor_lane, upward):
+        far, mid, near, old, beside, beside2 = outside(rows, rows1, inner, near_lane, near_lane)
+        sv2, sv1, pv2, pv1 = rows(8, 16), rows(16, 24), rows(24, 32), rows(32, 40)
+        flux = rows1(40, 42)
+        order = (mid, inner) if upward else (inner, mid)
+        new1 = halo_row(near, *order, *beside, sv1, pv1, flux[1:2])
+        order = (far, near) if upward else (near, far)
+        new2 = halo_row(mid, *order, *beside2, sv2, pv2, flux[0:1])
+        through_l = turn(left, -factor_lane) * old[0]
+        through_r = turn(right, FS - 1 - factor_lane) * old[1]
+        own = own_partial + factor * near
+        sv_here = sv[:, 0 if upward else FP - 1, :]
+        own = own + jnp.where(lane == 0, (SPREAD + ADVECT * sv_here) * through_l, 0.0)
+        own = own + jnp.where(lane == FS - 1, SPREAD * through_r, 0.0)
+        return new1, new2, own
+
+    low1, low2, x_first = finish(
+        lo, lo1, fluid1[:, 0, :], fluid2[:, 0, :], pv_first, up_factor(pv_first), 0, 96, True
+    )
+    high1, high2, x_last = finish(
+        hi, hi1, fluid1[:, FP - 1, :], fluid2[:, FP - 1, :], pv_last, down_factor(pv_last),
+        FP - 1, 97, False,
+    )
+
+    (r0, r1), (l0, l1) = column_blocks(mt)
+
+    def patched(block, column):
+        block = jnp.where(lane == 0, turn(x_first, -column), block)
+        return jnp.where(lane == FP - 1, turn(x_last, FP - 1 - column), block)
+
+    r0, r1 = patched(r0, FS - 1), patched(r1, FS - 2)
+    l0, l1 = patched(l0, 0), patched(l1, 1)
+    (sv_r, pv_r, film_r), (sv_l, pv_l, film_l) = flows(mt_old)
+
+    def ends(column):
+        return turn(low1, -column), turn(high1, FP - 1 - column)
+
+    right_part = edge_part(r0, *ends(FS - 1), r1, 0.0, sv_r, pv_r, film_r)
+    left_part = edge_part(l0, *ends(0), 0.0, l1, sv_l, pv_l, film_l)
+
+    def corner_row(column):
+        rows = []
+        for i, x in enumerate((low1, high1)):
+            spread = jnp.broadcast_to(x[:, column : column + 1], (FZ, FS))
+            rows.append(
+                jnp.sum(jnp.where(lane == sub + 8 * i, spread, 0.0), axis=0, keepdims=True)
+            )
+        return rows[0] + rows[1]
+
+    rows = (0, 1, FP - 2, FP - 1)
+
+    def stack(parts):
+        return jnp.concatenate(list(parts) + [jnp.zeros((4, FS), F32)], axis=0)
+
+    layer = {r: fluid2[0, r : r + 1, :] for r in (1, 2, FP - 3, FP - 2)}
+    layer[-1], layer[0], layer[FP - 1], layer[FP] = (
+        low1[0:1], x_first[0:1], x_last[0:1], high1[0:1],
+    )
+    here = stack(layer[r] for r in rows)
+    above = stack([x_first[1:2], fluid2[1, 1:2, :], fluid2[1, FP - 2 : FP - 1, :], x_last[1:2]])
+    f4 = stack(film[r : r + 1, :] for r in rows)
+    sv4 = stack(sv[0, r : r + 1, :] for r in rows)
+    pv4 = stack(pv[0, r : r + 1, :] for r in rows)
+    before = jnp.where(lane == 0, 0.0, turn(here, 1))
+    after = jnp.where(lane == FS - 1, 0.0, turn(here, -1))
+    moved = f4 * (
+        stencil(
+            here, stack(layer[r - 1] for r in rows), stack(layer[r + 1] for r in rows),
+            before, after, here, above, sv4, pv4,
+        )
+        - WALL * f4 * here
+    )
+    direct = f4 * here
+    a2, b3, h2 = sums[0:8, :], sums[8:16, :], sums[16:24, :]
+    for i, r in enumerate(rows):
+        hit = owner[r : r + 1, :] == sub.astype(F32)
+        b3 = b3 + jnp.where(hit, moved[i : i + 1], 0.0)
+        if r in (0, FP - 1):
+            a2 = a2 + jnp.where(hit, direct[i : i + 1], 0.0)
+    (film_bl, own_bl), (film_br, own_br) = edge_rows(recv, me)
+    _, part_r = block_of(recv, me, 32)
+    inside = lane < FP
+
+    def shared(own_row, term):
+        hit = (jnp.broadcast_to(own_row, (NB, FS)) == sub.astype(F32)) & inside
+        return jnp.sum(jnp.where(hit, term, 0.0), axis=1, keepdims=True)
+
+    right_term = film_br * turn(part_r, 64)[0:1] * r0[0:1] * keep_r
+    left_term = film_bl * SPREAD * l0[0:1] * keep_l
+    b3 = b3 + jnp.where(lane == 0, shared(own_br, right_term), 0.0)
+    b3 = b3 + jnp.where(lane == FS - 1, shared(own_bl, left_term), 0.0)
+
+    right_corner, left_corner = corner_row(FS - 1), corner_row(0)
+    to_right = jnp.where(inside, r0, turn(right_part, 64))
+    to_left = jnp.where(inside, l0, turn(left_part, 64))
+    relay_lo, relay_hi = lo1(32, 40), hi1(32, 40)
+    blank = jnp.zeros((2, FS), F32)
+    for peer in range(NB):
+        ahead = (me + 1 == peer).astype(F32)
+        behind = (me - 1 == peer).astype(F32)
+        out[peer, 0:8, :] = jnp.concatenate(
+            [
+                metal[1:2, :],
+                b3[peer : peer + 1],
+                h2[peer : peer + 1],
+                relay_lo[peer : peer + 1],
+                relay_hi[peer : peer + 1],
+                right_corner * ahead + left_corner * behind,
+                blank,
+            ],
+            axis=0,
+        )
+        out[peer, 8:16, :] = side[8:16, :]
+        out[peer, 16:24, :] = a2
+        out[peer, 24:32, :] = to_right * ahead + to_left * behind
+    kept = (
+        low1, low2, high1, high2, r0, l0, x_first, x_last,
+        lo(16, 24), lo(32, 40), hi(16, 24), hi(32, 40), lo(40, 48), hi(40, 48),
+    )
+    for i, value in enumerate(kept):
+        edge[8 * i : 8 * i + 8, :] = value
+
+
+def last_kernel(
+    recv1, recv, edge, side, metal, fluid2, sv, pv, film, cond, owner, fluid_out, solid_out,
+    tm, fluid3,
+):
+    me = lax.axis_index("blk")
+    lane, sub = lanes(FZ), subs(FZ)
+    (
+        low1, low2, high1, high2, mine_right, mine_left, x_first, x_last,
+        sv_lo, pv_lo, sv_hi, pv_hi, film_lo, film_hi,
+    ) = [edge[8 * i : 8 * i + 8, :] for i in range(14)]
+    left, right = block_of(recv1, me, 24)
+    corner_l, corner_r = (block[5:6] for block in block_of(recv1, me, 0))
+    part_l, part_r = block_of(recv, me, 32)
+    c0, c1, h = recv[:, 2, :], recv[:, 3, :], side[16:24, :]
+    tail, wall2, a2 = recv1[0, 0:8, :], recv1[0, 8:16, :], recv1[0, 16:24, :]
+    for j in range(1, NB):
+        tail = tail + recv1[j, 0:8, :]
+        wall2 = wall2 + recv1[j, 8:16, :]
+        a2 = a2 + recv1[j, 16:24, :]
+    under2 = recv1[:, 0, :]
+    wall3 = strip_row(wall2, conduct_of(c0, wall2), under2, conduct_of(c1, under2))
+    wall3 = wall3 + SOLID_STEP * (a2 - h * wall2)
+    inflow3 = tail[1:2] + WALL * tail[2:3] * row_of(wall2, me) - row_of(h * wall3, me)
+
+    new_l, new_r = halo_columns(
+        turn(left, 64), turn(right, 64), turn(part_l, 64), turn(part_r, 64),
+        edge_rows(recv, me), mine_right, mine_left, wall2, me,
+    )
+    tm[...] = jnp.zeros((FS, FS), F32)
+    tm[pl.ds(0, FZ, stride=2), :] = right
+    tm[pl.ds(1, FZ, stride=2), :] = left
+    tm[pl.ds(32, FZ, stride=2), :] = new_r
+    tm[pl.ds(33, FZ, stride=2), :] = new_l
+    columns = tm[...].T[:FP]
+
+    def corner(row, which):
+        spread = jnp.broadcast_to(row, (FZ, FS))
+        return jnp.sum(jnp.where(lane == sub + 8 * which, spread, 0.0), axis=1, keepdims=True)
+
+    new_low = halo_row(
+        low1, low2, x_first, corner(corner_l, 0), corner(corner_r, 0), sv_lo, pv_lo,
+        film_lo[0:1] * (low1[0:1] - tail[3:4]),
+    )
+    new_high = halo_row(
+        high1, x_last, high2, corner(corner_l, 1), corner(corner_r, 1), sv_hi, pv_hi,
+        film_hi[0:1] * (high1[0:1] - tail[4:5]),
+    )
+    named, f = owner[...], film[...]
+    source = [
+        set_row(set_row(fluid2[z], x_first[z : z + 1], 0), x_last[z : z + 1], 1)
+        for z in range(FZ)
+    ]
+    advance(source, fluid3, low1, high1, columns, 0, sv, pv, f, pick(named, wall2))
+    advance(fluid3, fluid_out, new_low, new_high, columns, 32, sv, pv, f, pick(named, wall3))
+
+    keep_l, keep_r = keeps(me)
+    keep = jnp.where(lanes(SD) >= FS // 2, keep_l, keep_r)
+    own, halo, c_halo = metal[0:SD, :], metal[SD : 2 * SD, :], metal[2 * SD : 3 * SD, :]
+    own, halo = set_walls(own, halo, wall2, me, keep)
+    own, halo = metal_step(own, halo, cond[...], c_halo, keep)
+    own, halo = set_walls(own, halo, wall3, me, keep)
+    own, _ = metal_step(own, halo, cond[...], c_halo, keep)
+    solid_out[...] = own + jnp.where(subs(SD) == 0, SOLID_STEP * inflow3, 0.0)
+
+
+def shape(*dims):
+    return jax.ShapeDtypeStruct(dims, F32)
+
+
+VMEM = pl.BlockSpec(memory_space=pltpu.VMEM)
+GRANT = 54 * 1024 * 1024
+HBM = pl.BlockSpec(memory_space=pltpu.HBM)
+
+
+def call(kernel, outs, args, name, scratch=(), far=0, limit=32 * 1024 * 1024):
+    return pl.pallas_call(
+        kernel,
+        out_shape=outs,
+        in_specs=[HBM] * far + [VMEM] * (len(args) - far),
+        out_specs=jax.tree.map(lambda _: VMEM, outs),
+        scratch_shapes=scratch,
+        name=name,
+        compiler_params=pltpu.CompilerParams(vmem_limit_bytes=limit),
+    )(*args)
+
+
+def both_ways(first, second):
+    count = lax.axis_size("sec")
+    near = [(i, i ^ 1) for i in range(count)]
+    far = [(i, (i + 1 if i % 2 else i - 1) % count) for i in range(count)]
+    second = lax.ppermute(second, "sec", far)
+    return lax.ppermute(first, "sec", near), second
+
+
+def swap(message):
+    return lax.all_to_all(message, "blk", split_axis=0, concat_axis=0, tiled=True)
+
+
+def two_exchanges(fluid, sv, pv, film, solid, cond, face_owner):
+    owner = face_owner.reshape(1, FP)
+    solid, cond = solid.reshape(SD, FS), cond.reshape(SD, FS)
+    field, rows = shape(FZ, FP, FS), shape(ROWS, FS)
+    held = [pltpu.VMEM((FZ, FP, FS), F32)] * 3
+    held += [pltpu.VMEM((n, FS), F32) for n in (FP, SD, SD)]
+    message, first, second, mt, owner = call(
+        open_kernel,
+        (shape(NB, R0, FS), rows, rows, shape(FS, FS), shape(FP, FS)),
+        (fluid, sv, pv, film, solid, cond, owner),
+        "open",
+        held + [pltpu.VMEM((1, FP), jnp.int32), pltpu.SemaphoreType.DMA((10,))],
+        far=7,
+        limit=GRANT - OPEN_ROOM,
+    )
+    first, second = both_ways(first, second)
+    recv = swap(message)
+    fluid1, first1, second1, turned, side = call(
+        first_kernel,
+        (field, rows, rows, shape(FS, FS), shape(24, FS)),
+        (recv, fluid, sv, pv, film, solid, cond, owner, first, second),
+        "first",
+        [pltpu.VMEM((FS, FS), F32)],
+    )
+    first1, second1 = both_ways(first1, second1)
+    fluid2, mt2, sums, metal = call(
+        sums_kernel,
+        (field, shape(FS, FS), shape(24, FS), shape(3 * SD, FS)),
+        (fluid1, turned, side, sv, pv, film, solid, cond, owner),
+        "sums",
+    )
+    message, edge = call(
+        pack_kernel,
+        (shape(NB, R1, FS), shape(14 * 8, FS)),
+        (
+            recv, mt, mt2, sums, metal, side, fluid1, fluid2, sv, pv, film, owner,
+            first, second, first1, second1,
+        ),
+        "pack",
+    )
+    recv1 = swap(message)
+    fluid, solid = call(
+        last_kernel,
+        (field, shape(SD, FS)),
+        (recv1, recv, edge, side, metal, fluid2, sv, pv, film, cond, owner),
+        "last",
+        [pltpu.VMEM((FS, FS), F32), pltpu.VMEM((FZ, FP, FS), F32)],
+    )
+    return fluid, solid.reshape(1, SD, FS)
 
 
 def padded(block, sides, width, periodic):
@@ -130,8 +862,15 @@
         P("sec", None, "blk"),
         P("sec", "blk", None, None),
     )
+    sizes = dict(mesh.shape)
+
+    def chosen(*args):
+        fits = args[0].shape == (FZ, FP, FS) and args[4].shape == (1, SD, FS)
+        fits = fits and sizes["blk"] == NB and sizes["sec"] % 2 == 0
+        return two_exchanges(*args) if fits else local(*args)
+
     return jax.shard_map(
-        local,
+        chosen,
         mesh=mesh,
         in_specs=placed,
         out_specs=(P(None, "sec", "blk"), P("sec", None, "blk")),

time: 157 us -> 34.7 us (0.22)
  blocking collectives: 83.3 us -> 10.3 us
  starting transfers between devices: 37.7 us -> 10.7 us
  waiting for transfers between devices: 20.5 us -> 6.9 us
  Pallas kernels: 0 us -> 5.75 us
  other arithmetic: 5.14 us -> 0 us
  matrix products: 3.96 us -> 0 us
  local copies, waits for them, and re-layouts: 3.96 us -> 0.04 us
    all_gather x4 -> x0, blocking collectives: 83.3 us -> none  [local(): lax.all_gather(wall_row, 'blk', axis=0, tiled=True)]
    ppermute x16 -> x4, starting transfers between devices: 24.4 us -> 3.34 us  [the longest x2 3.26 us: both_ways(): second = lax.ppermute(second, 'sec', far)]
    all_to_all x4 -> x1, waiting for transfers between devices: 20.4 us -> 4.03 us  [swap(): lax.all_to_all(message, 'blk', split_axis=0, concat_axis=0, tiled=True)]
    all_to_all x0 -> x1, blocking collectives: none -> 10.3 us  [swap(): lax.all_to_all(message, 'blk', split_axis=0, concat_axis=0, tiled=True)]
    all_to_all x4 -> x1, starting transfers between devices: 13.4 us -> 7.4 us  [swap(): lax.all_to_all(message, 'blk', split_axis=0, concat_axis=0, tiled=True)]
    pallas_call x0 -> x5, Pallas kernels: none -> 5.75 us  [call(): pl.pallas_call(kernel, out_shape=outs, in_specs=[HBM] * far + [VMEM] * (l...]
    dot_general x8 -> x0, matrix products: 3.96 us -> none  [the longest x4 3.11 us: local(): jnp.einsum('ocb,bf->ocf', placing, flux, precision=lax.Precision.HIGHEST)]
    ppermute x16 -> x4, waiting for transfers between devices: 0.04 us -> 2.87 us  [the longest x2 2.86 us: both_ways(): second = lax.ppermute(second, 'sec', far)]
  transfers between devices with their start and end apart: 20 -> 5, of which waited for: 4 -> 3; matrix products, arithmetic and copies ran while one was open for 2% -> 0% of each run, Pallas kernels for 0% -> 2%
where the time goes in v3:
time: 34.7 us; the launch traced here: 34.4 us
  starting transfers between devices  10.7 us (31%)
  blocking collectives  10.3 us (30%)
  waiting for transfers between devices  6.9 us (20%)
  Pallas kernels  5.75 us (17%)
  between operations  0.77 us (2%)
    all_to_all x1, blocking collectives, swap(): lax.all_to_all(message, 'blk', split_axis=0, concat_axis=0, tiled=True)  10.3 us
    all_to_all x1, starting transfers between devices, swap(): lax.all_to_all(message, 'blk', split_axis=0, concat_axis=0, tiled=True)  7.4 us
    pallas_call x5, Pallas kernels, call(): pl.pallas_call(kernel, out_shape=outs, in_specs=[HBM] * far + [VMEM] * (l...  5.75 us
    all_to_all x1, waiting for transfers between devices, swap(): lax.all_to_all(message, 'blk', split_axis=0, concat_axis=0, tiled=True)  4.03 us
    ppermute x2, starting transfers between devices, both_ways(): second = lax.ppermute(second, 'sec', far)  3.26 us
    ppermute x2, waiting for transfers between devices, both_ways(): second = lax.ppermute(second, 'sec', far)  2.86 us
  transfers between devices with their start and end apart: 5, of which 3 were waited for; matrix products, arithmetic and copies ran while one was open for 0% of the time, Pallas kernels for 2%

profile of v3, /device:TPU:0, one launch (start us, length us, event | category | flops | bytes accessed | tf_op | source)
XLA Modules:
  0.0 34.4 jit_solution(7489921840228906731)
XLA Ops:
  0.6 0.0 copy-start.1
  0.6 0.0 copy-start.2
  0.7 0.0 copy-start.5
  0.7 0.0 copy-start.6
  0.7 2.5 %open.1 = (f32[8,40,128]{2,1,0:T(8,128)}, f32[48,128]{1,0:T(8,128)}, f32[48,128]{1,0:T(8,128)}, f32[128,128]{1,0:T(8,128)}, f32[64,128]{1,0:T(8,128)}) custom-call(f32[8,64,128]{2,1,0:T(8,128)} %fluid.1, f32[8,64,128]{2,1,0:T(8,128)} %sv.7, f32[8,64,128]{2,1,0:T(8,128)} %pv.7, f32[64,128]{1,0:T(8,128)} %film.7, f32[32,128]{1,0:T(8,128)} %bitcast.8, ...), custom_call_target="tpu_custom_call" | custom-call | tf_op jit(solution)/shard_map/open/pallas_call | solution.py:675
  3.2 0.0 copy-start
  3.2 0.0 copy-start.3
  3.2 0.0 copy-start.4
  3.2 7.4 %all-to-all-start = ((f32[8,40,128]{2,1,0:T(8,128)}), f32[8,40,128]{2,1,0:T(8,128)S(1)}, u32[]{:S(2)}, u32[]{:S(2)}) async-start(f32[8,40,128]{2,1,0:T(8,128)} %get-tuple-element.20), calls=%async_computation | async-start | bytes 327680 | tf_op jit(solution)/shard_map/all_to_all | solution.py:695
  10.6 0.0 collective-permute-start
  10.6 1.6 %collective-permute-start.1 = (f32[48,128]{1,0:T(8,128)}, f32[48,128]{1,0:T(8,128)S(1)}, u32[]{:S(2)}, u32[]{:S(2)}) collective-permute-start(f32[48,128]{1,0:T(8,128)} %get-tuple-element.24), channel_id=1, source_target_pairs={{0,24},{8,16},{16,8},{24,0},{1,25},{9,17},{17,9},{25,1},{2,26},{10... | collective-permute-start | bytes 73736 | tf_op jit(solution)/shard_map/ppermute | solution.py:690
  12.2 0.0 collective-permute-done.first
  12.2 1.9 %collective-permute-done.1.second = f32[48,128]{1,0:T(8,128)S(1)} collective-permute-done((f32[48,128]{1,0:T(8,128)}, f32[48,128]{1,0:T(8,128)S(1)}, u32[]{:S(2)}, u32[]{:S(2)}) %collective-permute-start.1) | collective-permute-done | bytes 24608 | tf_op jit(solution)/shard_map/ppermute | solution.py:690
  14.1 4.0 %all-to-all-done.recv = f32[8,40,128]{2,1,0:T(8,128)S(1)} async-done(((f32[8,40,128]{2,1,0:T(8,128)}), f32[8,40,128]{2,1,0:T(8,128)S(1)}, u32[]{:S(2)}, u32[]{:S(2)}) %all-to-all-start) | async-done | bytes 163872 | tf_op jit(solution)/shard_map/all_to_all | solution.py:695
  18.2 0.0 copy-done.1
  18.2 0.0 copy-done.2
  18.2 0.0 copy-done.5
  18.2 0.0 copy-done.6
  18.2 0.0 copy-done
  18.2 0.0 copy-done.3
  18.2 0.0 copy-done.4
  18.2 0.6 %first.1 = (f32[8,64,128]{2,1,0:T(8,128)S(1)}, f32[48,128]{1,0:T(8,128)S(1)}, f32[48,128]{1,0:T(8,128)S(1)}, f32[128,128]{1,0:T(8,128)S(1)}, f32[24,128]{1,0:T(8,128)S(1)}) custom-call(f32[8,40,128]{2,1,0:T(8,128)S(1)} %all-to-all-done.recv, f32[8,64,128]{2,1,0:T(8,128)S(1)} %copy-done.2, f32[8,64,128]{2,1,0:T(8,128)S(1)} %copy-done, ...), custom_call_target="tpu_custom_call" | custom-call | tf_op jit(solution)/shard_map/first/pallas_call | solution.py:675
  18.9 0.1 collective-permute-start.2
  18.9 1.6 %collective-permute-start.3 = (f32[48,128]{1,0:T(8,128)S(1)}, f32[48,128]{1,0:T(8,128)S(1)}, u32[]{:S(2)}, u32[]{:S(2)}) collective-permute-start(f32[48,128]{1,0:T(8,128)S(1)} %get-tuple-element.33), channel_id=1, source_target_pairs={{0,24},{8,16},{16,8},{24,0},{1,25},{9,17},{17,9},{25,1},{2,26},{10... | collective-permute-start | bytes 73736 | tf_op jit(solution)/shard_map/ppermute | solution.py:690
  20.6 0.0 copy-start.7
  20.6 0.7 %sums.1 = (f32[8,64,128]{2,1,0:T(8,128)S(1)}, f32[128,128]{1,0:T(8,128)S(1)}, f32[24,128]{1,0:T(8,128)S(1)}, f32[96,128]{1,0:T(8,128)S(1)}) custom-call(f32[8,64,128]{2,1,0:T(8,128)S(1)} %get-tuple-element.25.fluid1, f32[128,128]{1,0:T(8,128)S(1)} %get-tuple-element.26.turned, f32[24,128]{1,0:T(8,128)S(1)} %get-tuple-element.27.side, ...), custom_call_target="tpu_custom_call" | custom-call | tf_op jit(solution)/shard_map/sums/pallas_call | solution.py:675
  21.3 0.0 collective-permute-done.2.first1
  21.3 1.0 %collective-permute-done.3.second1 = f32[48,128]{1,0:T(8,128)S(1)} collective-permute-done((f32[48,128]{1,0:T(8,128)S(1)}, f32[48,128]{1,0:T(8,128)S(1)}, u32[]{:S(2)}, u32[]{:S(2)}) %collective-permute-start.3) | collective-permute-done | bytes 24608 | tf_op jit(solution)/shard_map/ppermute | solution.py:690
  22.3 0.0 copy-done.7
  22.3 0.3 pack.1
  22.6 10.3 %all_to_all.10.recv1 = f32[8,32,128]{2,1,0:T(8,128)S(1)} all-to-all(f32[8,32,128]{2,1,0:T(8,128)S(1)} %get-tuple-element.34), channel_id=1, replica_groups=mesh['sec'=4,'blk'=8] {'blk'}, dimensions={0} | all-to-all | bytes 262144 | tf_op jit(solution)/shard_map/all_to_all | solution.py:695
  32.8 1.6 %last.1 = (f32[8,64,128]{2,1,0:T(8,128)}, f32[32,128]{1,0:T(8,128)}) custom-call(f32[8,32,128]{2,1,0:T(8,128)S(1)} %all_to_all.10.recv1, f32[8,40,128]{2,1,0:T(8,128)S(1)} %all-to-all-done.recv, f32[112,128]{1,0:T(8,128)S(1)} %get-tuple-element.35.edge, f32[24,128]{1,0:T(8,128)S(1)} %get-tuple-element.27.side, f32[96,128]{1,0:T(8,128)S(1)} %get-tuple-element.30.metal, ...), custom_call_target="tpu_custom_call" | custom-call | tf_op jit(solution)/shard_map/last/pallas_call | solution.py:675
Async XLA Ops:
  0.6 17.5 %copy-start.1 = (f32[8,64,128]{2,1,0:T(8,128)S(1)}, f32[8,64,128]{2,1,0:T(8,128)}, u32[]{:S(2)}) copy-start(f32[8,64,128]{2,1,0:T(8,128)} %pv.7) | copy-start | bytes 786436
  0.6 17.5 %copy-start.2 = (f32[8,64,128]{2,1,0:T(8,128)S(1)}, f32[8,64,128]{2,1,0:T(8,128)}, u32[]{:S(2)}) copy-start(f32[8,64,128]{2,1,0:T(8,128)} %fluid.1) | copy-start | bytes 786436
  0.7 17.5 %copy-start.5 = (f32[1,32,128]{2,1,0:T(8,128)S(1)}, f32[1,32,128]{2,1,0:T(8,128)}, u32[]{:S(2)}) copy-start(f32[1,32,128]{2,1,0:T(8,128)} %param.12) | copy-start | bytes 49156
  0.7 17.5 %copy-start.6 = (f32[1,32,128]{2,1,0:T(8,128)S(1)}, f32[1,32,128]{2,1,0:T(8,128)}, u32[]{:S(2)}) copy-start(f32[1,32,128]{2,1,0:T(8,128)} %param.11) | copy-start | bytes 49156
  3.2 15.0 %copy-start = (f32[8,64,128]{2,1,0:T(8,128)S(1)}, f32[8,64,128]{2,1,0:T(8,128)}, u32[]{:S(2)}) copy-start(f32[8,64,128]{2,1,0:T(8,128)} %sv.7) | copy-start | bytes 786436
  3.2 15.0 %copy-start.3 = (f32[64,128]{1,0:T(8,128)S(1)}, f32[64,128]{1,0:T(8,128)}, u32[]{:S(2)}) copy-start(f32[64,128]{1,0:T(8,128)} %film.7) | copy-start | bytes 98308
  3.2 15.0 %copy-start.4 = (f32[64,128]{1,0:T(8,128)S(1)}, f32[64,128]{1,0:T(8,128)}, u32[]{:S(2)}) copy-start(f32[64,128]{1,0:T(8,128)} %get-tuple-element.22.owner) | copy-start | bytes 98308
  3.2 15.0 %all-to-all-start = ((f32[8,40,128]{2,1,0:T(8,128)}), f32[8,40,128]{2,1,0:T(8,128)S(1)}, u32[]{:S(2)}, u32[]{:S(2)}) async-start(f32[8,40,128]{2,1,0:T(8,128)} %get-tuple-element.20), calls=%async_computation | async-start | bytes 327680 | tf_op jit(solution)/shard_map/all_to_all | solution.py:695
  10.6 1.6 %collective-permute-start = (f32[48,128]{1,0:T(8,128)}, f32[48,128]{1,0:T(8,128)S(1)}, u32[]{:S(2)}, u32[]{:S(2)}) collective-permute-start(f32[48,128]{1,0:T(8,128)} %get-tuple-element.23), channel_id=1, source_target_pairs={{0,8},{8,0},{16,24},{24,16},{1,9},{9,1},{17,25},{25,17},{2,10},{10... | collective-permute-start | bytes 73736 | tf_op jit(solution)/shard_map/ppermute | solution.py:691
  10.6 3.5 %collective-permute-start.1 = (f32[48,128]{1,0:T(8,128)}, f32[48,128]{1,0:T(8,128)S(1)}, u32[]{:S(2)}, u32[]{:S(2)}) collective-permute-start(f32[48,128]{1,0:T(8,128)} %get-tuple-element.24), channel_id=1, source_target_pairs={{0,24},{8,16},{16,8},{24,0},{1,25},{9,17},{17,9},{25,1},{2,26},{10... | collective-permute-start | bytes 73736 | tf_op jit(solution)/shard_map/ppermute | solution.py:690
  18.9 2.4 %collective-permute-start.2 = (f32[48,128]{1,0:T(8,128)S(1)}, f32[48,128]{1,0:T(8,128)S(1)}, u32[]{:S(2)}, u32[]{:S(2)}) collective-permute-start(f32[48,128]{1,0:T(8,128)S(1)} %get-tuple-element.32), channel_id=1, source_target_pairs={{0,8},{8,0},{16,24},{24,16},{1,9},{9,1},{17,25},{25,17},{2,10},{10... | collective-permute-start | bytes 73736 | tf_op jit(solution)/shard_map/ppermute | solution.py:691
  18.9 3.3 %collective-permute-start.3 = (f32[48,128]{1,0:T(8,128)S(1)}, f32[48,128]{1,0:T(8,128)S(1)}, u32[]{:S(2)}, u32[]{:S(2)}) collective-permute-start(f32[48,128]{1,0:T(8,128)S(1)} %get-tuple-element.33), channel_id=1, source_target_pairs={{0,24},{8,16},{16,8},{24,0},{1,25},{9,17},{17,9},{25,1},{2,26},{10... | collective-permute-start | bytes 73736 | tf_op jit(solution)/shard_map/ppermute | solution.py:690
  20.6 1.7 %copy-start.7 = (f32[128,128]{1,0:T(8,128)S(1)}, f32[128,128]{1,0:T(8,128)}, u32[]{:S(2)}) copy-start(f32[128,128]{1,0:T(8,128)} %get-tuple-element.21.mt_old) | copy-start | bytes 196612

commit v4 on v3

--- a/solution.py
+++ b/solution.py
@@ -25,6 +25,9 @@
 R1 = 32
 ROWS = 48
 OPEN_ROOM = 56 * 1024
+PREPARE_ROOM = 1400 * 1024
+ORDER = (5, 0, 1, 2, 6, 3, 4, 7)
+PLACE = tuple(ORDER.index(peer) for peer in range(NB))
 
 
 def lanes(rows):
@@ -73,6 +76,11 @@
     return x + spread + carried
 
 
+def factored(x, low, high, left, right, below, above, toward, up, down):
+    new = (1.0 - 3.0 * SPREAD) * x + SPREAD * (right + below + above)
+    return new + toward * (left - x) + up * (low - x) + down * (high - x)
+
+
 def span(x):
     sub = subs(FZ)
     below = jnp.where(sub == 0, x, turn(x, 1, 0))
@@ -104,8 +112,9 @@
     return jnp.concatenate([x[:-8], jnp.where(subs(8) == 7, row, x[-8:])], axis=0)
 
 
-def advance(src, dst, low_row, high_row, columns, base, sv, pv, film, wall):
+def advance(src, dst, low_row, high_row, columns, base, factors, film, wall):
     lane = lanes(FP)
+    toward, up, down = factors
     for z in range(FZ):
         x = src[z]
         low = set_row(turn(x, 1, 0), low_row[z : z + 1], 0)
@@ -113,12 +122,38 @@
         edge = turn(columns, -(base + 2 * z + 1))
         left = jnp.where(lane == 0, edge, turn(x, 1))
         right = jnp.where(lane == FS - 1, edge, turn(x, -1))
-        new = stencil(
-            x, low, high, left, right, src[max(z - 1, 0)], src[min(z + 1, FZ - 1)], sv[z], pv[z]
-        )
+        below, above = src[max(z - 1, 0)], src[min(z + 1, FZ - 1)]
+        new = factored(x, low, high, left, right, below, above, toward[z], up[z], down[z])
         if z == 0:
             new = new - WALL * film * (x - wall)
         dst[z] = new
+
+
+def prepare_kernel(fluid_in, sv_in, pv_in, film, toward, up, down, partial, fluid, sv, pv, sems):
+    started = fetch([(fluid_in, fluid), (sv_in, sv), (pv_in, pv)], sems)
+    for copy in started:
+        copy.wait()
+    for z in range(FZ):
+        toward[z] = SPREAD + ADVECT * sv[z]
+        up[z] = up_factor(pv[z])
+        down[z] = down_factor(pv[z])
+    none = jnp.zeros((FZ, FS), F32)
+    columns = jnp.zeros((FP, FS), F32)
+    advance(fluid, partial, none, none, columns, 0, (toward, up, down), film[...], 0.0)
+
+
+def complete(partial, dst, low_row, high_row, columns, factors, film, wall):
+    lane = lanes(FP)
+    toward, up, down = factors
+    for z in range(FZ):
+        edge = turn(columns, -(2 * z + 1))
+        gain = jnp.where(lane == 0, toward[z], jnp.where(lane == FS - 1, SPREAD, 0.0))
+        new = partial[z] + gain * edge
+        if z == 0:
+            new = new + WALL * film * wall
+        first = new[:8] + jnp.where(subs(8) == 0, up[z, :8, :] * low_row[z : z + 1], 0.0)
+        last = new[-8:] + jnp.where(subs(8) == 7, down[z, FP - 8 :, :] * high_row[z : z + 1], 0.0)
+        dst[z] = jnp.concatenate([first, new[8:-8], last], axis=0)
 
 
 def strip_row(here, k_here, under, k_under):
@@ -193,13 +228,22 @@
     return placed(108, 104), placed(104, 100)
 
 
+def place_of(peer):
+    return sum(jnp.where(peer == k, PLACE[k], 0) for k in range(NB))
+
+
+def rows_of(recv, row):
+    return jnp.concatenate([recv[PLACE[k], row : row + 1, :] for k in range(NB)], axis=0)
+
+
 def keeps(me):
     return (me > 0).astype(F32), (me < NB - 1).astype(F32)
 
 
 def block_of(recv, me, start):
     keep_l, keep_r = keeps(me)
-    before, after = jnp.maximum(me - 1, 0), jnp.minimum(me + 1, NB - 1)
+    before = place_of(jnp.maximum(me - 1, 0))
+    after = place_of(jnp.minimum(me + 1, NB - 1))
     part = slice(start, start + 8)
     return recv[before, part, :] * keep_l, recv[after, part, :] * keep_r
 
@@ -292,16 +336,16 @@
     )
     for copy in started[6:]:
         copy.wait()
-    send_rows(first, second, 8, sv[:, FP - 2, :], sv[:, 1, :])
-    send_rows(first, second, 16, sv[:, FP - 1, :], sv[:, 0, :])
-    send_rows(first, second, 24, pv[:, FP - 2, :], pv[:, 1, :])
-    send_rows(first, second, 32, pv[:, FP - 1, :], pv[:, 0, :])
     bottom = jnp.zeros((FP, FS), F32)
     pair = (lane - 32) // 2
     for z in range(FZ):
         here = (pair == z) & (lane >= 32)
         top = jnp.where(here, turn(pv[z], 33 + 2 * z), top)
         bottom = jnp.where(here, turn(sv[z], 33 + 2 * z), bottom)
+    send_rows(first, second, 8, sv[:, FP - 2, :], sv[:, 1, :])
+    send_rows(first, second, 16, sv[:, FP - 1, :], sv[:, 0, :])
+    send_rows(first, second, 24, pv[:, FP - 2, :], pv[:, 1, :])
+    send_rows(first, second, 32, pv[:, FP - 1, :], pv[:, 0, :])
     top = jnp.where(lane // 2 == 24, turn(film[...], 49), top)
     top = jnp.where(lane == 50, named, top)
     metal = jnp.where(thin < 32, metal, bottom[:SD])
@@ -328,12 +372,12 @@
         ahead = (me + 1 == peer).astype(F32)
         behind = (me - 1 == peer).astype(F32)
         special = right_row * ahead + left_row * behind
-        out[peer, 0:8, :] = jnp.concatenate([head, special, special], axis=0)
-        out[peer, 8:16, :] = a0
-        out[peer, 16:24, :] = h
+        out[PLACE[peer], 0:8, :] = jnp.concatenate([head, special, special], axis=0)
+        out[PLACE[peer], 8:16, :] = a0
+        out[PLACE[peer], 16:24, :] = h
         same = (me == peer).astype(F32)
-        out[peer, 24:32, :] = r0 * ahead + l0 * behind + r0 * same
-        out[peer, 32:40, :] = right_part * ahead + left_part * behind + l0 * same
+        out[PLACE[peer], 24:32, :] = r0 * ahead + l0 * behind + r0 * same
+        out[PLACE[peer], 32:40, :] = right_part * ahead + left_part * behind + l0 * same
 
 
 def halo_columns(known_l, known_r, factor_l, factor_r, rows, mine_right, mine_left, walls, me):
@@ -351,22 +395,22 @@
 
 
 def first_kernel(
-    recv, fluid, sv, pv, film, solid, cond, owner, first, second,
+    recv, partial, toward, up, down, film, solid, cond, owner, first, second,
     fluid1, first_out, second_out, turned, side, tm,
 ):
     me = lax.axis_index("blk")
     lo, hi = sorted_rows(first, second)
     left, right = block_of(recv, me, 24)
     part_l, part_r = block_of(recv, me, 32)
-    wall0, under0 = recv[:, 0, :], recv[:, 1, :]
-    c0, c1 = recv[:, 2, :], recv[:, 3, :]
+    wall0, under0 = rows_of(recv, 0), rows_of(recv, 1)
+    c0, c1 = rows_of(recv, 2), rows_of(recv, 3)
     a0, h = recv[0, 8:16, :], recv[0, 16:24, :]
     for j in range(1, NB):
         a0, h = a0 + recv[j, 8:16, :], h + recv[j, 16:24, :]
     wall1 = strip_row(wall0, conduct_of(c0, wall0), under0, conduct_of(c1, under0))
     wall1 = wall1 + SOLID_STEP * (a0 - h * wall0)
 
-    mine_right, mine_left = recv[me, 24:32, :], recv[me, 32:40, :]
+    mine_right, mine_left = recv[place_of(me), 24:32, :], recv[place_of(me), 32:40, :]
     new_l, new_r = halo_columns(
         part_l, part_r, turn(part_l, 64), turn(part_r, 64), edge_rows(recv, me),
         mine_right, mine_left, wall0, me,
@@ -381,7 +425,9 @@
     turned[...] = tm[...].T
     named = owner[...]
     walls0, walls1 = pick(named, wall0), pick(named, wall1)
-    advance(fluid, fluid1, lo(0, 8), hi(0, 8), turned[:FP, :], 0, sv, pv, film[...], walls0)
+    factors = (toward, up, down)
+    columns = turned[:FP, :]
+    complete(partial, fluid1, lo(0, 8), hi(0, 8), columns, factors, film[...], walls0)
     flux = film[...] * (fluid1[0] - walls1)
     (shares,) = by_owner(named, [flux])
 
@@ -409,7 +455,7 @@
     for i in range(3):
         send_rows(first_out, second_out, 8 * i, fluid1[:, FP - 3 + i, :], fluid1[:, 2 - i, :])
     send_rows(first_out, second_out, 24, corners(FP - 1, FP - 2, 97), corners(0, 1, 96))
-    send_rows(first_out, second_out, 32, pick(recv[:, 4, :], shares), pick(recv[:, 5, :], shares))
+    send_rows(first_out, second_out, 32, pick(rows_of(recv, 4), shares), pick(rows_of(recv, 5), shares))
     send_rows(
         first_out, second_out, 40,
         jnp.concatenate([flux[FP - 2 : FP], blank], axis=0),
@@ -418,19 +464,23 @@
 
 
 def sums_kernel(
-    fluid1, turned, side, sv, pv, film, solid, cond, owner, fluid2, mt, sums, metal
+    fluid1, turned, side, toward, up, down, film, solid, cond, owner,
+    fluid2, mt, sums, metal,
 ):
     me = lax.axis_index("blk")
     lane, sub = lanes(FP), subs(FP)
     named, f = owner[...], film[...]
     wall1 = side[0:8, :]
     none = jnp.zeros((FZ, FS), F32)
-    advance(fluid1, fluid2, none, none, turned[:FP, :], 32, sv, pv, f, pick(named, wall1))
+    factors = (toward, up, down)
+    advance(fluid1, fluid2, none, none, turned[:FP, :], 32, factors, f, pick(named, wall1))
     x = fluid2[0]
     low, high = turn(x, 1, 0), turn(x, -1, 0)
     before = jnp.where(lane == 0, 0.0, turn(x, 1))
     after = jnp.where(lane == FS - 1, 0.0, turn(x, -1))
-    moved = stencil(x, low, high, before, after, x, fluid2[1], sv[0], pv[0]) - WALL * f * x
+    moved = factored(
+        x, low, high, before, after, x, fluid2[1], toward[0], up[0], down[0]
+    ) - WALL * f * x
     within = jnp.where((sub == 0) | (sub == FP - 1), 0.0, f)
     deep = jnp.where((sub < 2) | (sub >= FP - 2), 0.0, f)
     sums[0:8, :], sums[8:16, :], sums[16:24, :] = by_owner(
@@ -448,8 +498,8 @@
 
 
 def pack_kernel(
-    recv, mt_old, mt, sums, metal, side, fluid1, fluid2, sv, pv, film, owner,
-    first, second, first1, second1, out, edge,
+    recv, mt_old, mt, sums, metal, side, fluid1, fluid2, toward, up, down, film, owner,
+    first, second, first1, second1, sent, out, edge,
 ):
     me = lax.axis_index("blk")
     lane, sub = lanes(FZ), subs(FZ)
@@ -457,7 +507,6 @@
     lo, hi = sorted_rows(first, second)
     lo1, hi1 = sorted_rows(first1, second1)
     left, right = block_of(recv, me, 24)
-    pv_first, pv_last = pv[:, 0, :], pv[:, FP - 1, :]
 
     def outside(rows, rows1, inner, near_l, near_r):
         far, mid, near = rows1(0, 8), rows1(8, 16), rows1(16, 24)
@@ -474,7 +523,7 @@
         side_r = at(5, FS - 1) + at(6, FS - 1) * lane_at(right, near_r, FS - 1)
         return far, mid, near, (old_l, old_r), (side_l, side_r), (at(3, 0), at(7, FS - 1))
 
-    def finish(rows, rows1, inner, own_partial, own_pv, factor, near_lane, factor_lane, upward):
+    def finish(rows, rows1, inner, own_partial, factor, near_lane, factor_lane, upward):
         far, mid, near, old, beside, beside2 = outside(rows, rows1, inner, near_lane, near_lane)
         sv2, sv1, pv2, pv1 = rows(8, 16), rows(16, 24), rows(24, 32), rows(32, 40)
         flux = rows1(40, 42)
@@ -485,16 +534,16 @@
         through_l = turn(left, -factor_lane) * old[0]
         through_r = turn(right, FS - 1 - factor_lane) * old[1]
         own = own_partial + factor * near
-        sv_here = sv[:, 0 if upward else FP - 1, :]
-        own = own + jnp.where(lane == 0, (SPREAD + ADVECT * sv_here) * through_l, 0.0)
+        toward_here = toward[:, 0 if upward else FP - 1, :]
+        own = own + jnp.where(lane == 0, toward_here * through_l, 0.0)
         own = own + jnp.where(lane == FS - 1, SPREAD * through_r, 0.0)
         return new1, new2, own
 
     low1, low2, x_first = finish(
-        lo, lo1, fluid1[:, 0, :], fluid2[:, 0, :], pv_first, up_factor(pv_first), 0, 96, True
+        lo, lo1, fluid1[:, 0, :], fluid2[:, 0, :], up[:, 0, :], 0, 96, True
     )
     high1, high2, x_last = finish(
-        hi, hi1, fluid1[:, FP - 1, :], fluid2[:, FP - 1, :], pv_last, down_factor(pv_last),
+        hi, hi1, fluid1[:, FP - 1, :], fluid2[:, FP - 1, :], down[:, FP - 1, :],
         FP - 1, 97, False,
     )
 
@@ -535,14 +584,13 @@
     here = stack(layer[r] for r in rows)
     above = stack([x_first[1:2], fluid2[1, 1:2, :], fluid2[1, FP - 2 : FP - 1, :], x_last[1:2]])
     f4 = stack(film[r : r + 1, :] for r in rows)
-    sv4 = stack(sv[0, r : r + 1, :] for r in rows)
-    pv4 = stack(pv[0, r : r + 1, :] for r in rows)
+    factors = [stack(part[0, r : r + 1, :] for r in rows) for part in (toward, up, down)]
     before = jnp.where(lane == 0, 0.0, turn(here, 1))
     after = jnp.where(lane == FS - 1, 0.0, turn(here, -1))
     moved = f4 * (
-        stencil(
+        factored(
             here, stack(layer[r - 1] for r in rows), stack(layer[r + 1] for r in rows),
-            before, after, here, above, sv4, pv4,
+            before, after, here, above, *factors,
         )
         - WALL * f4 * here
     )
@@ -574,7 +622,7 @@
     for peer in range(NB):
         ahead = (me + 1 == peer).astype(F32)
         behind = (me - 1 == peer).astype(F32)
-        out[peer, 0:8, :] = jnp.concatenate(
+        out[PLACE[peer], 0:8, :] = jnp.concatenate(
             [
                 metal[1:2, :],
                 b3[peer : peer + 1],
@@ -586,9 +634,9 @@
             ],
             axis=0,
         )
-        out[peer, 8:16, :] = side[8:16, :]
-        out[peer, 16:24, :] = a2
-        out[peer, 24:32, :] = to_right * ahead + to_left * behind
+        out[PLACE[peer], 8:16, :] = side[8:16, :]
+        out[PLACE[peer], 16:24, :] = a2
+        out[PLACE[peer], 24:32, :] = to_right * ahead + to_left * behind
     kept = (
         low1, low2, high1, high2, r0, l0, x_first, x_last,
         lo(16, 24), lo(32, 40), hi(16, 24), hi(32, 40), lo(40, 48), hi(40, 48),
@@ -598,7 +646,8 @@
 
 
 def last_kernel(
-    recv1, recv, edge, side, metal, fluid2, sv, pv, film, cond, owner, fluid_out, solid_out,
+    recv1, recv, edge, side, metal, fluid2, toward, up, down, film, cond, owner,
+    fluid_out, solid_out,
     tm, fluid3,
 ):
     me = lax.axis_index("blk")
@@ -610,13 +659,13 @@
     left, right = block_of(recv1, me, 24)
     corner_l, corner_r = (block[5:6] for block in block_of(recv1, me, 0))
     part_l, part_r = block_of(recv, me, 32)
-    c0, c1, h = recv[:, 2, :], recv[:, 3, :], side[16:24, :]
+    c0, c1, h = rows_of(recv, 2), rows_of(recv, 3), side[16:24, :]
     tail, wall2, a2 = recv1[0, 0:8, :], recv1[0, 8:16, :], recv1[0, 16:24, :]
     for j in range(1, NB):
         tail = tail + recv1[j, 0:8, :]
         wall2 = wall2 + recv1[j, 8:16, :]
         a2 = a2 + recv1[j, 16:24, :]
-    under2 = recv1[:, 0, :]
+    under2 = rows_of(recv1, 0)
     wall3 = strip_row(wall2, conduct_of(c0, wall2), under2, conduct_of(c1, under2))
     wall3 = wall3 + SOLID_STEP * (a2 - h * wall2)
     inflow3 = tail[1:2] + WALL * tail[2:3] * row_of(wall2, me) - row_of(h * wall3, me)
@@ -649,8 +698,10 @@
         set_row(set_row(fluid2[z], x_first[z : z + 1], 0), x_last[z : z + 1], 1)
         for z in range(FZ)
     ]
-    advance(source, fluid3, low1, high1, columns, 0, sv, pv, f, pick(named, wall2))
-    advance(fluid3, fluid_out, new_low, new_high, columns, 32, sv, pv, f, pick(named, wall3))
+    factors = (toward, up, down)
+    advance(source, fluid3, low1, high1, columns, 0, factors, f, pick(named, wall2))
+    walls3 = pick(named, wall3)
+    advance(fluid3, fluid_out, new_low, new_high, columns, 32, factors, f, walls3)
 
     keep_l, keep_r = keeps(me)
     keep = jnp.where(lanes(SD) >= FS // 2, keep_l, keep_r)
@@ -692,7 +743,9 @@
 
 
 def swap(message):
-    return lax.all_to_all(message, "blk", split_axis=0, concat_axis=0, tiled=True)
+    return lax.all_to_all(
+        message, "blk", split_axis=0, concat_axis=0, tiled=True, axis_index_groups=[list(ORDER)]
+    )
 
 
 def two_exchanges(fluid, sv, pv, film, solid, cond, face_owner):
@@ -712,26 +765,35 @@
     )
     first, second = both_ways(first, second)
     recv = swap(message)
-    fluid1, first1, second1, turned, side = call(
+    *factors, partial = call(
+        prepare_kernel,
+        (field,) * 4,
+        (fluid, sv, pv, film),
+        "prepare",
+        [pltpu.VMEM((FZ, FP, FS), F32)] * 3 + [pltpu.SemaphoreType.DMA((3,))],
+        far=3,
+        limit=GRANT - PREPARE_ROOM,
+    )
+    fluid1, first_sent, second_sent, turned, side = call(
         first_kernel,
         (field, rows, rows, shape(FS, FS), shape(24, FS)),
-        (recv, fluid, sv, pv, film, solid, cond, owner, first, second),
+        (recv, partial, *factors, film, solid, cond, owner, first, second),
         "first",
         [pltpu.VMEM((FS, FS), F32)],
     )
-    first1, second1 = both_ways(first1, second1)
+    first1, second1 = both_ways(first_sent, second_sent)
     fluid2, mt2, sums, metal = call(
         sums_kernel,
         (field, shape(FS, FS), shape(24, FS), shape(3 * SD, FS)),
-        (fluid1, turned, side, sv, pv, film, solid, cond, owner),
+        (fluid1, turned, side, *factors, film, solid, cond, owner),
         "sums",
     )
     message, edge = call(
         pack_kernel,
         (shape(NB, R1, FS), shape(14 * 8, FS)),
         (
-            recv, mt, mt2, sums, metal, side, fluid1, fluid2, sv, pv, film, owner,
-            first, second, first1, second1,
+            recv, mt, mt2, sums, metal, side, fluid1, fluid2, *factors, film, owner,
+            first, second, first1, second1, first_sent,
         ),
         "pack",
     )
@@ -739,7 +801,7 @@
     fluid, solid = call(
         last_kernel,
         (field, shape(SD, FS)),
-        (recv1, recv, edge, side, metal, fluid2, sv, pv, film, cond, owner),
+        (recv1, recv, edge, side, metal, fluid2, *factors, film, cond, owner),
         "last",
         [pltpu.VMEM((FS, FS), F32), pltpu.VMEM((FZ, FP, FS), F32)],
     )

time: 34.7 us -> 31.2 us (0.90)
  waiting for transfers between devices: 6.9 us -> 2.42 us
  blocking collectives: 10.3 us -> 9.22 us
  starting transfers between devices: 10.7 us -> 11.7 us
  Pallas kernels: 5.75 us -> 6.74 us
    all_to_all x1, waiting for transfers between devices: 4.03 us -> 0.97 us  [swap(): lax.all_to_all(message, 'blk', split_axis=0, concat_axis=0, tiled=True, a...]
    ppermute x2, waiting for transfers between devices: 2.86 us -> 1.44 us  [both_ways(): second = lax.ppermute(second, 'sec', far)]
    all_to_all x1, blocking collectives: 10.3 us -> 9.22 us  [swap(): lax.all_to_all(message, 'blk', split_axis=0, concat_axis=0, tiled=True, a...]
    all_to_all x1, starting transfers between devices: 7.4 us -> 8.39 us  [swap(): lax.all_to_all(message, 'blk', split_axis=0, concat_axis=0, tiled=True, a...]
    pallas_call x5 -> x6, Pallas kernels: 5.75 us -> 6.74 us  [call(): pl.pallas_call(kernel, out_shape=outs, in_specs=[HBM] * far + [VMEM] * (l...]
    ppermute x2, starting transfers between devices: 0.07 us -> 0.73 us  [both_ways(): return (lax.ppermute(first, 'sec', near), second)]
    ppermute x2, starting transfers between devices: 3.26 us -> 2.6 us  [both_ways(): second = lax.ppermute(second, 'sec', far)]
  transfers between devices with their start and end apart: 5 -> 5, of which waited for: 3 -> 3; matrix products, arithmetic and copies ran while one was open for 0% -> 0% of each run, Pallas kernels for 2% -> 6%
where the time goes in v4:
time: 31.2 us; the launch traced here: 30.9 us
  starting transfers between devices  11.7 us (38%)
  blocking collectives  9.22 us (30%)
  Pallas kernels  6.74 us (22%)
  waiting for transfers between devices  2.42 us (8%)
  between operations  0.72 us (2%)
    all_to_all x1, blocking collectives, swap(): lax.all_to_all(message, 'blk', split_axis=0, concat_axis=0, tiled=True, a...  9.22 us
    all_to_all x1, starting transfers between devices, swap(): lax.all_to_all(message, 'blk', split_axis=0, concat_axis=0, tiled=True, a...  8.39 us
    pallas_call x6, Pallas kernels, call(): pl.pallas_call(kernel, out_shape=outs, in_specs=[HBM] * far + [VMEM] * (l...  6.74 us
    ppermute x2, starting transfers between devices, both_ways(): second = lax.ppermute(second, 'sec', far)  2.6 us
    ppermute x2, waiting for transfers between devices, both_ways(): second = lax.ppermute(second, 'sec', far)  1.44 us
    all_to_all x1, waiting for transfers between devices, swap(): lax.all_to_all(message, 'blk', split_axis=0, concat_axis=0, tiled=True, a...  0.97 us
    ppermute x2, starting transfers between devices, both_ways(): return (lax.ppermute(first, 'sec', near), second)  0.73 us
  transfers between devices with their start and end apart: 5, of which 3 were waited for; matrix products, arithmetic and copies ran while one was open for 0% of the time, Pallas kernels for 6%

profile of v4, /device:TPU:0, one launch (start us, length us, event | category | flops | bytes accessed | tf_op | source)
XLA Modules:
  0.0 30.9 jit_solution(337998468502644086)
XLA Ops:
  0.6 2.4 %open.1 = (f32[8,40,128]{2,1,0:T(8,128)}, f32[48,128]{1,0:T(8,128)}, f32[48,128]{1,0:T(8,128)}, f32[128,128]{1,0:T(8,128)}, f32[64,128]{1,0:T(8,128)}) custom-call(f32[8,64,128]{2,1,0:T(8,128)} %fluid_in.3, f32[8,64,128]{2,1,0:T(8,128)} %sv_in.3, f32[8,64,128]{2,1,0:T(8,128)} %pv_in.3, f32[64,128]{1,0:T(8,128)} %film.9, f32[32,128]{1,0:T(8,128)} %bitcast.8, ...), custom_call_target="tpu_custom_call" | custom-call | tf_op jit(solution)/shard_map/open/pallas_call | solution.py:726
  3.1 0.0 copy-start.1
  3.1 0.0 copy-start.6
  3.1 0.0 copy-start
  3.1 8.4 %all-to-all-start = ((f32[8,40,128]{2,1,0:T(8,128)}), f32[8,40,128]{2,1,0:T(8,128)S(1)}, u32[]{:S(2)}, u32[]{:S(2)}) async-start(f32[8,40,128]{2,1,0:T(8,128)} %get-tuple-element.24), calls=%async_computation | async-start | bytes 327680 | tf_op jit(solution)/shard_map/all_to_all | solution.py:746
  11.5 0.0 collective-permute-start
  11.5 0.0 copy-done.6
  11.5 0.0 copy-start.2
  11.5 1.6 %collective-permute-start.1 = (f32[48,128]{1,0:T(8,128)S(1)}, f32[48,128]{1,0:T(8,128)S(1)}, u32[]{:S(2)}, u32[]{:S(2)}) collective-permute-start(f32[48,128]{1,0:T(8,128)S(1)} %copy-done.6), channel_id=1, source_target_pairs={{0,24},{8,16},{16,8},{24,0},{1,25},{9,17},{17,9},{25,1},{2,26},{10... | collective-permute-start | bytes 73736 | tf_op jit(solution)/shard_map/ppermute | solution.py:741
  13.2 0.0 copy-done.1
  13.2 0.0 copy-done
  13.2 0.0 copy-start.3
  13.2 0.0 copy-start.4
  13.2 1.3 %prepare.1 = (f32[8,64,128]{2,1,0:T(8,128)S(1)}, f32[8,64,128]{2,1,0:T(8,128)S(1)}, f32[8,64,128]{2,1,0:T(8,128)S(1)}, f32[8,64,128]{2,1,0:T(8,128)S(1)}) custom-call(f32[8,64,128]{2,1,0:T(8,128)S(1)} %copy-done.1, f32[8,64,128]{2,1,0:T(8,128)} %sv_in.3, f32[8,64,128]{2,1,0:T(8,128)} %pv_in.3, f32[64,128]{1,0:T(8,128)S(1)} %copy-done), custom_call_target="tpu_custom_call" | custom-call | tf_op jit(solution)/shard_map/prepare/pallas_call | solution.py:726
  14.5 0.0 collective-permute-done.first
  14.5 0.3 collective-permute-done.1.second
  14.8 1.0 %all-to-all-done.recv = f32[8,40,128]{2,1,0:T(8,128)S(1)} async-done(((f32[8,40,128]{2,1,0:T(8,128)}), f32[8,40,128]{2,1,0:T(8,128)S(1)}, u32[]{:S(2)}, u32[]{:S(2)}) %all-to-all-start) | async-done | bytes 163872 | tf_op jit(solution)/shard_map/all_to_all | solution.py:746
  15.8 0.0 copy-done.2
  15.8 0.0 copy-done.3
  15.8 0.0 copy-done.4
  15.8 0.5 %first.1 = (f32[8,64,128]{2,1,0:T(8,128)S(1)}, f32[48,128]{1,0:T(8,128)S(1)}, f32[48,128]{1,0:T(8,128)S(1)}, f32[128,128]{1,0:T(8,128)S(1)}, f32[24,128]{1,0:T(8,128)S(1)}) custom-call(f32[8,40,128]{2,1,0:T(8,128)S(1)} %all-to-all-done.recv, f32[8,64,128]{2,1,0:T(8,128)S(1)} %get-tuple-element.26.partial, f32[8,64,128]{2,1,0:T(8,128)S(1)} %get-tuple-element.27.toward, ...), custom_call_target="tpu_custom_call" | custom-call | tf_op jit(solution)/shard_map/first/pallas_call | solution.py:726
  16.3 1.0 %collective-permute-start.3 = (f32[48,128]{1,0:T(8,128)S(1)}, f32[48,128]{1,0:T(8,128)S(1)}, u32[]{:S(2)}, u32[]{:S(2)}) collective-permute-start(f32[48,128]{1,0:T(8,128)S(1)} %get-tuple-element.41), channel_id=1, source_target_pairs={{0,24},{8,16},{16,8},{24,0},{1,25},{9,17},{17,9},{25,1},{2,26},{10... | collective-permute-start | bytes 73736 | tf_op jit(solution)/shard_map/ppermute | solution.py:741
  17.3 0.7 %collective-permute-start.2 = (f32[48,128]{1,0:T(8,128)S(1)}, f32[48,128]{1,0:T(8,128)S(1)}, u32[]{:S(2)}, u32[]{:S(2)}) collective-permute-start(f32[48,128]{1,0:T(8,128)S(1)} %get-tuple-element.40.sent), channel_id=1, source_target_pairs={{0,8},{8,0},{16,24},{24,16},{1,9},{9,1},{17,25},{25,17},{2,10},{10... | collective-permute-start | bytes 73736 | tf_op jit(solution)/shard_map/ppermute | solution.py:742
  18.0 0.0 copy-start.5
  18.0 0.6 %sums.1 = (f32[8,64,128]{2,1,0:T(8,128)S(1)}, f32[128,128]{1,0:T(8,128)S(1)}, f32[24,128]{1,0:T(8,128)S(1)}, f32[96,128]{1,0:T(8,128)S(1)}) custom-call(f32[8,64,128]{2,1,0:T(8,128)S(1)} %get-tuple-element.33.fluid1, f32[128,128]{1,0:T(8,128)S(1)} %get-tuple-element.34.turned, f32[24,128]{1,0:T(8,128)S(1)} %get-tuple-element.35.side, ...), custom_call_target="tpu_custom_call" | custom-call | tf_op jit(solution)/shard_map/sums/pallas_call | solution.py:726
  18.6 1.1 %collective-permute-done.3.second1 = f32[48,128]{1,0:T(8,128)S(1)} collective-permute-done((f32[48,128]{1,0:T(8,128)S(1)}, f32[48,128]{1,0:T(8,128)S(1)}, u32[]{:S(2)}, u32[]{:S(2)}) %collective-permute-start.3) | collective-permute-done | bytes 24608 | tf_op jit(solution)/shard_map/ppermute | solution.py:741
  19.8 0.0 collective-permute-done.2.first1
  19.8 0.0 copy-done.5
  19.8 0.3 %pack.1 = (f32[8,32,128]{2,1,0:T(8,128)S(1)}, f32[112,128]{1,0:T(8,128)S(1)}) custom-call(f32[8,40,128]{2,1,0:T(8,128)S(1)} %all-to-all-done.recv, f32[128,128]{1,0:T(8,128)S(1)} %copy-done.5, f32[128,128]{1,0:T(8,128)S(1)} %get-tuple-element.36.mt, f32[24,128]{1,0:T(8,128)S(1)} %get-tuple-element.37.sums, f32[96,128]{1,0:T(8,128)S(1)} %get-tuple-element.38.metal, ...), custom_call_target="tpu_custom_call" | custom-call | tf_op jit(solution)/shard_map/pack/pallas_call | solution.py:726
  20.1 9.2 %all_to_all.10.recv1 = f32[8,32,128]{2,1,0:T(8,128)S(1)} all-to-all(f32[8,32,128]{2,1,0:T(8,128)S(1)} %get-tuple-element.42), channel_id=1, replica_groups={{5,0,1,2,6,3,4,7},{13,8,9,10,14,11,12,15},{21,16,17,18,22,19,20,23},{29..., dimensions={0} | all-to-all | bytes 262144 | tf_op jit(solution)/shard_map/all_to_all | solution.py:746
  29.4 1.5 %last.1 = (f32[8,64,128]{2,1,0:T(8,128)}, f32[32,128]{1,0:T(8,128)}) custom-call(f32[8,32,128]{2,1,0:T(8,128)S(1)} %all_to_all.10.recv1, f32[8,40,128]{2,1,0:T(8,128)S(1)} %all-to-all-done.recv, f32[112,128]{1,0:T(8,128)S(1)} %get-tuple-element.43.edge, f32[24,128]{1,0:T(8,128)S(1)} %get-tuple-element.35.side, f32[96,128]{1,0:T(8,128)S(1)} %get-tuple-element.38.metal, ...), custom_call_target="tpu_custom_call" | custom-call | tf_op jit(solution)/shard_map/last/pallas_call | solution.py:726
Async XLA Ops:
  3.1 10.1 %copy-start.1 = (f32[8,64,128]{2,1,0:T(8,128)S(1)}, f32[8,64,128]{2,1,0:T(8,128)}, u32[]{:S(2)}) copy-start(f32[8,64,128]{2,1,0:T(8,128)} %fluid_in.3) | copy-start | bytes 786436
  3.1 8.4 %copy-start.6 = (f32[48,128]{1,0:T(8,128)S(1)}, f32[48,128]{1,0:T(8,128)}, u32[]{:S(2)}) copy-start(f32[48,128]{1,0:T(8,128)} %get-tuple-element.32) | copy-start | bytes 73732
  3.1 10.1 %copy-start = (f32[64,128]{1,0:T(8,128)S(1)}, f32[64,128]{1,0:T(8,128)}, u32[]{:S(2)}) copy-start(f32[64,128]{1,0:T(8,128)} %film.9) | copy-start | bytes 98308
  3.1 12.7 %all-to-all-start = ((f32[8,40,128]{2,1,0:T(8,128)}), f32[8,40,128]{2,1,0:T(8,128)S(1)}, u32[]{:S(2)}, u32[]{:S(2)}) async-start(f32[8,40,128]{2,1,0:T(8,128)} %get-tuple-element.24), calls=%async_computation | async-start | bytes 327680 | tf_op jit(solution)/shard_map/all_to_all | solution.py:746
  11.5 3.0 %collective-permute-start = (f32[48,128]{1,0:T(8,128)}, f32[48,128]{1,0:T(8,128)S(1)}, u32[]{:S(2)}, u32[]{:S(2)}) collective-permute-start(f32[48,128]{1,0:T(8,128)} %get-tuple-element.31), channel_id=1, source_target_pairs={{0,8},{8,0},{16,24},{24,16},{1,9},{9,1},{17,25},{25,17},{2,10},{10... | collective-permute-start | bytes 73736 | tf_op jit(solution)/shard_map/ppermute | solution.py:742
  11.5 4.3 %copy-start.2 = (f32[64,128]{1,0:T(8,128)S(1)}, f32[64,128]{1,0:T(8,128)}, u32[]{:S(2)}) copy-start(f32[64,128]{1,0:T(8,128)} %get-tuple-element.30.owner) | copy-start | bytes 98308
  11.5 3.3 %collective-permute-start.1 = (f32[48,128]{1,0:T(8,128)S(1)}, f32[48,128]{1,0:T(8,128)S(1)}, u32[]{:S(2)}, u32[]{:S(2)}) collective-permute-start(f32[48,128]{1,0:T(8,128)S(1)} %copy-done.6), channel_id=1, source_target_pairs={{0,24},{8,16},{16,8},{24,0},{1,25},{9,17},{17,9},{25,1},{2,26},{10... | collective-permute-start | bytes 73736 | tf_op jit(solution)/shard_map/ppermute | solution.py:741
  13.2 2.7 %copy-start.3 = (f32[1,32,128]{2,1,0:T(8,128)S(1)}, f32[1,32,128]{2,1,0:T(8,128)}, u32[]{:S(2)}) copy-start(f32[1,32,128]{2,1,0:T(8,128)} %param.12) | copy-start | bytes 49156
  13.2 2.7 %copy-start.4 = (f32[1,32,128]{2,1,0:T(8,128)S(1)}, f32[1,32,128]{2,1,0:T(8,128)}, u32[]{:S(2)}) copy-start(f32[1,32,128]{2,1,0:T(8,128)} %param.11) | copy-start | bytes 49156
  16.3 3.5 %collective-permute-start.3 = (f32[48,128]{1,0:T(8,128)S(1)}, f32[48,128]{1,0:T(8,128)S(1)}, u32[]{:S(2)}, u32[]{:S(2)}) collective-permute-start(f32[48,128]{1,0:T(8,128)S(1)} %get-tuple-element.41), channel_id=1, source_target_pairs={{0,24},{8,16},{16,8},{24,0},{1,25},{9,17},{17,9},{25,1},{2,26},{10... | collective-permute-start | bytes 73736 | tf_op jit(solution)/shard_map/ppermute | solution.py:741
  17.3 2.5 %collective-permute-start.2 = (f32[48,128]{1,0:T(8,128)S(1)}, f32[48,128]{1,0:T(8,128)S(1)}, u32[]{:S(2)}, u32[]{:S(2)}) collective-permute-start(f32[48,128]{1,0:T(8,128)S(1)} %get-tuple-element.40.sent), channel_id=1, source_target_pairs={{0,8},{8,0},{16,24},{24,16},{1,9},{9,1},{17,25},{25,17},{2,10},{10... | collective-permute-start | bytes 73736 | tf_op jit(solution)/shard_map/ppermute | solution.py:742
  18.0 1.8 %copy-start.5 = (f32[128,128]{1,0:T(8,128)S(1)}, f32[128,128]{1,0:T(8,128)}, u32[]{:S(2)}) copy-start(f32[128,128]{1,0:T(8,128)} %get-tuple-element.25.mt_old) | copy-start | bytes 196612

commit v5 on v4

--- a/solution.py
+++ b/solution.py
@@ -26,8 +26,8 @@
 ROWS = 48
 OPEN_ROOM = 56 * 1024
 PREPARE_ROOM = 1400 * 1024
-ORDER = (5, 0, 1, 2, 6, 3, 4, 7)
-PLACE = tuple(ORDER.index(peer) for peer in range(NB))
+ORDER0 = (5, 0, 1, 2, 6, 3, 4, 7)
+ORDER1 = (5, 2, 6, 4, 1, 0, 7, 3)
 
 
 def lanes(rows):
@@ -228,22 +228,22 @@
     return placed(108, 104), placed(104, 100)
 
 
-def place_of(peer):
-    return sum(jnp.where(peer == k, PLACE[k], 0) for k in range(NB))
-
-
-def rows_of(recv, row):
-    return jnp.concatenate([recv[PLACE[k], row : row + 1, :] for k in range(NB)], axis=0)
+def place_of(peer, order):
+    return sum(jnp.where(peer == k, order.index(k), 0) for k in range(NB))
+
+
+def rows_of(recv, row, order):
+    return jnp.concatenate([recv[order.index(k), row : row + 1, :] for k in range(NB)], axis=0)
 
 
 def keeps(me):
     return (me > 0).astype(F32), (me < NB - 1).astype(F32)
 
 
-def block_of(recv, me, start):
+def block_of(recv, me, start, order=ORDER0):
     keep_l, keep_r = keeps(me)
-    before = place_of(jnp.maximum(me - 1, 0))
-    after = place_of(jnp.minimum(me + 1, NB - 1))
+    before = place_of(jnp.maximum(me - 1, 0), order)
+    after = place_of(jnp.minimum(me + 1, NB - 1), order)
     part = slice(start, start + 8)
     return recv[before, part, :] * keep_l, recv[after, part, :] * keep_r
 
@@ -305,9 +305,7 @@
     me = lax.axis_index("blk")
     half = FZ // 2
     copies = [(owner, ids), (film_in, film), (solid_in, solid), (cond_in, cond)]
-    for src, dst in ((fluid_in, fluid), (pv_in, pv), (sv_in, sv)):
-        for part in range(2):
-            copies.append((src.at[pl.ds(half * part, half)], dst.at[pl.ds(half * part, half)]))
+    copies += [(fluid_in, fluid), (pv_in, pv), (sv_in, sv)]
     started = fetch(copies, sems)
     lane = lanes(FP)
     for copy in started[:4]:
@@ -325,7 +323,6 @@
         metal = jnp.where(thin == 4 * k + 18, turn(c, 3 * k + 18), metal)
     started[4].wait()
     a0, h = by_owner(named, [film[...] * fluid[0], film[...]])
-    started[5].wait()
     top = gather_columns(fluid, lane)
     send_rows(first, second, 0, fluid[:, FP - 1, :], fluid[:, 0, :])
     blank = jnp.zeros((7, FS), F32)
@@ -334,7 +331,7 @@
         jnp.concatenate([film[FP - 1 : FP, :], blank], axis=0),
         jnp.concatenate([film[0:1, :], blank], axis=0),
     )
-    for copy in started[6:]:
+    for copy in started[5:]:
         copy.wait()
     bottom = jnp.zeros((FP, FS), F32)
     pair = (lane - 32) // 2
@@ -372,12 +369,12 @@
         ahead = (me + 1 == peer).astype(F32)
         behind = (me - 1 == peer).astype(F32)
         special = right_row * ahead + left_row * behind
-        out[PLACE[peer], 0:8, :] = jnp.concatenate([head, special, special], axis=0)
-        out[PLACE[peer], 8:16, :] = a0
-        out[PLACE[peer], 16:24, :] = h
+        out[ORDER0.index(peer), 0:8, :] = jnp.concatenate([head, special, special], axis=0)
+        out[ORDER0.index(peer), 8:16, :] = a0
+        out[ORDER0.index(peer), 16:24, :] = h
         same = (me == peer).astype(F32)
-        out[PLACE[peer], 24:32, :] = r0 * ahead + l0 * behind + r0 * same
-        out[PLACE[peer], 32:40, :] = right_part * ahead + left_part * behind + l0 * same
+        out[ORDER0.index(peer), 24:32, :] = r0 * ahead + l0 * behind + r0 * same
+        out[ORDER0.index(peer), 32:40, :] = right_part * ahead + left_part * behind + l0 * same
 
 
 def halo_columns(known_l, known_r, factor_l, factor_r, rows, mine_right, mine_left, walls, me):
@@ -402,15 +399,16 @@
     lo, hi = sorted_rows(first, second)
     left, right = block_of(recv, me, 24)
     part_l, part_r = block_of(recv, me, 32)
-    wall0, under0 = rows_of(recv, 0), rows_of(recv, 1)
-    c0, c1 = rows_of(recv, 2), rows_of(recv, 3)
+    wall0, under0 = rows_of(recv, 0, ORDER0), rows_of(recv, 1, ORDER0)
+    c0, c1 = rows_of(recv, 2, ORDER0), rows_of(recv, 3, ORDER0)
     a0, h = recv[0, 8:16, :], recv[0, 16:24, :]
     for j in range(1, NB):
         a0, h = a0 + recv[j, 8:16, :], h + recv[j, 16:24, :]
     wall1 = strip_row(wall0, conduct_of(c0, wall0), under0, conduct_of(c1, under0))
     wall1 = wall1 + SOLID_STEP * (a0 - h * wall0)
 
-    mine_right, mine_left = recv[place_of(me), 24:32, :], recv[place_of(me), 32:40, :]
+    here = place_of(me, ORDER0)
+    mine_right, mine_left = recv[here, 24:32, :], recv[here, 32:40, :]
     new_l, new_r = halo_columns(
         part_l, part_r, turn(part_l, 64), turn(part_r, 64), edge_rows(recv, me),
         mine_right, mine_left, wall0, me,
@@ -455,7 +453,8 @@
     for i in range(3):
         send_rows(first_out, second_out, 8 * i, fluid1[:, FP - 3 + i, :], fluid1[:, 2 - i, :])
     send_rows(first_out, second_out, 24, corners(FP - 1, FP - 2, 97), corners(0, 1, 96))
-    send_rows(first_out, second_out, 32, pick(rows_of(recv, 4), shares), pick(rows_of(recv, 5), shares))
+    ids_last, ids_first = rows_of(recv, 4, ORDER0), rows_of(recv, 5, ORDER0)
+    send_rows(first_out, second_out, 32, pick(ids_last, shares), pick(ids_first, shares))
     send_rows(
         first_out, second_out, 40,
         jnp.concatenate([flux[FP - 2 : FP], blank], axis=0),
@@ -622,7 +621,7 @@
     for peer in range(NB):
         ahead = (me + 1 == peer).astype(F32)
         behind = (me - 1 == peer).astype(F32)
-        out[PLACE[peer], 0:8, :] = jnp.concatenate(
+        out[ORDER1.index(peer), 0:8, :] = jnp.concatenate(
             [
                 metal[1:2, :],
                 b3[peer : peer + 1],
@@ -634,9 +633,9 @@
             ],
             axis=0,
         )
-        out[PLACE[peer], 8:16, :] = side[8:16, :]
-        out[PLACE[peer], 16:24, :] = a2
-        out[PLACE[peer], 24:32, :] = to_right * ahead + to_left * behind
+        out[ORDER1.index(peer), 8:16, :] = side[8:16, :]
+        out[ORDER1.index(peer), 16:24, :] = a2
+        out[ORDER1.index(peer), 24:32, :] = to_right * ahead + to_left * behind
     kept = (
         low1, low2, high1, high2, r0, l0, x_first, x_last,
         lo(16, 24), lo(32, 40), hi(16, 24), hi(32, 40), lo(40, 48), hi(40, 48),
@@ -656,16 +655,16 @@
         low1, low2, high1, high2, mine_right, mine_left, x_first, x_last,
         sv_lo, pv_lo, sv_hi, pv_hi, film_lo, film_hi,
     ) = [edge[8 * i : 8 * i + 8, :] for i in range(14)]
-    left, right = block_of(recv1, me, 24)
-    corner_l, corner_r = (block[5:6] for block in block_of(recv1, me, 0))
+    left, right = block_of(recv1, me, 24, ORDER1)
+    corner_l, corner_r = (block[5:6] for block in block_of(recv1, me, 0, ORDER1))
     part_l, part_r = block_of(recv, me, 32)
-    c0, c1, h = rows_of(recv, 2), rows_of(recv, 3), side[16:24, :]
+    c0, c1, h = rows_of(recv, 2, ORDER0), rows_of(recv, 3, ORDER0), side[16:24, :]
     tail, wall2, a2 = recv1[0, 0:8, :], recv1[0, 8:16, :], recv1[0, 16:24, :]
     for j in range(1, NB):
         tail = tail + recv1[j, 0:8, :]
         wall2 = wall2 + recv1[j, 8:16, :]
         a2 = a2 + recv1[j, 16:24, :]
-    under2 = rows_of(recv1, 0)
+    under2 = rows_of(recv1, 0, ORDER1)
     wall3 = strip_row(wall2, conduct_of(c0, wall2), under2, conduct_of(c1, under2))
     wall3 = wall3 + SOLID_STEP * (a2 - h * wall2)
     inflow3 = tail[1:2] + WALL * tail[2:3] * row_of(wall2, me) - row_of(h * wall3, me)
@@ -742,9 +741,9 @@
     return lax.ppermute(first, "sec", near), second
 
 
-def swap(message):
+def swap(message, order):
     return lax.all_to_all(
-        message, "blk", split_axis=0, concat_axis=0, tiled=True, axis_index_groups=[list(ORDER)]
+        message, "blk", split_axis=0, concat_axis=0, tiled=True, axis_index_groups=[list(order)]
     )
 
 
@@ -764,7 +763,7 @@
         limit=GRANT - OPEN_ROOM,
     )
     first, second = both_ways(first, second)
-    recv = swap(message)
+    recv = swap(message, ORDER0)
     *factors, partial = call(
         prepare_kernel,
         (field,) * 4,
@@ -797,7 +796,7 @@
         ),
         "pack",
     )
-    recv1 = swap(message)
+    recv1 = swap(message, ORDER1)
     fluid, solid = call(
         last_kernel,
         (field, shape(SD, FS)),

time: 31.2 us -> 30.7 us (0.984)
  blocking collectives: 9.22 us -> 8.86 us
    all_to_all x1, blocking collectives: 9.22 us -> 8.86 us  [swap(): lax.all_to_all(message, 'blk', split_axis=0, concat_axis=0, tiled=True, a...]
  transfers between devices with their start and end apart: 5 -> 5, of which waited for: 3 -> 3; matrix products, arithmetic and copies ran while one was open for 0% -> 0% of each run, Pallas kernels for 6% -> 7%
where the time goes in v5:
time: 30.7 us; the launch traced here: 30.4 us
  starting transfers between devices  11.7 us (38%)
  blocking collectives  8.86 us (29%)
  Pallas kernels  6.66 us (22%)
  waiting for transfers between devices  2.42 us (8%)
  between operations  0.72 us (2%)
    all_to_all x1, blocking collectives, swap(): lax.all_to_all(message, 'blk', split_axis=0, concat_axis=0, tiled=True, a...  8.86 us
    all_to_all x1, starting transfers between devices, swap(): lax.all_to_all(message, 'blk', split_axis=0, concat_axis=0, tiled=True, a...  8.39 us
    pallas_call x6, Pallas kernels, call(): pl.pallas_call(kernel, out_shape=outs, in_specs=[HBM] * far + [VMEM] * (l...  6.66 us
    ppermute x2, starting transfers between devices, both_ways(): second = lax.ppermute(second, 'sec', far)  2.6 us
    ppermute x2, waiting for transfers between devices, both_ways(): second = lax.ppermute(second, 'sec', far)  1.44 us
    all_to_all x1, waiting for transfers between devices, swap(): lax.all_to_all(message, 'blk', split_axis=0, concat_axis=0, tiled=True, a...  0.97 us
    ppermute x2, starting transfers between devices, both_ways(): return (lax.ppermute(first, 'sec', near), second)  0.73 us
  transfers between devices with their start and end apart: 5, of which 3 were waited for; matrix products, arithmetic and copies ran while one was open for 0% of the time, Pallas kernels for 7%

profile of v5, /device:TPU:0, one launch (start us, length us, event | category | flops | bytes accessed | tf_op | source)
XLA Modules:
  0.0 30.4 jit_solution(307494370749852648)
XLA Ops:
  0.6 2.4 %open.1 = (f32[8,40,128]{2,1,0:T(8,128)}, f32[48,128]{1,0:T(8,128)}, f32[48,128]{1,0:T(8,128)}, f32[128,128]{1,0:T(8,128)}, f32[64,128]{1,0:T(8,128)}) custom-call(f32[8,64,128]{2,1,0:T(8,128)} %fluid_in.3, f32[8,64,128]{2,1,0:T(8,128)} %sv_in.3, f32[8,64,128]{2,1,0:T(8,128)} %pv_in.3, f32[64,128]{1,0:T(8,128)} %film.9, f32[32,128]{1,0:T(8,128)} %bitcast.8, ...), custom_call_target="tpu_custom_call" | custom-call | tf_op jit(solution)/shard_map/open/pallas_call | solution.py:725
  3.0 0.0 copy-start.1
  3.0 0.0 copy-start.6
  3.0 0.0 copy-start
  3.0 8.4 %all-to-all-start = ((f32[8,40,128]{2,1,0:T(8,128)}), f32[8,40,128]{2,1,0:T(8,128)S(1)}, u32[]{:S(2)}, u32[]{:S(2)}) async-start(f32[8,40,128]{2,1,0:T(8,128)} %get-tuple-element.24), calls=%async_computation | async-start | bytes 327680 | tf_op jit(solution)/shard_map/all_to_all | solution.py:745
  11.4 0.0 collective-permute-start
  11.4 0.0 copy-done.6
  11.4 0.0 copy-start.2
  11.4 1.6 %collective-permute-start.1 = (f32[48,128]{1,0:T(8,128)S(1)}, f32[48,128]{1,0:T(8,128)S(1)}, u32[]{:S(2)}, u32[]{:S(2)}) collective-permute-start(f32[48,128]{1,0:T(8,128)S(1)} %copy-done.6), channel_id=1, source_target_pairs={{0,24},{8,16},{16,8},{24,0},{1,25},{9,17},{17,9},{25,1},{2,26},{10... | collective-permute-start | bytes 73736 | tf_op jit(solution)/shard_map/ppermute | solution.py:740
  13.1 0.0 copy-done.1
  13.1 0.0 copy-done
  13.1 0.0 copy-start.3
  13.1 0.0 copy-start.4
  13.1 1.3 %prepare.1 = (f32[8,64,128]{2,1,0:T(8,128)S(1)}, f32[8,64,128]{2,1,0:T(8,128)S(1)}, f32[8,64,128]{2,1,0:T(8,128)S(1)}, f32[8,64,128]{2,1,0:T(8,128)S(1)}) custom-call(f32[8,64,128]{2,1,0:T(8,128)S(1)} %copy-done.1, f32[8,64,128]{2,1,0:T(8,128)} %sv_in.3, f32[8,64,128]{2,1,0:T(8,128)} %pv_in.3, f32[64,128]{1,0:T(8,128)S(1)} %copy-done), custom_call_target="tpu_custom_call" | custom-call | tf_op jit(solution)/shard_map/prepare/pallas_call | solution.py:725
  14.4 0.0 collective-permute-done.first
  14.5 0.3 collective-permute-done.1.second
  14.8 1.0 %all-to-all-done.recv = f32[8,40,128]{2,1,0:T(8,128)S(1)} async-done(((f32[8,40,128]{2,1,0:T(8,128)}), f32[8,40,128]{2,1,0:T(8,128)S(1)}, u32[]{:S(2)}, u32[]{:S(2)}) %all-to-all-start) | async-done | bytes 163872 | tf_op jit(solution)/shard_map/all_to_all | solution.py:745
  15.7 0.0 copy-done.2
  15.7 0.0 copy-done.3
  15.7 0.0 copy-done.4
  15.7 0.5 %first.1 = (f32[8,64,128]{2,1,0:T(8,128)S(1)}, f32[48,128]{1,0:T(8,128)S(1)}, f32[48,128]{1,0:T(8,128)S(1)}, f32[128,128]{1,0:T(8,128)S(1)}, f32[24,128]{1,0:T(8,128)S(1)}) custom-call(f32[8,40,128]{2,1,0:T(8,128)S(1)} %all-to-all-done.recv, f32[8,64,128]{2,1,0:T(8,128)S(1)} %get-tuple-element.26.partial, f32[8,64,128]{2,1,0:T(8,128)S(1)} %get-tuple-element.27.toward, ...), custom_call_target="tpu_custom_call" | custom-call | tf_op jit(solution)/shard_map/first/pallas_call | solution.py:725
  16.2 1.0 %collective-permute-start.3 = (f32[48,128]{1,0:T(8,128)S(1)}, f32[48,128]{1,0:T(8,128)S(1)}, u32[]{:S(2)}, u32[]{:S(2)}) collective-permute-start(f32[48,128]{1,0:T(8,128)S(1)} %get-tuple-element.41), channel_id=1, source_target_pairs={{0,24},{8,16},{16,8},{24,0},{1,25},{9,17},{17,9},{25,1},{2,26},{10... | collective-permute-start | bytes 73736 | tf_op jit(solution)/shard_map/ppermute | solution.py:740
  17.2 0.7 %collective-permute-start.2 = (f32[48,128]{1,0:T(8,128)S(1)}, f32[48,128]{1,0:T(8,128)S(1)}, u32[]{:S(2)}, u32[]{:S(2)}) collective-permute-start(f32[48,128]{1,0:T(8,128)S(1)} %get-tuple-element.40.sent), channel_id=1, source_target_pairs={{0,8},{8,0},{16,24},{24,16},{1,9},{9,1},{17,25},{25,17},{2,10},{10... | collective-permute-start | bytes 73736 | tf_op jit(solution)/shard_map/ppermute | solution.py:741
  17.9 0.0 copy-start.5
  17.9 0.6 %sums.1 = (f32[8,64,128]{2,1,0:T(8,128)S(1)}, f32[128,128]{1,0:T(8,128)S(1)}, f32[24,128]{1,0:T(8,128)S(1)}, f32[96,128]{1,0:T(8,128)S(1)}) custom-call(f32[8,64,128]{2,1,0:T(8,128)S(1)} %get-tuple-element.33.fluid1, f32[128,128]{1,0:T(8,128)S(1)} %get-tuple-element.34.turned, f32[24,128]{1,0:T(8,128)S(1)} %get-tuple-element.35.side, ...), custom_call_target="tpu_custom_call" | custom-call | tf_op jit(solution)/shard_map/sums/pallas_call | solution.py:725
  18.6 1.1 %collective-permute-done.3.second1 = f32[48,128]{1,0:T(8,128)S(1)} collective-permute-done((f32[48,128]{1,0:T(8,128)S(1)}, f32[48,128]{1,0:T(8,128)S(1)}, u32[]{:S(2)}, u32[]{:S(2)}) %collective-permute-start.3) | collective-permute-done | bytes 24608 | tf_op jit(solution)/shard_map/ppermute | solution.py:740
  19.7 0.0 collective-permute-done.2.first1
  19.7 0.0 copy-done.5
  19.7 0.3 %pack.1 = (f32[8,32,128]{2,1,0:T(8,128)S(1)}, f32[112,128]{1,0:T(8,128)S(1)}) custom-call(f32[8,40,128]{2,1,0:T(8,128)S(1)} %all-to-all-done.recv, f32[128,128]{1,0:T(8,128)S(1)} %copy-done.5, f32[128,128]{1,0:T(8,128)S(1)} %get-tuple-element.36.mt, f32[24,128]{1,0:T(8,128)S(1)} %get-tuple-element.37.sums, f32[96,128]{1,0:T(8,128)S(1)} %get-tuple-element.38.metal, ...), custom_call_target="tpu_custom_call" | custom-call | tf_op jit(solution)/shard_map/pack/pallas_call | solution.py:725
  20.0 8.9 %all_to_all.10.recv1 = f32[8,32,128]{2,1,0:T(8,128)S(1)} all-to-all(f32[8,32,128]{2,1,0:T(8,128)S(1)} %get-tuple-element.42), channel_id=1, replica_groups={{5,2,6,4,1,0,7,3},{13,10,14,12,9,8,15,11},{21,18,22,20,17,16,23,19},{29..., dimensions={0} | all-to-all | bytes 262144 | tf_op jit(solution)/shard_map/all_to_all | solution.py:745
  28.9 1.5 %last.1 = (f32[8,64,128]{2,1,0:T(8,128)}, f32[32,128]{1,0:T(8,128)}) custom-call(f32[8,32,128]{2,1,0:T(8,128)S(1)} %all_to_all.10.recv1, f32[8,40,128]{2,1,0:T(8,128)S(1)} %all-to-all-done.recv, f32[112,128]{1,0:T(8,128)S(1)} %get-tuple-element.43.edge, f32[24,128]{1,0:T(8,128)S(1)} %get-tuple-element.35.side, f32[96,128]{1,0:T(8,128)S(1)} %get-tuple-element.38.metal, ...), custom_call_target="tpu_custom_call" | custom-call | tf_op jit(solution)/shard_map/last/pallas_call | solution.py:725
Async XLA Ops:
  3.0 10.1 %copy-start.1 = (f32[8,64,128]{2,1,0:T(8,128)S(1)}, f32[8,64,128]{2,1,0:T(8,128)}, u32[]{:S(2)}) copy-start(f32[8,64,128]{2,1,0:T(8,128)} %fluid_in.3) | copy-start | bytes 786436
  3.0 8.4 %copy-start.6 = (f32[48,128]{1,0:T(8,128)S(1)}, f32[48,128]{1,0:T(8,128)}, u32[]{:S(2)}) copy-start(f32[48,128]{1,0:T(8,128)} %get-tuple-element.32) | copy-start | bytes 73732
  3.0 10.1 %copy-start = (f32[64,128]{1,0:T(8,128)S(1)}, f32[64,128]{1,0:T(8,128)}, u32[]{:S(2)}) copy-start(f32[64,128]{1,0:T(8,128)} %film.9) | copy-start | bytes 98308
  3.0 12.7 %all-to-all-start = ((f32[8,40,128]{2,1,0:T(8,128)}), f32[8,40,128]{2,1,0:T(8,128)S(1)}, u32[]{:S(2)}, u32[]{:S(2)}) async-start(f32[8,40,128]{2,1,0:T(8,128)} %get-tuple-element.24), calls=%async_computation | async-start | bytes 327680 | tf_op jit(solution)/shard_map/all_to_all | solution.py:745
  11.4 3.0 %collective-permute-start = (f32[48,128]{1,0:T(8,128)}, f32[48,128]{1,0:T(8,128)S(1)}, u32[]{:S(2)}, u32[]{:S(2)}) collective-permute-start(f32[48,128]{1,0:T(8,128)} %get-tuple-element.31), channel_id=1, source_target_pairs={{0,8},{8,0},{16,24},{24,16},{1,9},{9,1},{17,25},{25,17},{2,10},{10... | collective-permute-start | bytes 73736 | tf_op jit(solution)/shard_map/ppermute | solution.py:741
  11.4 4.3 %copy-start.2 = (f32[64,128]{1,0:T(8,128)S(1)}, f32[64,128]{1,0:T(8,128)}, u32[]{:S(2)}) copy-start(f32[64,128]{1,0:T(8,128)} %get-tuple-element.30.owner) | copy-start | bytes 98308
  11.4 3.3 %collective-permute-start.1 = (f32[48,128]{1,0:T(8,128)S(1)}, f32[48,128]{1,0:T(8,128)S(1)}, u32[]{:S(2)}, u32[]{:S(2)}) collective-permute-start(f32[48,128]{1,0:T(8,128)S(1)} %copy-done.6), channel_id=1, source_target_pairs={{0,24},{8,16},{16,8},{24,0},{1,25},{9,17},{17,9},{25,1},{2,26},{10... | collective-permute-start | bytes 73736 | tf_op jit(solution)/shard_map/ppermute | solution.py:740
  13.1 2.7 %copy-start.3 = (f32[1,32,128]{2,1,0:T(8,128)S(1)}, f32[1,32,128]{2,1,0:T(8,128)}, u32[]{:S(2)}) copy-start(f32[1,32,128]{2,1,0:T(8,128)} %param.12) | copy-start | bytes 49156
  13.1 2.7 %copy-start.4 = (f32[1,32,128]{2,1,0:T(8,128)S(1)}, f32[1,32,128]{2,1,0:T(8,128)}, u32[]{:S(2)}) copy-start(f32[1,32,128]{2,1,0:T(8,128)} %param.11) | copy-start | bytes 49156
  16.2 3.5 %collective-permute-start.3 = (f32[48,128]{1,0:T(8,128)S(1)}, f32[48,128]{1,0:T(8,128)S(1)}, u32[]{:S(2)}, u32[]{:S(2)}) collective-permute-start(f32[48,128]{1,0:T(8,128)S(1)} %get-tuple-element.41), channel_id=1, source_target_pairs={{0,24},{8,16},{16,8},{24,0},{1,25},{9,17},{17,9},{25,1},{2,26},{10... | collective-permute-start | bytes 73736 | tf_op jit(solution)/shard_map/ppermute | solution.py:740
  17.2 2.5 %collective-permute-start.2 = (f32[48,128]{1,0:T(8,128)S(1)}, f32[48,128]{1,0:T(8,128)S(1)}, u32[]{:S(2)}, u32[]{:S(2)}) collective-permute-start(f32[48,128]{1,0:T(8,128)S(1)} %get-tuple-element.40.sent), channel_id=1, source_target_pairs={{0,8},{8,0},{16,24},{24,16},{1,9},{9,1},{17,25},{25,17},{2,10},{10... | collective-permute-start | bytes 73736 | tf_op jit(solution)/shard_map/ppermute | solution.py:741
  17.9 1.8 %copy-start.5 = (f32[128,128]{1,0:T(8,128)S(1)}, f32[128,128]{1,0:T(8,128)}, u32[]{:S(2)}) copy-start(f32[128,128]{1,0:T(8,128)} %get-tuple-element.25.mt_old) | copy-start | bytes 196612

commit v6 on v5

--- a/solution.py
+++ b/solution.py
@@ -26,8 +26,8 @@
 ROWS = 48
 OPEN_ROOM = 56 * 1024
 PREPARE_ROOM = 1400 * 1024
-ORDER0 = (5, 0, 1, 2, 6, 3, 4, 7)
-ORDER1 = (5, 2, 6, 4, 1, 0, 7, 3)
+ORDER0 = ((5, 0, 1, 2, 6, 3, 4, 7), (4, 1, 0, 3, 7, 2, 5, 6))
+ORDER1 = ((5, 2, 6, 4, 1, 0, 7, 3),) * 2
 
 
 def lanes(rows):
@@ -228,12 +228,19 @@
     return placed(108, 104), placed(104, 100)
 
 
+def place(peer, order):
+    lower, upper = order[0].index(peer), order[1].index(peer)
+    if lower == upper:
+        return lower
+    return jnp.where(2 * lax.axis_index("sec") >= lax.axis_size("sec"), upper, lower)
+
+
 def place_of(peer, order):
-    return sum(jnp.where(peer == k, order.index(k), 0) for k in range(NB))
+    return sum(jnp.where(peer == k, place(k, order), 0) for k in range(NB))
 
 
 def rows_of(recv, row, order):
-    return jnp.concatenate([recv[order.index(k), row : row + 1, :] for k in range(NB)], axis=0)
+    return jnp.concatenate([recv[place(k, order), row : row + 1, :] for k in range(NB)], axis=0)
 
 
 def keeps(me):
@@ -369,12 +376,12 @@
         ahead = (me + 1 == peer).astype(F32)
         behind = (me - 1 == peer).astype(F32)
         special = right_row * ahead + left_row * behind
-        out[ORDER0.index(peer), 0:8, :] = jnp.concatenate([head, special, special], axis=0)
-        out[ORDER0.index(peer), 8:16, :] = a0
-        out[ORDER0.index(peer), 16:24, :] = h
+        out[place(peer, ORDER0), 0:8, :] = jnp.concatenate([head, special, special], axis=0)
+        out[place(peer, ORDER0), 8:16, :] = a0
+        out[place(peer, ORDER0), 16:24, :] = h
         same = (me == peer).astype(F32)
-        out[ORDER0.index(peer), 24:32, :] = r0 * ahead + l0 * behind + r0 * same
-        out[ORDER0.index(peer), 32:40, :] = right_part * ahead + left_part * behind + l0 * same
+        out[place(peer, ORDER0), 24:32, :] = r0 * ahead + l0 * behind + r0 * same
+        out[place(peer, ORDER0), 32:40, :] = right_part * ahead + left_part * behind + l0 * same
 
 
 def halo_columns(known_l, known_r, factor_l, factor_r, rows, mine_right, mine_left, walls, me):
@@ -621,7 +628,7 @@
     for peer in range(NB):
         ahead = (me + 1 == peer).astype(F32)
         behind = (me - 1 == peer).astype(F32)
-        out[ORDER1.index(peer), 0:8, :] = jnp.concatenate(
+        out[place(peer, ORDER1), 0:8, :] = jnp.concatenate(
             [
                 metal[1:2, :],
                 b3[peer : peer + 1],
@@ -633,9 +640,9 @@
             ],
             axis=0,
         )
-        out[ORDER1.index(peer), 8:16, :] = side[8:16, :]
-        out[ORDER1.index(peer), 16:24, :] = a2
-        out[ORDER1.index(peer), 24:32, :] = to_right * ahead + to_left * behind
+        out[place(peer, ORDER1), 8:16, :] = side[8:16, :]
+        out[place(peer, ORDER1), 16:24, :] = a2
+        out[place(peer, ORDER1), 24:32, :] = to_right * ahead + to_left * behind
     kept = (
         low1, low2, high1, high2, r0, l0, x_first, x_last,
         lo(16, 24), lo(32, 40), hi(16, 24), hi(32, 40), lo(40, 48), hi(40, 48),
@@ -742,8 +749,10 @@
 
 
 def swap(message, order):
+    count = lax.axis_size("sec")
+    groups = [[NB * s + k for k in order[2 * s >= count]] for s in range(count)]
     return lax.all_to_all(
-        message, "blk", split_axis=0, concat_axis=0, tiled=True, axis_index_groups=[list(order)]
+        message, ("sec", "blk"), split_axis=0, concat_axis=0, tiled=True, axis_index_groups=groups
     )
 
 

time: 30.7 us -> 30.6 us (level)
  waiting for transfers between devices: 2.42 us -> 2.01 us
    ppermute x2, starting transfers between devices: 0.73 us -> 1.83 us  [both_ways(): return (lax.ppermute(first, 'sec', near), second)]
    ppermute x2, starting transfers between devices: 2.6 us -> 1.73 us  [both_ways(): second = lax.ppermute(second, 'sec', far)]
    ppermute x2, waiting for transfers between devices: 1.44 us -> 1.03 us  [both_ways(): second = lax.ppermute(second, 'sec', far)]
where the time goes in v6:
time: 30.6 us; the launch traced here: 30.3 us
  starting transfers between devices  12 us (39%)
  blocking collectives  8.86 us (29%)
  Pallas kernels  6.69 us (22%)
  waiting for transfers between devices  2.01 us (7%)
  between operations  0.72 us (2%)
    all_to_all x1, blocking collectives, swap(): lax.all_to_all(message, ('sec', 'blk'), split_axis=0, concat_axis=0, tile...  8.86 us
    all_to_all x1, starting transfers between devices, swap(): lax.all_to_all(message, ('sec', 'blk'), split_axis=0, concat_axis=0, tile...  8.39 us
    pallas_call x6, Pallas kernels, call(): pl.pallas_call(kernel, out_shape=outs, in_specs=[HBM] * far + [VMEM] * (l...  6.69 us
    ppermute x2, starting transfers between devices, both_ways(): return (lax.ppermute(first, 'sec', near), second)  1.83 us
    ppermute x2, starting transfers between devices, both_ways(): second = lax.ppermute(second, 'sec', far)  1.73 us
    ppermute x2, waiting for transfers between devices, both_ways(): second = lax.ppermute(second, 'sec', far)  1.03 us
    all_to_all x1, waiting for transfers between devices, swap(): lax.all_to_all(message, ('sec', 'blk'), split_axis=0, concat_axis=0, tile...  0.97 us
  transfers between devices with their start and end apart: 5, of which 3 were waited for; matrix products, arithmetic and copies ran while one was open for 0% of the time, Pallas kernels for 7%

profile of v6, /device:TPU:0, one launch (start us, length us, event | category | flops | bytes accessed | tf_op | source)
XLA Modules:
  0.0 30.3 jit_solution(15530117465218560620)
XLA Ops:
  0.6 2.4 %open.1 = (f32[8,40,128]{2,1,0:T(8,128)}, f32[48,128]{1,0:T(8,128)}, f32[48,128]{1,0:T(8,128)}, f32[128,128]{1,0:T(8,128)}, f32[64,128]{1,0:T(8,128)}) custom-call(f32[8,64,128]{2,1,0:T(8,128)} %fluid_in.3, f32[8,64,128]{2,1,0:T(8,128)} %sv_in.3, f32[8,64,128]{2,1,0:T(8,128)} %pv_in.3, f32[64,128]{1,0:T(8,128)} %film.9, f32[32,128]{1,0:T(8,128)} %bitcast.8, ...), custom_call_target="tpu_custom_call" | custom-call | tf_op jit(solution)/shard_map/open/pallas_call | solution.py:732
  3.0 0.0 copy-start.1
  3.0 0.0 copy-start.6
  3.0 0.0 copy-start
  3.0 8.4 %all-to-all-start = ((f32[8,40,128]{2,1,0:T(8,128)}), f32[8,40,128]{2,1,0:T(8,128)S(1)}, u32[]{:S(2)}, u32[]{:S(2)}) async-start(f32[8,40,128]{2,1,0:T(8,128)} %get-tuple-element.24), calls=%async_computation | async-start | bytes 327680 | tf_op jit(solution)/shard_map/all_to_all | solution.py:754
  11.4 0.0 collective-permute-start
  11.4 0.0 copy-done.6
  11.4 0.0 copy-start.2
  11.4 1.2 %collective-permute-start.1 = (f32[48,128]{1,0:T(8,128)S(1)}, f32[48,128]{1,0:T(8,128)S(1)}, u32[]{:S(2)}, u32[]{:S(2)}) collective-permute-start(f32[48,128]{1,0:T(8,128)S(1)} %copy-done.6), channel_id=1, source_target_pairs={{0,24},{8,16},{16,8},{24,0},{1,25},{9,17},{17,9},{25,1},{2,26},{10... | collective-permute-start | bytes 73736 | tf_op jit(solution)/shard_map/ppermute | solution.py:747
  12.6 0.0 copy-done.1
  12.6 0.0 copy-done
  12.6 0.0 copy-start.3
  12.6 0.0 copy-start.4
  12.7 1.3 %prepare.1 = (f32[8,64,128]{2,1,0:T(8,128)S(1)}, f32[8,64,128]{2,1,0:T(8,128)S(1)}, f32[8,64,128]{2,1,0:T(8,128)S(1)}, f32[8,64,128]{2,1,0:T(8,128)S(1)}) custom-call(f32[8,64,128]{2,1,0:T(8,128)S(1)} %copy-done.1, f32[8,64,128]{2,1,0:T(8,128)} %sv_in.3, f32[8,64,128]{2,1,0:T(8,128)} %pv_in.3, f32[64,128]{1,0:T(8,128)S(1)} %copy-done), custom_call_target="tpu_custom_call" | custom-call | tf_op jit(solution)/shard_map/prepare/pallas_call | solution.py:732
  14.0 0.0 collective-permute-done.first
  14.0 0.7 %collective-permute-done.1.second = f32[48,128]{1,0:T(8,128)S(1)} collective-permute-done((f32[48,128]{1,0:T(8,128)S(1)}, f32[48,128]{1,0:T(8,128)S(1)}, u32[]{:S(2)}, u32[]{:S(2)}) %collective-permute-start.1) | collective-permute-done | bytes 24608 | tf_op jit(solution)/shard_map/ppermute | solution.py:747
  14.8 1.0 %all-to-all-done.recv = f32[8,40,128]{2,1,0:T(8,128)S(1)} async-done(((f32[8,40,128]{2,1,0:T(8,128)}), f32[8,40,128]{2,1,0:T(8,128)S(1)}, u32[]{:S(2)}, u32[]{:S(2)}) %all-to-all-start) | async-done | bytes 163872 | tf_op jit(solution)/shard_map/all_to_all | solution.py:754
  15.7 0.0 copy-done.2
  15.7 0.0 copy-done.3
  15.7 0.0 copy-done.4
  15.7 0.5 %first.1 = (f32[8,64,128]{2,1,0:T(8,128)S(1)}, f32[48,128]{1,0:T(8,128)S(1)}, f32[48,128]{1,0:T(8,128)S(1)}, f32[128,128]{1,0:T(8,128)S(1)}, f32[24,128]{1,0:T(8,128)S(1)}) custom-call(f32[8,40,128]{2,1,0:T(8,128)S(1)} %all-to-all-done.recv, f32[8,64,128]{2,1,0:T(8,128)S(1)} %get-tuple-element.26.partial, f32[8,64,128]{2,1,0:T(8,128)S(1)} %get-tuple-element.27.toward, ...), custom_call_target="tpu_custom_call" | custom-call | tf_op jit(solution)/shard_map/first/pallas_call | solution.py:732
  16.2 0.5 %collective-permute-start.3 = (f32[48,128]{1,0:T(8,128)S(1)}, f32[48,128]{1,0:T(8,128)S(1)}, u32[]{:S(2)}, u32[]{:S(2)}) collective-permute-start(f32[48,128]{1,0:T(8,128)S(1)} %get-tuple-element.41), channel_id=1, source_target_pairs={{0,24},{8,16},{16,8},{24,0},{1,25},{9,17},{17,9},{25,1},{2,26},{10... | collective-permute-start | bytes 73736 | tf_op jit(solution)/shard_map/ppermute | solution.py:747
  16.8 1.8 %collective-permute-start.2 = (f32[48,128]{1,0:T(8,128)S(1)}, f32[48,128]{1,0:T(8,128)S(1)}, u32[]{:S(2)}, u32[]{:S(2)}) collective-permute-start(f32[48,128]{1,0:T(8,128)S(1)} %get-tuple-element.40.sent), channel_id=1, source_target_pairs={{0,8},{8,0},{16,24},{24,16},{1,9},{9,1},{17,25},{25,17},{2,10},{10... | collective-permute-start | bytes 73736 | tf_op jit(solution)/shard_map/ppermute | solution.py:748
  18.6 0.0 copy-start.5
  18.6 0.6 %sums.1 = (f32[8,64,128]{2,1,0:T(8,128)S(1)}, f32[128,128]{1,0:T(8,128)S(1)}, f32[24,128]{1,0:T(8,128)S(1)}, f32[96,128]{1,0:T(8,128)S(1)}) custom-call(f32[8,64,128]{2,1,0:T(8,128)S(1)} %get-tuple-element.33.fluid1, f32[128,128]{1,0:T(8,128)S(1)} %get-tuple-element.34.turned, f32[24,128]{1,0:T(8,128)S(1)} %get-tuple-element.35.side, ...), custom_call_target="tpu_custom_call" | custom-call | tf_op jit(solution)/shard_map/sums/pallas_call | solution.py:732
  19.2 0.3 collective-permute-done.3.second1
  19.5 0.0 collective-permute-done.2.first1
  19.5 0.0 copy-done.5
  19.5 0.3 %pack.1 = (f32[8,32,128]{2,1,0:T(8,128)S(1)}, f32[112,128]{1,0:T(8,128)S(1)}) custom-call(f32[8,40,128]{2,1,0:T(8,128)S(1)} %all-to-all-done.recv, f32[128,128]{1,0:T(8,128)S(1)} %copy-done.5, f32[128,128]{1,0:T(8,128)S(1)} %get-tuple-element.36.mt, f32[24,128]{1,0:T(8,128)S(1)} %get-tuple-element.37.sums, f32[96,128]{1,0:T(8,128)S(1)} %get-tuple-element.38.metal, ...), custom_call_target="tpu_custom_call" | custom-call | tf_op jit(solution)/shard_map/pack/pallas_call | solution.py:732
  19.9 8.9 %all_to_all.10.recv1 = f32[8,32,128]{2,1,0:T(8,128)S(1)} all-to-all(f32[8,32,128]{2,1,0:T(8,128)S(1)} %get-tuple-element.42), channel_id=1, replica_groups={{5,2,6,4,1,0,7,3},{13,10,14,12,9,8,15,11},{21,18,22,20,17,16,23,19},{29..., dimensions={0} | all-to-all | bytes 262144 | tf_op jit(solution)/shard_map/all_to_all | solution.py:754
  28.8 1.5 %last.1 = (f32[8,64,128]{2,1,0:T(8,128)}, f32[32,128]{1,0:T(8,128)}) custom-call(f32[8,32,128]{2,1,0:T(8,128)S(1)} %all_to_all.10.recv1, f32[8,40,128]{2,1,0:T(8,128)S(1)} %all-to-all-done.recv, f32[112,128]{1,0:T(8,128)S(1)} %get-tuple-element.43.edge, f32[24,128]{1,0:T(8,128)S(1)} %get-tuple-element.35.side, f32[96,128]{1,0:T(8,128)S(1)} %get-tuple-element.38.metal, ...), custom_call_target="tpu_custom_call" | custom-call | tf_op jit(solution)/shard_map/last/pallas_call | solution.py:732
Async XLA Ops:
  3.0 9.6 %copy-start.1 = (f32[8,64,128]{2,1,0:T(8,128)S(1)}, f32[8,64,128]{2,1,0:T(8,128)}, u32[]{:S(2)}) copy-start(f32[8,64,128]{2,1,0:T(8,128)} %fluid_in.3) | copy-start | bytes 786436
  3.0 8.4 %copy-start.6 = (f32[48,128]{1,0:T(8,128)S(1)}, f32[48,128]{1,0:T(8,128)}, u32[]{:S(2)}) copy-start(f32[48,128]{1,0:T(8,128)} %get-tuple-element.32) | copy-start | bytes 73732
  3.0 9.6 %copy-start = (f32[64,128]{1,0:T(8,128)S(1)}, f32[64,128]{1,0:T(8,128)}, u32[]{:S(2)}) copy-start(f32[64,128]{1,0:T(8,128)} %film.9) | copy-start | bytes 98308
  3.0 12.7 %all-to-all-start = ((f32[8,40,128]{2,1,0:T(8,128)}), f32[8,40,128]{2,1,0:T(8,128)S(1)}, u32[]{:S(2)}, u32[]{:S(2)}) async-start(f32[8,40,128]{2,1,0:T(8,128)} %get-tuple-element.24), calls=%async_computation | async-start | bytes 327680 | tf_op jit(solution)/shard_map/all_to_all | solution.py:754
  11.4 2.6 %collective-permute-start = (f32[48,128]{1,0:T(8,128)}, f32[48,128]{1,0:T(8,128)S(1)}, u32[]{:S(2)}, u32[]{:S(2)}) collective-permute-start(f32[48,128]{1,0:T(8,128)} %get-tuple-element.31), channel_id=1, source_target_pairs={{0,8},{8,0},{16,24},{24,16},{1,9},{9,1},{17,25},{25,17},{2,10},{10... | collective-permute-start | bytes 73736 | tf_op jit(solution)/shard_map/ppermute | solution.py:748
  11.4 4.3 %copy-start.2 = (f32[64,128]{1,0:T(8,128)S(1)}, f32[64,128]{1,0:T(8,128)}, u32[]{:S(2)}) copy-start(f32[64,128]{1,0:T(8,128)} %get-tuple-element.30.owner) | copy-start | bytes 98308
  11.4 3.3 %collective-permute-start.1 = (f32[48,128]{1,0:T(8,128)S(1)}, f32[48,128]{1,0:T(8,128)S(1)}, u32[]{:S(2)}, u32[]{:S(2)}) collective-permute-start(f32[48,128]{1,0:T(8,128)S(1)} %copy-done.6), channel_id=1, source_target_pairs={{0,24},{8,16},{16,8},{24,0},{1,25},{9,17},{17,9},{25,1},{2,26},{10... | collective-permute-start | bytes 73736 | tf_op jit(solution)/shard_map/ppermute | solution.py:747
  12.6 3.1 %copy-start.3 = (f32[1,32,128]{2,1,0:T(8,128)S(1)}, f32[1,32,128]{2,1,0:T(8,128)}, u32[]{:S(2)}) copy-start(f32[1,32,128]{2,1,0:T(8,128)} %param.12) | copy-start | bytes 49156
  12.6 3.1 %copy-start.4 = (f32[1,32,128]{2,1,0:T(8,128)S(1)}, f32[1,32,128]{2,1,0:T(8,128)}, u32[]{:S(2)}) copy-start(f32[1,32,128]{2,1,0:T(8,128)} %param.11) | copy-start | bytes 49156
  16.2 3.3 %collective-permute-start.3 = (f32[48,128]{1,0:T(8,128)S(1)}, f32[48,128]{1,0:T(8,128)S(1)}, u32[]{:S(2)}, u32[]{:S(2)}) collective-permute-start(f32[48,128]{1,0:T(8,128)S(1)} %get-tuple-element.41), channel_id=1, source_target_pairs={{0,24},{8,16},{16,8},{24,0},{1,25},{9,17},{17,9},{25,1},{2,26},{10... | collective-permute-start | bytes 73736 | tf_op jit(solution)/shard_map/ppermute | solution.py:747
  16.8 2.8 %collective-permute-start.2 = (f32[48,128]{1,0:T(8,128)S(1)}, f32[48,128]{1,0:T(8,128)S(1)}, u32[]{:S(2)}, u32[]{:S(2)}) collective-permute-start(f32[48,128]{1,0:T(8,128)S(1)} %get-tuple-element.40.sent), channel_id=1, source_target_pairs={{0,8},{8,0},{16,24},{24,16},{1,9},{9,1},{17,25},{25,17},{2,10},{10... | collective-permute-start | bytes 73736 | tf_op jit(solution)/shard_map/ppermute | solution.py:748
  18.6 1.0 %copy-start.5 = (f32[128,128]{1,0:T(8,128)S(1)}, f32[128,128]{1,0:T(8,128)}, u32[]{:S(2)}) copy-start(f32[128,128]{1,0:T(8,128)} %get-tuple-element.25.mt_old) | copy-start | bytes 196612

commit v7 on v6

--- a/solution.py
+++ b/solution.py
@@ -399,7 +399,7 @@
 
 
 def first_kernel(
-    recv, partial, toward, up, down, film, solid, cond, owner, first, second,
+    recv, partial, toward, up, down, film, solid, cond, owner, first, second, sent,
     fluid1, first_out, second_out, turned, side, tm,
 ):
     me = lax.axis_index("blk")
@@ -771,6 +771,7 @@
         far=7,
         limit=GRANT - OPEN_ROOM,
     )
+    first_out, second_out = first, second
     first, second = both_ways(first, second)
     recv = swap(message, ORDER0)
     *factors, partial = call(
@@ -785,7 +786,7 @@
     fluid1, first_sent, second_sent, turned, side = call(
         first_kernel,
         (field, rows, rows, shape(FS, FS), shape(24, FS)),
-        (recv, partial, *factors, film, solid, cond, owner, first, second),
+        (recv, partial, *factors, film, solid, cond, owner, first, second, first_out),
         "first",
         [pltpu.VMEM((FS, FS), F32)],
     )

time: 30.6 us -> 30.6 us (level)
    ppermute x2, starting transfers between devices: 1.73 us -> 0.07 us  [both_ways(): second = lax.ppermute(second, 'sec', far)]
    ppermute x2, starting transfers between devices: 1.83 us -> 3.47 us  [both_ways(): return (lax.ppermute(first, 'sec', near), second)]
where the time goes in v7:
time: 30.6 us; the launch traced here: 30.3 us
  starting transfers between devices  11.9 us (39%)
  blocking collectives  8.86 us (29%)
  Pallas kernels  6.69 us (22%)
  waiting for transfers between devices  2.03 us (7%)
  between operations  0.72 us (2%)
    all_to_all x1, blocking collectives, swap(): lax.all_to_all(message, ('sec', 'blk'), split_axis=0, concat_axis=0, tile...  8.86 us
    all_to_all x1, starting transfers between devices, swap(): lax.all_to_all(message, ('sec', 'blk'), split_axis=0, concat_axis=0, tile...  8.39 us
    pallas_call x6, Pallas kernels, call(): pl.pallas_call(kernel, out_shape=outs, in_specs=[HBM] * far + [VMEM] * (l...  6.69 us
    ppermute x2, starting transfers between devices, both_ways(): return (lax.ppermute(first, 'sec', near), second)  3.47 us
    ppermute x2, waiting for transfers between devices, both_ways(): second = lax.ppermute(second, 'sec', far)  1.18 us
    all_to_all x1, waiting for transfers between devices, swap(): lax.all_to_all(message, ('sec', 'blk'), split_axis=0, concat_axis=0, tile...  0.84 us
  transfers between devices with their start and end apart: 5, of which 3 were waited for; matrix products, arithmetic and copies ran while one was open for 0% of the time, Pallas kernels for 7%

profile of v7, /device:TPU:0, one launch (start us, length us, event | category | flops | bytes accessed | tf_op | source)
XLA Modules:
  0.0 30.3 jit_solution(17932018415805363715)
XLA Ops:
  0.6 2.4 %open.1 = (f32[8,40,128]{2,1,0:T(8,128)}, f32[48,128]{1,0:T(8,128)}, f32[48,128]{1,0:T(8,128)}, f32[128,128]{1,0:T(8,128)}, f32[64,128]{1,0:T(8,128)}) custom-call(f32[8,64,128]{2,1,0:T(8,128)} %fluid_in.3, f32[8,64,128]{2,1,0:T(8,128)} %sv_in.3, f32[8,64,128]{2,1,0:T(8,128)} %pv_in.3, f32[64,128]{1,0:T(8,128)} %film.9, f32[32,128]{1,0:T(8,128)} %bitcast.8, ...), custom_call_target="tpu_custom_call" | custom-call | tf_op jit(solution)/shard_map/open/pallas_call | solution.py:732
  3.0 0.0 copy-start.1
  3.0 0.0 copy-start.6
  3.0 0.0 copy-start
  3.0 8.4 %all-to-all-start = ((f32[8,40,128]{2,1,0:T(8,128)}), f32[8,40,128]{2,1,0:T(8,128)S(1)}, u32[]{:S(2)}, u32[]{:S(2)}) async-start(f32[8,40,128]{2,1,0:T(8,128)} %get-tuple-element.24), calls=%async_computation | async-start | bytes 327680 | tf_op jit(solution)/shard_map/all_to_all | solution.py:754
  11.4 0.0 collective-permute-start.1
  11.4 0.0 copy-done.6
  11.4 0.0 copy-start.2
  11.4 1.2 %collective-permute-start = (f32[48,128]{1,0:T(8,128)S(1)}, f32[48,128]{1,0:T(8,128)S(1)}, u32[]{:S(2)}, u32[]{:S(2)}) collective-permute-start(f32[48,128]{1,0:T(8,128)S(1)} %copy-done.6), channel_id=1, source_target_pairs={{0,8},{8,0},{16,24},{24,16},{1,9},{9,1},{17,25},{25,17},{2,10},{10... | collective-permute-start | bytes 73736 | tf_op jit(solution)/shard_map/ppermute | solution.py:748
  12.6 0.0 copy-done.1
  12.6 0.0 copy-done
  12.6 0.0 copy-start.3
  12.6 0.0 copy-start.4
  12.6 1.3 %prepare.1 = (f32[8,64,128]{2,1,0:T(8,128)S(1)}, f32[8,64,128]{2,1,0:T(8,128)S(1)}, f32[8,64,128]{2,1,0:T(8,128)S(1)}, f32[8,64,128]{2,1,0:T(8,128)S(1)}) custom-call(f32[8,64,128]{2,1,0:T(8,128)S(1)} %copy-done.1, f32[8,64,128]{2,1,0:T(8,128)} %sv_in.3, f32[8,64,128]{2,1,0:T(8,128)} %pv_in.3, f32[64,128]{1,0:T(8,128)S(1)} %copy-done), custom_call_target="tpu_custom_call" | custom-call | tf_op jit(solution)/shard_map/prepare/pallas_call | solution.py:732
  14.0 0.9 %collective-permute-done.1.second = f32[48,128]{1,0:T(8,128)S(1)} collective-permute-done((f32[48,128]{1,0:T(8,128)}, f32[48,128]{1,0:T(8,128)S(1)}, u32[]{:S(2)}, u32[]{:S(2)}) %collective-permute-start.1) | collective-permute-done | bytes 24608 | tf_op jit(solution)/shard_map/ppermute | solution.py:747
  14.9 0.0 collective-permute-done.first
  14.9 0.8 %all-to-all-done.recv = f32[8,40,128]{2,1,0:T(8,128)S(1)} async-done(((f32[8,40,128]{2,1,0:T(8,128)}), f32[8,40,128]{2,1,0:T(8,128)S(1)}, u32[]{:S(2)}, u32[]{:S(2)}) %all-to-all-start) | async-done | bytes 163872 | tf_op jit(solution)/shard_map/all_to_all | solution.py:754
  15.7 0.0 copy-done.2
  15.7 0.0 copy-done.3
  15.7 0.0 copy-done.4
  15.7 0.5 %first.1 = (f32[8,64,128]{2,1,0:T(8,128)S(1)}, f32[48,128]{1,0:T(8,128)S(1)}, f32[48,128]{1,0:T(8,128)S(1)}, f32[128,128]{1,0:T(8,128)S(1)}, f32[24,128]{1,0:T(8,128)S(1)}) custom-call(f32[8,40,128]{2,1,0:T(8,128)S(1)} %all-to-all-done.recv, f32[8,64,128]{2,1,0:T(8,128)S(1)} %get-tuple-element.26.partial, f32[8,64,128]{2,1,0:T(8,128)S(1)} %get-tuple-element.27.toward, ...), custom_call_target="tpu_custom_call" | custom-call | tf_op jit(solution)/shard_map/first/pallas_call | solution.py:732
  16.2 0.1 collective-permute-start.3
  16.3 2.3 %collective-permute-start.2 = (f32[48,128]{1,0:T(8,128)S(1)}, f32[48,128]{1,0:T(8,128)S(1)}, u32[]{:S(2)}, u32[]{:S(2)}) collective-permute-start(f32[48,128]{1,0:T(8,128)S(1)} %get-tuple-element.40.sent), channel_id=1, source_target_pairs={{0,8},{8,0},{16,24},{24,16},{1,9},{9,1},{17,25},{25,17},{2,10},{10... | collective-permute-start | bytes 73736 | tf_op jit(solution)/shard_map/ppermute | solution.py:748
  18.6 0.0 copy-start.5
  18.6 0.6 %sums.1 = (f32[8,64,128]{2,1,0:T(8,128)S(1)}, f32[128,128]{1,0:T(8,128)S(1)}, f32[24,128]{1,0:T(8,128)S(1)}, f32[96,128]{1,0:T(8,128)S(1)}) custom-call(f32[8,64,128]{2,1,0:T(8,128)S(1)} %get-tuple-element.33.fluid1, f32[128,128]{1,0:T(8,128)S(1)} %get-tuple-element.34.turned, f32[24,128]{1,0:T(8,128)S(1)} %get-tuple-element.35.side, ...), custom_call_target="tpu_custom_call" | custom-call | tf_op jit(solution)/shard_map/sums/pallas_call | solution.py:732
  19.3 0.3 collective-permute-done.3.second1
  19.5 0.0 collective-permute-done.2.first1
  19.6 0.0 copy-done.5
  19.6 0.3 %pack.1 = (f32[8,32,128]{2,1,0:T(8,128)S(1)}, f32[112,128]{1,0:T(8,128)S(1)}) custom-call(f32[8,40,128]{2,1,0:T(8,128)S(1)} %all-to-all-done.recv, f32[128,128]{1,0:T(8,128)S(1)} %copy-done.5, f32[128,128]{1,0:T(8,128)S(1)} %get-tuple-element.36.mt, f32[24,128]{1,0:T(8,128)S(1)} %get-tuple-element.37.sums, f32[96,128]{1,0:T(8,128)S(1)} %get-tuple-element.38.metal, ...), custom_call_target="tpu_custom_call" | custom-call | tf_op jit(solution)/shard_map/pack/pallas_call | solution.py:732
  19.9 8.9 %all_to_all.10.recv1 = f32[8,32,128]{2,1,0:T(8,128)S(1)} all-to-all(f32[8,32,128]{2,1,0:T(8,128)S(1)} %get-tuple-element.42), channel_id=1, replica_groups={{5,2,6,4,1,0,7,3},{13,10,14,12,9,8,15,11},{21,18,22,20,17,16,23,19},{29..., dimensions={0} | all-to-all | bytes 262144 | tf_op jit(solution)/shard_map/all_to_all | solution.py:754
  28.8 1.5 %last.1 = (f32[8,64,128]{2,1,0:T(8,128)}, f32[32,128]{1,0:T(8,128)}) custom-call(f32[8,32,128]{2,1,0:T(8,128)S(1)} %all_to_all.10.recv1, f32[8,40,128]{2,1,0:T(8,128)S(1)} %all-to-all-done.recv, f32[112,128]{1,0:T(8,128)S(1)} %get-tuple-element.43.edge, f32[24,128]{1,0:T(8,128)S(1)} %get-tuple-element.35.side, f32[96,128]{1,0:T(8,128)S(1)} %get-tuple-element.38.metal, ...), custom_call_target="tpu_custom_call" | custom-call | tf_op jit(solution)/shard_map/last/pallas_call | solution.py:732
Async XLA Ops:
  3.0 9.6 %copy-start.1 = (f32[8,64,128]{2,1,0:T(8,128)S(1)}, f32[8,64,128]{2,1,0:T(8,128)}, u32[]{:S(2)}) copy-start(f32[8,64,128]{2,1,0:T(8,128)} %fluid_in.3) | copy-start | bytes 786436
  3.0 8.4 %copy-start.6 = (f32[48,128]{1,0:T(8,128)S(1)}, f32[48,128]{1,0:T(8,128)}, u32[]{:S(2)}) copy-start(f32[48,128]{1,0:T(8,128)} %get-tuple-element.31.sent) | copy-start | bytes 73732
  3.0 9.6 %copy-start = (f32[64,128]{1,0:T(8,128)S(1)}, f32[64,128]{1,0:T(8,128)}, u32[]{:S(2)}) copy-start(f32[64,128]{1,0:T(8,128)} %film.9) | copy-start | bytes 98308
  3.0 12.7 %all-to-all-start = ((f32[8,40,128]{2,1,0:T(8,128)}), f32[8,40,128]{2,1,0:T(8,128)S(1)}, u32[]{:S(2)}, u32[]{:S(2)}) async-start(f32[8,40,128]{2,1,0:T(8,128)} %get-tuple-element.24), calls=%async_computation | async-start | bytes 327680 | tf_op jit(solution)/shard_map/all_to_all | solution.py:754
  11.4 3.5 %collective-permute-start.1 = (f32[48,128]{1,0:T(8,128)}, f32[48,128]{1,0:T(8,128)S(1)}, u32[]{:S(2)}, u32[]{:S(2)}) collective-permute-start(f32[48,128]{1,0:T(8,128)} %get-tuple-element.32), channel_id=1, source_target_pairs={{0,24},{8,16},{16,8},{24,0},{1,25},{9,17},{17,9},{25,1},{2,26},{10... | collective-permute-start | bytes 73736 | tf_op jit(solution)/shard_map/ppermute | solution.py:747
  11.4 4.3 %copy-start.2 = (f32[64,128]{1,0:T(8,128)S(1)}, f32[64,128]{1,0:T(8,128)}, u32[]{:S(2)}) copy-start(f32[64,128]{1,0:T(8,128)} %get-tuple-element.30.owner) | copy-start | bytes 98308
  11.4 3.4 %collective-permute-start = (f32[48,128]{1,0:T(8,128)S(1)}, f32[48,128]{1,0:T(8,128)S(1)}, u32[]{:S(2)}, u32[]{:S(2)}) collective-permute-start(f32[48,128]{1,0:T(8,128)S(1)} %copy-done.6), channel_id=1, source_target_pairs={{0,8},{8,0},{16,24},{24,16},{1,9},{9,1},{17,25},{25,17},{2,10},{10... | collective-permute-start | bytes 73736 | tf_op jit(solution)/shard_map/ppermute | solution.py:748
  12.6 3.1 %copy-start.3 = (f32[1,32,128]{2,1,0:T(8,128)S(1)}, f32[1,32,128]{2,1,0:T(8,128)}, u32[]{:S(2)}) copy-start(f32[1,32,128]{2,1,0:T(8,128)} %param.12) | copy-start | bytes 49156
  12.6 3.1 %copy-start.4 = (f32[1,32,128]{2,1,0:T(8,128)S(1)}, f32[1,32,128]{2,1,0:T(8,128)}, u32[]{:S(2)}) copy-start(f32[1,32,128]{2,1,0:T(8,128)} %param.11) | copy-start | bytes 49156
  16.2 3.3 %collective-permute-start.3 = (f32[48,128]{1,0:T(8,128)S(1)}, f32[48,128]{1,0:T(8,128)S(1)}, u32[]{:S(2)}, u32[]{:S(2)}) collective-permute-start(f32[48,128]{1,0:T(8,128)S(1)} %get-tuple-element.41), channel_id=1, source_target_pairs={{0,24},{8,16},{16,8},{24,0},{1,25},{9,17},{17,9},{25,1},{2,26},{10... | collective-permute-start | bytes 73736 | tf_op jit(solution)/shard_map/ppermute | solution.py:747
  16.3 3.2 %collective-permute-start.2 = (f32[48,128]{1,0:T(8,128)S(1)}, f32[48,128]{1,0:T(8,128)S(1)}, u32[]{:S(2)}, u32[]{:S(2)}) collective-permute-start(f32[48,128]{1,0:T(8,128)S(1)} %get-tuple-element.40.sent), channel_id=1, source_target_pairs={{0,8},{8,0},{16,24},{24,16},{1,9},{9,1},{17,25},{25,17},{2,10},{10... | collective-permute-start | bytes 73736 | tf_op jit(solution)/shard_map/ppermute | solution.py:748
  18.6 1.0 %copy-start.5 = (f32[128,128]{1,0:T(8,128)S(1)}, f32[128,128]{1,0:T(8,128)}, u32[]{:S(2)}) copy-start(f32[128,128]{1,0:T(8,128)} %get-tuple-element.25.mt_old) | copy-start | bytes 196612
